TPU v7x, 32 devices: a whole 2x2x4 slice. The times are simulated.
32 devices in a mesh: seg: 4 (over z), tm: 8 (over y, x, core).
Axes of the slice: x: 2, y: 2, z: 4, core: 2. Of those that a mesh axis runs over, the one named last changes fastest.
Arguments:
- feats: bfloat16 [32, 4096, 192], P('seg', 'tm'), may hold values from -6 to 6
- spectral: bfloat16 [32, 1024, 384], P('seg', 'tm'), may hold values from -6 to 6
- target: bfloat16 [32, 1024, 128], P('seg', 'tm'), may hold values from -6 to 6
- valid_samples: int32 [32], P('seg'), may hold values from 5461 to 16384, as said below
- stem_weights: int32 [32, 4], P('seg'), may hold values from 1 to 4
- conv_weight: float32 [1536, 384], P('tm'), may hold values from -0.15625 to 0.15625
- query_weight: float32 [384, 384], P('tm'), may hold values from -0.046875 to 0.046875
- keyval_weight: float32 [384, 768], P('tm'), may hold values from -0.3125 to 0.3125
- out_weight: float32 [384, 384], P('tm'), may hold values from -6 to 6
- up_weight: float32 [384, 1536], P('tm'), may hold values from -0.3125 to 0.3125
- down_weight: float32 [1536, 384], P('tm'), may hold values from -0.15625 to 0.15625
- head_weight: float32 [384, 128], P('tm'), may hold values from -0.3125 to 0.3125
- gains: float32 [5, 384], P(None, 'tm'), may hold values from 0.5 to 1.5
- conv_first: float32 [1536, 384], P('tm'), as said below
- query_first: float32 [384, 384], P('tm')
- keyval_first: float32 [384, 768], P('tm')
- out_first: float32 [384, 384], P('tm')
- up_first: float32 [384, 1536], P('tm')
- down_first: float32 [1536, 384], P('tm')
- head_first: float32 [384, 128], P('tm')
- gain_first: float32 [5, 384], P(None, 'tm')
- conv_second: float32 [1536, 384], P('tm'), as said below
- query_second: float32 [384, 384], P('tm')
- keyval_second: float32 [384, 768], P('tm')
- out_second: float32 [384, 384], P('tm')
- up_second: float32 [384, 1536], P('tm')
- down_second: float32 [1536, 384], P('tm')
- head_second: float32 [384, 128], P('tm')
- gain_second: float32 [5, 384], P(None, 'tm')
Outputs:
- loss_sum: float32 [], replicated
- sample_count: float32 [], replicated
- grad_norm: float32 [], replicated
- conv_new: float32 [1536, 384], P('tm')
- query_new: float32 [384, 384], P('tm')
- keyval_new: float32 [384, 768], P('tm')
- out_new: float32 [384, 384], P('tm')
- up_new: float32 [384, 1536], P('tm')
- down_new: float32 [1536, 384], P('tm')
- head_new: float32 [384, 128], P('tm')
- gains_new: float32 [5, 384], P(None, 'tm')
- conv_first_new: float32 [1536, 384], P('tm')
- query_first_new: float32 [384, 384], P('tm')
- keyval_first_new: float32 [384, 768], P('tm')
- out_first_new: float32 [384, 384], P('tm')
- up_first_new: float32 [384, 1536], P('tm')
- down_first_new: float32 [1536, 384], P('tm')
- head_first_new: float32 [384, 128], P('tm')
- gain_first_new: float32 [5, 384], P(None, 'tm')
- conv_second_new: float32 [1536, 384], P('tm')
- query_second_new: float32 [384, 384], P('tm')
- keyval_second_new: float32 [384, 768], P('tm')
- out_second_new: float32 [384, 384], P('tm')
- up_second_new: float32 [384, 1536], P('tm')
- down_second_new: float32 [1536, 384], P('tm')
- head_second_new: float32 [384, 128], P('tm')
- gain_second_new: float32 [5, 384], P(None, 'tm')
Inputs may be any that keep to these rules, and one draw needn't show every extreme that they name: `valid_samples`: in each aligned run of 8 segments (those of one index of seg) at least one segment has more than 14336 valid samples; some segment is complete. `conv_first`: first moments have both signs. `conv_second`: second moments are positive.
All inputs are finite; a program needn't handle non-finite values.
Results may differ from a plain program's by a relative error of at most 0.005.
The roundings to bfloat16 on the way count: a program that leaves them out, or rounds other values in their place, can miss the bound.
Values may be sent and summed in bfloat16 or wider, within the bound.
No kernel may reach another device: no remote copies, remote signals or barrier semaphores. Data moves between devices by JAX's collectives and lax.ppermute only.
A program may use at most 320 MiB of HBM per device.

v0:
```python
import functools
import jax
import jax.numpy as jnp
from jax import lax
from jax.experimental import pallas as pl
from jax.experimental.pallas import tpu as pltpu
from jax.sharding import PartitionSpec as P

H = 8
STEMS = 4
SUB = 16
STEP = 10
LANES = 128

clip_limit = 0.001
beta_first = 0.9
beta_second = 0.999
learn_rate = 0.03
fast_rate = 0.5
weight_decay = 0.05
adam_epsilon = 1e-08
norm_epsilon = 1e-05

bfloat = jnp.bfloat16
float32 = jnp.float32
VMEM_LIMIT = 60 * 1024 * 1024


def mm(left, right):
    return lax.dot_general(left, right, (((1,), (0,)), ((), ())), preferred_element_type=float32)


def nt(left, right):
    return lax.dot_general(left, right, (((1,), (1,)), ((), ())), preferred_element_type=float32)


def tn(left, right):
    return lax.dot_general(left, right, (((0,), (0,)), ((), ())), preferred_element_type=float32)


def iota(shape, dim):
    return lax.broadcasted_iota(jnp.int32, shape, dim)


def norm_parts(values):
    centred = values - jnp.mean(values, -1, keepdims=True)
    scale = lax.rsqrt(jnp.mean(centred * centred, -1, keepdims=True) + norm_epsilon)
    return centred * scale, scale


def norm_back(unit, scale, gain, upstream):
    inner = upstream * gain
    value_grad = scale * (
        inner
        - jnp.mean(inner, -1, keepdims=True)
        - unit * jnp.mean(inner * unit, -1, keepdims=True)
    )
    return value_grad, jnp.sum(upstream * unit, 0, keepdims=True)


def gelu_both(values):
    upper = 0.5 * (1.0 + lax.erf(values * 0.7071067811865476))
    density = jnp.exp(-0.5 * values * values) * 0.3989422804014327
    return values * upper, upper + values * density


def spread_matrix(width, head_size):
    shape = (width, width // head_size * LANES)
    lane = iota(shape, 1)
    inside = lane % LANES
    source = (lane // LANES) * head_size + inside
    hit = jnp.logical_and(iota(shape, 0) == source, inside < head_size)
    return jnp.where(hit, 1.0, 0.0).astype(bfloat)


def with_column(block, column, head_size):
    lane = iota(block.shape, 1)
    high = column.astype(bfloat).astype(float32)
    rest = column - high
    middle = rest.astype(bfloat).astype(float32)
    low = rest - middle
    pieces = jnp.where(lane == head_size, high, jnp.where(lane == head_size + 1, middle, low))
    spare = jnp.logical_and(lane >= head_size, lane < head_size + 3)
    return jnp.where(spare, pieces, block.astype(float32)).astype(bfloat)


class Sizes:
    def __init__(self, n, planes, feats, spectral, target, conv_weight, up_weight):
        self.n = n
        self.planes = planes
        self.segments = feats.shape[0]
        self.parts = n // self.segments
        self.channels = feats.shape[2]
        self.tokens_dev = spectral.shape[1]
        self.D = spectral.shape[2]
        self.taps = conv_weight.shape[0] * n
        self.frame = self.taps // 2
        self.F = up_weight.shape[1]
        self.out = target.shape[2]
        self.tokens = self.segments * self.tokens_dev
        self.keys = self.tokens * self.parts
        self.hd = self.D // H
        self.wide = H * LANES
        self.w = self.D // n
        self.cw = self.taps // n
        self.uw = self.w * (self.F // self.D)
        self.fw = self.F // n
        self.hw = self.w * self.out // self.D
        self.first_rows = self.cw + 3 * self.w + 16
        self.second_rows = self.w + self.uw + self.fw + self.hw
        step = 16 * planes
        self.first_grads = -(-self.first_rows // step) * step
        self.second_grads = -(-self.second_rows // step) * step
        self.direct = self.parts == 1 and self.w % 16 == 0 and self.hw % 16 == 0 and self.hw > 0
        self.block = 256
        self.middle_block = 256
        self.query_block = 1024 if self.keys <= 1024 else 256


def smem():
    return pl.BlockSpec(memory_space=pltpu.SMEM)


def anywhere():
    return pl.BlockSpec(memory_space=pl.ANY)


def whole(shape):
    return pl.BlockSpec(shape, lambda i: (0,) * len(shape))


def pack_weights(z, tm_place, masters):
    D, w, O, cw = z.D, z.w, z.out, z.cw

    def kernel(place_ref, conv_r, query_r, keyval_r, out_r, up_r, down_r, head_r, gains_r, first_o, second_o):
        first_o[:cw, :] = conv_r[...].astype(bfloat)
        first_o[cw : cw + w, :] = query_r[...].astype(bfloat)
        first_o[cw + w : cw + 2 * w, :] = keyval_r[:, :D].astype(bfloat)
        first_o[cw + 2 * w : cw + 3 * w, :] = keyval_r[:, D:].astype(bfloat)
        start = place_ref[0] * w
        shift = jnp.where(iota((w, D), 1) == iota((w, D), 0) + start, 1.0, 0.0).astype(bfloat)
        placed = mm(gains_r[...].astype(bfloat), shift)
        padded = jnp.concatenate([placed, jnp.zeros((16 - placed.shape[0], D), float32)], 0)
        first_o[cw + 3 * w :, :] = padded.astype(bfloat)
        second_o[:w, :] = out_r[...].astype(bfloat)
        for c in range(z.F // D):
            second_o[w + c * w : 2 * w + c * w, :] = up_r[:, c * D : (c + 1) * D].astype(bfloat)
        row = w + z.uw
        second_o[row : row + z.fw, :] = down_r[...].astype(bfloat)
        row += z.fw
        for g in range(D // O):
            here = head_r[g * z.hw : (g + 1) * z.hw, :]
            second_o[row : row + z.hw, g * O : (g + 1) * O] = here.astype(bfloat)

    vmem = pl.BlockSpec(memory_space=pltpu.VMEM)
    return pl.pallas_call(
        kernel,
        out_shape=[
            jax.ShapeDtypeStruct((z.first_rows, D), bfloat),
            jax.ShapeDtypeStruct((z.second_rows, D), bfloat),
        ],
        in_specs=[smem()] + [vmem] * 8,
        out_specs=[vmem] * 2,
        name="pack_weights",
    )(tm_place, *masters)


def pack_tokens(z, feats, spectral, target):
    rows, D, C = z.tokens_dev, z.D, z.channels

    def kernel(f_ref, s_ref, t_ref, o_ref, buffer, in_sem, out_sem):
        arriving, leaving = [], []
        for i in range(z.segments):
            arriving.append(
                [
                    pltpu.make_async_copy(f_ref.at[i], buffer.at[i, rows:, :], in_sem.at[i, 0]),
                    pltpu.make_async_copy(s_ref.at[i], buffer.at[i, :rows, :D], in_sem.at[i, 1]),
                    pltpu.make_async_copy(t_ref.at[i], buffer.at[i, :rows, D:], in_sem.at[i, 2]),
                ]
            )
            leaving.append(pltpu.make_async_copy(buffer.at[i], o_ref.at[i], out_sem.at[i]))
            for copy in arriving[i]:
                copy.start()
        for i in range(z.segments):
            for copy in arriving[i]:
                copy.wait()
            leaving[i].start()
        for copy in leaving:
            copy.wait()

    shape = (z.segments, rows + C, 4 * rows)
    return pl.pallas_call(
        kernel,
        out_shape=jax.ShapeDtypeStruct(shape, bfloat),
        in_specs=[anywhere()] * 3,
        out_specs=anywhere(),
        scratch_shapes=[
            pltpu.VMEM(shape, bfloat),
            pltpu.SemaphoreType.DMA((z.segments, 3)),
            pltpu.SemaphoreType.DMA((z.segments,)),
        ],
        compiler_params=pltpu.CompilerParams(vmem_limit_bytes=VMEM_LIMIT),
        name="pack_tokens",
    )(feats, spectral, target)


def spectral_copies(z, source, home, sem, first):
    if z.parts > 1:
        return [pltpu.make_async_copy(source, home, sem.at[first])]
    rows = z.tokens_dev
    return [
        pltpu.make_async_copy(source.at[i, :rows, : z.D], home.at[i * rows : (i + 1) * rows, :], sem.at[first + i])
        for i in range(z.segments)
    ]


def share_copies(z, meta_ref, shares, home, rows, sem, first):
    place = meta_ref[6] * 2 + meta_ref[7]
    return [
        pltpu.make_async_copy(share.at[rows], home.at[place ^ x], sem.at[first + x])
        for x, share in enumerate(shares)
    ]


def front(z, meta, moved, spectral, halo, weights):
    D, T, K, W, B = z.D, z.tokens, z.keys, z.wide, z.block
    frame, taps, hd = z.frame, z.taps, z.hd
    half = frame // 2
    QB = z.query_block
    count = z.tokens_dev
    CB = 2 * LANES
    extra = 2 if z.parts > 1 else 0
    n_weights = z.n if z.direct else 4

    def kernel(meta_ref, *refs):
        refs = list(refs)
        frames_ref, sp_ref = refs[:2]
        before_after = refs[2 : 2 + extra]
        weight_refs = refs[2 + extra : 2 + extra + n_weights]
        refs = refs[2 + extra + n_weights :]
        (x_o, stream_o, slope_o, normed_o, sn_o, q_o, k_o, v_o, att_o) = refs[:9]
        (frames_s, sp_s, x_s, stream_s, slope_s, normed_s, sn_s) = refs[9:16]
        (conv_s, wq_s, wk_s, wv_s, q_s, k_s, v_s, in_sem, out_sem) = refs[16:25]
        refs = refs[25:]
        h = pl.program_id(0)
        outgoing = [
            pltpu.make_async_copy(src, dst, out_sem.at[i])
            for i, (src, dst) in enumerate(
                ((x_s, x_o), (stream_s, stream_o), (slope_s, slope_o), (normed_s, normed_o), (sn_s, sn_o))
            )
        ]

        @pl.when(h == 0)
        def _():
            frames_copy = pltpu.make_async_copy(frames_ref.at[:, count:, :], frames_s, in_sem.at[0])
            spectral_in = spectral_copies(z, sp_ref, sp_s, in_sem, 1)
            if z.direct:
                blob_s, wc, wqkv = refs
                blob_in = share_copies(z, meta_ref, weight_refs, blob_s, slice(0, z.first_rows), in_sem, 1 + z.segments)
                for copy in blob_in:
                    copy.start()
            for copy in spectral_in:
                copy.start()
            frames_copy.start()
            if z.direct:
                for copy in blob_in:
                    copy.wait()
                w, cw = z.w, z.cw
                total = jnp.zeros((16, D), float32)
                for j in range(z.n):
                    wc[j * cw : (j + 1) * cw, :] = blob_s[j, 0:cw, :]
                    for c in range(3):
                        first = cw + c * w
                        wqkv[j * w : (j + 1) * w, c * D : (c + 1) * D] = blob_s[j, first : first + w, :]
                    total = total + blob_s[j, cw + 3 * w : cw + 3 * w + 16, :].astype(float32)
                gain_query, gain_keys = total[0:1, :], total[1:2, :]
                parts_w = [wqkv[:, c * D : (c + 1) * D] for c in range(3)]
            else:
                wc, wq, wkv, gains_ref = weight_refs
                gain_query, gain_keys = gains_ref[0:1, :], gains_ref[1:2, :]
                parts_w = [wq[...], wkv[:, :D], wkv[:, D:]]
            spread = spread_matrix(D, hd)
            for target_s, part in zip((wq_s, wk_s, wv_s), parts_w):
                target_s[...] = mm(part, spread).astype(bfloat)
            for copy in spectral_in:
                copy.wait()

            def key_block(i, carry):
                rows = pl.ds(pl.multiple_of(i * B, B), B)
                unit, _ = norm_parts(sp_s[rows, :].astype(float32))
                sn_s[rows, :] = (unit * gain_keys).astype(bfloat)
                return carry

            lax.fori_loop(0, K // B, key_block, 0)
            outgoing[4].start()
            inside = iota((K, CB), 1) % LANES
            spare = jnp.logical_and(inside >= hd, inside < hd + 3)
            for home, part in ((k_s, wk_s), (v_s, wv_s)):
                for c in range(0, W, CB):
                    product = mm(sn_s[...], part[:, c : c + CB])
                    home[:, c : c + CB] = jnp.where(spare, -1.0, product).astype(bfloat)
            frames_copy.wait()
            shape = (4 * count, 4 * count)
            row, column = iota(shape, 0), iota(shape, 1)
            order = jnp.where(column == (row % count) * 4 + row // count, 1.0, 0.0).astype(bfloat)
            for i in range(z.segments):
                taps_rows = nt(order, frames_s[i])
                x_s[i * count : (i + 1) * count, :] = jnp.concatenate(
                    [taps_rows[j * count : (j + 1) * count, :] for j in range(4)], 1
                ).astype(bfloat)
            outgoing[0].start()
            conv_s[...] = mm(x_s[...], wc[half : half + frame, :])
            row = iota((T, D), 0)
            older = pltpu.roll(mm(x_s[:, half:], wc[:half, :]), 1, 0)
            first_row, last_row = 0.0, 0.0
            if z.parts > 1:
                first_row = mm(before_after[0][...], wc[:half, :])[0:1, :]
                last_row = mm(before_after[1][...], wc[half + frame :, :])[0:1, :]
            conv_s[...] += jnp.where(row == 0, first_row, older)
            newer = pltpu.roll(mm(x_s[:, :half], wc[half + frame :, :]), T - 1, 0)
            conv_s[...] += jnp.where(row == T - 1, last_row, newer)

            def token_block(i, carry):
                rows = pl.ds(pl.multiple_of(i * B, B), B)
                stream, slope = gelu_both(conv_s[rows, :])
                stream_s[rows, :] = stream
                slope_s[rows, :] = slope
                unit, _ = norm_parts(stream)
                normed = (unit * gain_query).astype(bfloat)
                normed_s[rows, :] = normed
                return carry

            lax.fori_loop(0, T // B, token_block, 0)
            for c in range(0, W, CB):
                q_s[:, c : c + CB] = mm(normed_s[...], wq_s[:, c : c + CB]).astype(bfloat)
            for copy in outgoing[1:4]:
                copy.start()

        lanes = pl.ds(pl.multiple_of(h * LANES, LANES), LANES)
        k_o[...] = k_s[:, lanes]
        v_o[...] = v_s[:, lanes]
        def finish(rows, count, grown, top):
            q = q_s[rows, lanes]
            mass = jnp.sum(grown, 0, keepdims=True)
            probs = (grown * (1.0 / mass)).astype(bfloat)
            total = top + jnp.log(mass)
            result = tn(v_o[...], probs)
            high = total.astype(bfloat).astype(float32)
            rest = total - high
            mid = rest.astype(bfloat).astype(float32)
            sub = iota((LANES, count), 0)
            spare = jnp.where(sub == hd, high, jnp.where(sub == hd + 1, mid, rest - mid))
            spare = jnp.where(sub < hd + 3, spare, 0.0)
            both = jnp.where(sub < hd, result, spare).T
            att_o[rows, :] = both.astype(bfloat)
            lane = iota((count, LANES), 1)
            q_o[rows, :] = jnp.where(lane < hd, q.astype(float32), both).astype(bfloat)
            return mass

        least, most = jnp.inf, 0.0
        for b in range(T // QB):
            rows = slice(b * QB, (b + 1) * QB)
            mass = finish(rows, QB, jnp.exp(nt(k_o[...], q_s[rows, lanes])), 0.0)
            least = jnp.minimum(least, jnp.min(mass))
            most = jnp.maximum(most, jnp.max(mass))
        safe = jnp.logical_and(least > 1e-20, most < 1e30)

        @pl.when(jnp.logical_not(safe))
        def _():
            def again(i, carry):
                rows = pl.ds(pl.multiple_of(i * LANES, LANES), LANES)
                scores = nt(k_o[...], q_s[rows, lanes])
                top = jnp.max(scores, 0, keepdims=True)
                finish(rows, LANES, jnp.exp(scores - top), top)
                return carry

            lax.fori_loop(0, T // LANES, again, 0)

        @pl.when(h == H - 1)
        def _():
            for copy in outgoing:
                copy.wait()

    def lanes_of(rows):
        return pl.BlockSpec((rows, LANES), lambda h: (0, h))

    in_specs = [smem(), anywhere(), anywhere()]
    args = [meta, moved, moved if z.parts == 1 else spectral]
    if z.parts > 1:
        args += list(halo)
        in_specs += [whole((16, D))] * 2
    scratch = [
        pltpu.VMEM((z.segments, z.channels, 4 * count), bfloat),
        pltpu.VMEM((K, D), bfloat),
        pltpu.VMEM((T, frame), bfloat),
        pltpu.VMEM((T, D), float32),
        pltpu.VMEM((T, D), float32),
        pltpu.VMEM((T, D), bfloat),
        pltpu.VMEM((K, D), bfloat),
        pltpu.VMEM((T, D), float32),
        pltpu.VMEM((D, W), bfloat),
        pltpu.VMEM((D, W), bfloat),
        pltpu.VMEM((D, W), bfloat),
        pltpu.VMEM((T, W), bfloat),
        pltpu.VMEM((K, W), bfloat),
        pltpu.VMEM((K, W), bfloat),
        pltpu.SemaphoreType.DMA((1 + z.segments + z.n,)),
        pltpu.SemaphoreType.DMA((5,)),
    ]
    if z.direct:
        args += weights[0]
        in_specs += [anywhere()] * z.n
        scratch += [
            pltpu.VMEM((z.n, z.first_rows, D), bfloat),
            pltpu.VMEM((taps, D), bfloat),
            pltpu.VMEM((D, 3 * D), bfloat),
        ]
    else:
        for array in (weights[0], weights[1], weights[2], weights[7]):
            args.append(array)
            in_specs.append(whole(array.shape))
    shapes = [
        ((T, frame), bfloat),
        ((T, D), float32),
        ((T, D), float32),
        ((T, D), bfloat),
        ((K, D), bfloat),
        ((T, W), bfloat),
        ((K, W), bfloat),
        ((K, W), bfloat),
        ((T, W), bfloat),
    ]
    return pl.pallas_call(
        kernel,
        grid=(H,),
        out_shape=[jax.ShapeDtypeStruct(s, d) for s, d in shapes],
        in_specs=in_specs,
        out_specs=[anywhere()] * 5 + [lanes_of(T), lanes_of(K), lanes_of(K), lanes_of(T)],
        scratch_shapes=scratch,
        compiler_params=pltpu.CompilerParams(vmem_limit_bytes=VMEM_LIMIT),
        cost_estimate=pl.CostEstimate(flops=20_000_000_000, bytes_accessed=20_000_000, transcendentals=10_000_000),
        name="front",
    )(*args)


def emit_blocks(z, meta_ref, keep_o, send_o, sources):
    chip, core, plane = meta_ref[6], meta_ref[7], meta_ref[8]
    quarter = keep_o.shape[2]

    def write(out, m, row, here, lanes):
        first = 0
        while first < here.shape[0]:
            part, inside = divmod(row + first, quarter)
            size = min(here.shape[0] - first, quarter - inside)
            out[m, part ^ plane, inside : inside + size, lanes] = here[first : first + size].astype(out.dtype)
            first += size

    for m in range(z.n // 2):
        owner = (chip ^ m) * 2
        for out, place in ((keep_o, owner + core), (send_o, owner + 1 - core)):
            row = 0
            for ref, rows, pieces in sources:
                width = ref.shape[-1]
                if width >= z.D:
                    start = pl.multiple_of(place * rows, 16)
                    for lane in range(0, width, z.D):
                        write(out, m, row, ref[pl.ds(start, rows), lane : lane + z.D], slice(0, z.D))
                        row += rows
                else:
                    size = rows // pieces
                    for g in range(pieces):
                        start = pl.multiple_of(place * rows + g * size, 16)
                        write(out, m, row, ref[pl.ds(start, size), :], slice(g * width, (g + 1) * width))
                    row += size
            if row < quarter * z.planes:
                rest = quarter * z.planes - row
                write(out, m, row, jnp.zeros((rest, z.D), float32), slice(0, z.D))


def block_shapes(z, rows):
    shape = (z.n // 2, z.planes, rows // z.planes, z.D)
    return [(shape, float32), (shape, bfloat)]


def middle(z, meta, count, stream, att, target, weights):
    D, T, W, F, O = z.D, z.tokens, z.wide, z.F, z.out
    B = z.middle_block
    hd = z.hd

    def kernel(meta_ref, count_ref, stream_ref, att_ref, target_ref, *refs):
        refs = list(refs)
        if z.direct:
            first_refs, second_refs = refs[: z.n], refs[z.n : 2 * z.n]
            refs = refs[2 * z.n :]
            do_out, mid_out, misc_o, keep_o, send_o = refs[:5]
            refs = refs[5:]
        else:
            wo, wu, wd, wh, gains_ref = refs[:5]
            do_out, mid_out, misc_o, go_s, gu_s, gd_s, gh_s = refs[5:12]
            refs = refs[12:]
        wop, att_s, stream_s, do_o, mid_o, act_s, hg_s, fin_s, fg_s, low_s, pg_s, bg_s, sem = refs[:13]
        refs = refs[13:]
        if z.direct:
            go_s, gu_s, gd_s, gh_s, blob_s, gain_s, wo, wu, wd, wh = refs

        att_copy = pltpu.make_async_copy(att_ref, att_s, sem.at[0])
        stream_copy = pltpu.make_async_copy(stream_ref, stream_s, sem.at[1])
        if z.direct:
            w, uw, fw, hw = z.w, z.uw, z.fw, z.hw
            ends = (0, w, w + uw, w + uw + fw, z.second_rows)
            pieces = [
                share_copies(z, meta_ref, second_refs, blob_s.at[:, p:q], slice(p, q), sem, 9 + c * z.n)
                for c, (p, q) in enumerate(zip(ends[:-1], ends[1:]))
            ]
            last = slice(z.first_rows - 16, z.first_rows)
            gain_in = share_copies(z, meta_ref, first_refs, gain_s, last, sem, 9 + 4 * z.n)
            for copy in pieces[0] + gain_in:
                copy.start()
        att_copy.start()
        stream_copy.start()
        if z.direct:
            for piece in pieces[1:]:
                for copy in piece:
                    copy.start()
            for copy in pieces[0] + gain_in:
                copy.wait()
            total = jnp.zeros((16, D), float32)
            for j in range(z.n):
                wo[j * w : (j + 1) * w, :] = blob_s[j, 0:w, :]
                total = total + gain_s[j].astype(float32)
        else:
            total = gains_ref[...]
        wop[...] = tn(spread_matrix(D, hd), wo[...]).astype(bfloat)
        misc_o[...] = jnp.zeros_like(misc_o)
        gain_ffn, scale_attn, scale_ffn = total[2:3, :], total[3:4, :], total[4:5, :]
        base, valid = meta_ref[0], meta_ref[1]
        samples = count_ref[0]
        att_copy.wait()
        stream_copy.wait()
        if z.direct:
            for copy in pieces[1]:
                copy.wait()
            for j in range(z.n):
                for c in range(F // D):
                    first = w + c * w
                    wu[j * w : (j + 1) * w, c * D : (c + 1) * D] = blob_s[j, first : first + w, :]
        if z.direct:
            for copy in pieces[2] + pieces[3]:
                copy.wait()
            for j in range(z.n):
                wd[j * fw : (j + 1) * fw, :] = blob_s[j, w + uw : w + uw + fw, :]
                for g in range(D // O):
                    start = j * w + g * hw
                    wh[start : start + hw, :] = blob_s[j, w + uw + fw :, g * O : (g + 1) * O]
        chunks = B // z.tokens_dev

        def block(i, carry):
            rows = pl.ds(pl.multiple_of(i * B, B), B)
            branch = mm(att_s[rows, :], wop[...])
            stream_mid = stream_s[rows, :] + scale_attn * branch
            unit, scale = norm_parts(stream_mid)
            ffn_in = (unit * gain_ffn).astype(bfloat)
            fin_s[rows, :] = ffn_in
            hidden = mm(ffn_in, wu[...])
            active, slope = gelu_both(hidden)
            active = active.astype(bfloat)
            act_s[rows, :] = active
            ffn_out = mm(active, wd[...])
            stream_low = (stream_mid + scale_ffn * ffn_out).astype(bfloat)
            low_s[rows, :] = stream_low
            predicted = mm(stream_low, wh[...])
            column = iota((B, O), 1)
            position = (base + i * B + iota((B, O), 0)) * SUB + column % SUB
            stem = column // (2 * SUB)
            weight = jnp.zeros((B, O), float32)
            for k in range(STEMS):
                weight = jnp.where(stem == k, meta_ref[2 + k].astype(float32), weight)
            weight = jnp.where(position < valid, weight, 0.0)
            error = predicted - target_ref[pl.ds(i * chunks, chunks)].reshape(B, O).astype(float32)
            root = jnp.sqrt(error * error + 1.0)
            misc_o[5:6, :O] += jnp.sum(weight * (root - 1.0), 0, keepdims=True)
            predicted_grad = (weight * error / root / samples).astype(bfloat)
            pg_s[rows, :] = predicted_grad
            end_grad = nt(predicted_grad, wh[...])
            misc_o[4:5, :] += jnp.sum(end_grad * ffn_out, 0, keepdims=True)
            ffn_grad = (scale_ffn * end_grad).astype(bfloat)
            fg_s[rows, :] = ffn_grad
            hidden_grad = (nt(ffn_grad, wd[...]) * slope).astype(bfloat)
            hg_s[rows, :] = hidden_grad
            mid_part, gain_grad = norm_back(unit, scale, gain_ffn, nt(hidden_grad, wu[...]))
            misc_o[2:3, :] += gain_grad
            mid_grad = end_grad + mid_part
            mid_o[rows, :] = mid_grad
            misc_o[3:4, :] += jnp.sum(mid_grad * branch, 0, keepdims=True)
            branch_grad = (scale_attn * mid_grad).astype(bfloat)
            bg_s[rows, :] = branch_grad
            att_grad = nt(branch_grad, wop[...]).astype(bfloat)
            for h in range(H):
                lanes = slice(h * LANES, (h + 1) * LANES)
                one = att_grad[:, lanes].astype(float32)
                delta = jnp.sum(one * att_s[rows, lanes].astype(float32), -1, keepdims=True)
                do_o[rows, lanes] = with_column(one, delta, hd)
            return carry

        lax.fori_loop(0, T // B, block, 0)
        outgoing = [
            pltpu.make_async_copy(do_o, do_out, sem.at[7]),
            pltpu.make_async_copy(mid_o, mid_out, sem.at[8]),
        ]
        for copy in outgoing:
            copy.start()
        spare_grad = tn(att_s[...], bg_s[...])
        for h in range(H):
            go_s[h * hd : (h + 1) * hd, :] = spare_grad[h * LANES : h * LANES + hd, :]
        gu_s[...] = tn(fin_s[...], hg_s[...])
        gd_s[...] = tn(act_s[...], fg_s[...])
        gh_s[...] = tn(low_s[...], pg_s[...])
        if z.direct:
            emit_blocks(
                z,
                meta_ref,
                keep_o,
                send_o,
                ((go_s, z.w, 1), (gu_s, z.w, 1), (gd_s, z.fw, 1), (gh_s, z.w, D // O)),
            )
        for copy in outgoing:
            copy.wait()

    if z.parts == 1:
        target_spec = pl.BlockSpec((z.segments, z.tokens_dev, O), lambda i: (0, 0, D // O))
    else:
        target_spec = whole(target.shape)
    in_specs = [smem(), smem(), anywhere(), anywhere(), target_spec]
    args = [meta, count, stream, att, target]
    scratch = [
        pltpu.VMEM((W, D), bfloat),
        pltpu.VMEM((T, W), bfloat),
        pltpu.VMEM((T, D), float32),
        pltpu.VMEM((T, W), bfloat),
        pltpu.VMEM((T, D), float32),
        pltpu.VMEM((T, F), bfloat),
        pltpu.VMEM((T, F), bfloat),
        pltpu.VMEM((T, D), bfloat),
        pltpu.VMEM((T, D), bfloat),
        pltpu.VMEM((T, D), bfloat),
        pltpu.VMEM((T, O), bfloat),
        pltpu.VMEM((T, D), bfloat),
        pltpu.SemaphoreType.DMA((9 + 5 * z.n,)),
    ]
    shapes = [((T, W), bfloat), ((T, D), float32), ((8, D), float32)]
    grads = [((D, D), float32), ((D, F), float32), ((F, D), float32), ((D, O), float32)]
    if z.direct:
        args += weights[0] + weights[1]
        in_specs += [anywhere()] * (2 * z.n)
        scratch += [pltpu.VMEM(s, d) for s, d in grads] + [
            pltpu.VMEM((z.n, z.second_rows, D), bfloat),
            pltpu.VMEM((z.n, 16, D), bfloat),
            pltpu.VMEM((D, D), bfloat),
            pltpu.VMEM((D, F), bfloat),
            pltpu.VMEM((F, D), bfloat),
            pltpu.VMEM((D, O), bfloat),
        ]
        shapes += block_shapes(z, z.second_grads)
    else:
        for array in weights[3:]:
            args.append(array)
            in_specs.append(whole(array.shape))
        shapes += grads
    return pl.pallas_call(
        kernel,
        grid=(1,),
        out_shape=[jax.ShapeDtypeStruct(s, d) for s, d in shapes],
        in_specs=in_specs,
        out_specs=[anywhere(), anywhere()] + [whole(s) for s, d in shapes[2:]],
        scratch_shapes=scratch,
        compiler_params=pltpu.CompilerParams(vmem_limit_bytes=VMEM_LIMIT),
        cost_estimate=pl.CostEstimate(flops=20_000_000_000, bytes_accessed=20_000_000, transcendentals=4_000_000),
        name="middle",
    )(*args)


def head_back(z, q_ref, k_ref, v_ref, do_ref, put_query, dk_s, dv_s):
    T, hd = z.tokens, z.hd
    QB = 256 if z.keys <= 1024 else 128
    dk_s[...] = jnp.zeros_like(dk_s)
    dv_s[...] = jnp.zeros_like(dv_s)

    def block(i, carry):
        for b in range(2):
            rows = pl.ds(pl.multiple_of((i * 2 + b) * QB, QB), QB)
            q, do = q_ref[rows, :], do_ref[rows, :]
            probs = jnp.exp(nt(q, k_ref[...]))
            score_grad = (probs * nt(do, v_ref[...])).astype(bfloat)
            low = probs.astype(bfloat)
            put_query(rows, mm(score_grad, k_ref[...]).astype(bfloat))
            dk_s[...] += tn(q, score_grad)[:hd, :]
            dv_s[...] += tn(do, low)[:hd, :]
        return carry

    lax.fori_loop(0, T // (2 * QB), block, 0)
    return dk_s[...].astype(bfloat), dv_s[...].astype(bfloat)


def attend_back(z, q, k, v, do, heads):
    T, K, W, D = z.tokens, z.keys, z.wide, z.D
    hd = z.hd

    def kernel(q_ref, k_ref, v_ref, do_ref, dq_o, dkv_o, dk_s, dv_s):
        def put_query(rows, value):
            dq_o[rows, :] = value

        dkv_o[0], dkv_o[1] = head_back(z, q_ref, k_ref, v_ref, do_ref, put_query, dk_s, dv_s)

    def lanes(rows):
        return pl.BlockSpec((rows, LANES), lambda h: (0, h))

    return pl.pallas_call(
        kernel,
        grid=(heads,),
        out_shape=[
            jax.ShapeDtypeStruct((T, heads * LANES), bfloat),
            jax.ShapeDtypeStruct((2, heads * hd, K), bfloat),
        ],
        in_specs=[lanes(T), lanes(K), lanes(K), lanes(T)],
        out_specs=[lanes(T), pl.BlockSpec((2, hd, K), lambda h: (0, h, 0))],
        scratch_shapes=[pltpu.VMEM((hd, K), float32)] * 2,
        compiler_params=pltpu.CompilerParams(vmem_limit_bytes=VMEM_LIMIT),
        cost_estimate=pl.CostEstimate(
            flops=heads * 4_000_000_000, bytes_accessed=12_000_000, transcendentals=heads * 1_000_000
        ),
        name="attend_back",
    )(q, k, v, do)


def back(z, done, meta, q, k, v, do, dq, dkv, x, spectral, halo, stream, slope, normed, sn, mid, misc, weights):
    D, T, K, W, B, O = z.D, z.tokens, z.keys, z.wide, z.block, z.out
    frame, taps, hd = z.frame, z.taps, z.hd
    half = frame // 2
    steps = H - done
    extra = 2 if z.parts > 1 else 0
    n_weights = z.n if z.direct else 3
    n_out = 2 if z.direct else 4

    def kernel(meta_ref, q_ref, k_ref, v_ref, do_ref, misc_ref, *refs):
        refs = list(refs)
        before_after = refs[:extra]
        remote = refs[extra : extra + 9]
        refs = refs[extra + 9 :]
        weight_refs, refs = refs[:n_weights], refs[n_weights:]
        outs, refs = refs[:n_out], refs[n_out:]
        (dq_s, dkv_s, x_ref, sp_ref, stream_ref, slope_ref, normed_ref, sn_ref, mid_ref) = refs[:9]
        refs = refs[9:]
        cg_s, dn_s, dqc_s, dkvt_s, dk_s, dv_s, sem = refs[:7]
        refs = refs[7:]
        if z.direct:
            gc_s, gq_s, gkv_s, misc_s, place_s, blob_s, wq, wkv = refs
        else:
            gc_s, gq_s, gkv_s, misc_s = outs
            wq, wkv, gains_ref = weight_refs
        i = pl.program_id(0)
        old = done * LANES
        homes = [dq_s.at[:, :old], dkv_s.at[:, : done * hd]] + [
            x_ref, sp_ref, stream_ref, slope_ref, normed_ref, sn_ref, mid_ref
        ]
        copies = [
            pltpu.make_async_copy(a, b, sem.at[c])
            for c, (a, b) in enumerate(zip(remote, homes))
            if c != 3
        ]
        copies += spectral_copies(z, remote[3], sp_ref, sem, 10)
        if z.direct:
            copies += share_copies(
                z, meta_ref, weight_refs, blob_s, slice(z.cw, z.first_rows), sem, 10 + z.segments
            )

        @pl.when(i == 0)
        def _():
            for copy in copies:
                copy.start()

        lanes = pl.ds(pl.multiple_of((i + done) * LANES, LANES), LANES)

        def put_query(rows, value):
            dq_s[rows, lanes] = value

        dk, dv = head_back(z, q_ref, k_ref, v_ref, do_ref, put_query, dk_s, dv_s)
        here = pl.ds(pl.multiple_of((i + done) * hd, 16), hd)
        dkv_s[0, here, :] = dk
        dkv_s[1, here, :] = dv

        @pl.when(i == steps - 1)
        def _():
            for copy in copies:
                copy.wait()
            if z.direct:
                w = z.w
                total = jnp.zeros((16, D), float32)
                for j in range(z.n):
                    here = slice(j * w, (j + 1) * w)
                    wq[here, :] = blob_s[j, 0:w, :]
                    wkv[here, :D] = blob_s[j, w : 2 * w, :]
                    wkv[here, D:] = blob_s[j, 2 * w : 3 * w, :]
                    total = total + blob_s[j, 3 * w :, :].astype(float32)
            else:
                total = gains_ref[...]
            gain_query = total[0:1, :]
            misc_s[...] = misc_ref[...]
            dqc_s[...] = nt(dq_s[...], spread_matrix(D, hd)).astype(bfloat)
            dkvt_s[:, :D] = dkv_s[0].T
            dkvt_s[:, D:] = dkv_s[1].T
            gkv_s[...] = tn(sn_ref[...], dkvt_s[...])
            gq_s[...] = tn(normed_ref[...], dqc_s[...])

            for c in range(K // T):
                cg_s[...] = nt(dkvt_s[c * T : (c + 1) * T, :], wkv[...])

                def key_block(i, carry):
                    rows = pl.ds(pl.multiple_of(i * B, B), B)
                    source = pl.ds(pl.multiple_of(c * T + i * B, B), B)
                    unit, _ = norm_parts(sp_ref[source, :].astype(float32))
                    misc_s[1:2, :] += jnp.sum(cg_s[rows, :] * unit, 0, keepdims=True)
                    return carry

                lax.fori_loop(0, T // B, key_block, 0)
            dn_s[...] = nt(dqc_s[...], wq[...])

            def token_block(i, carry):
                rows = pl.ds(pl.multiple_of(i * B, B), B)
                unit, scale = norm_parts(stream_ref[rows, :])
                part, gain_grad = norm_back(unit, scale, gain_query, dn_s[rows, :])
                misc_s[0:1, :] += gain_grad
                conv_grad = (mid_ref[rows, :] + part) * slope_ref[rows, :]
                cg_s[rows, :] = conv_grad.astype(bfloat).astype(float32)
                return carry

            lax.fori_loop(0, T // B, token_block, 0)
            conv_grad = cg_s[...]
            gc_s[half : half + frame, :] = tn(x_ref[...], conv_grad.astype(bfloat))
            row = iota((T, D), 0)
            later = jnp.where(row == T - 1, 0.0, pltpu.roll(conv_grad, T - 1, 0)).astype(bfloat)
            gc_s[:half, :] = tn(x_ref[:, half:], later)
            sooner = jnp.where(row == 0, 0.0, pltpu.roll(conv_grad, 1, 0)).astype(bfloat)
            gc_s[half + frame :, :] = tn(x_ref[:, :half], sooner)
            if z.parts > 1:
                first = iota((16, D), 0) == 0
                top = jnp.where(first, conv_grad[0:16, :], 0.0).astype(bfloat)
                gc_s[:half, :] += tn(before_after[0][...], top)
                tail = jnp.where(first, pltpu.roll(conv_grad[T - 16 :, :], 1, 0), 0.0)
                gc_s[half + frame :, :] += tn(before_after[1][...], tail.astype(bfloat))
            if z.direct:
                for j in range(z.n):
                    row, lane = iota((D, LANES), 0), iota((D, LANES), 1)
                    hit = jnp.logical_and(row == lane + j * z.w, lane < z.w)
                    chosen = lax.dot_general(
                        misc_s[...], jnp.where(hit, 1.0, 0.0), (((1,), (0,)), ((), ())),
                        precision=lax.Precision.HIGHEST, preferred_element_type=float32,
                    )
                    low_rows = jnp.where(iota((8, LANES), 0) == 5, misc_s[:, :LANES], chosen)
                    place_s[j * 16 : (j + 1) * 16, :] = jnp.zeros((16, D), float32)
                    place_s[j * 16 : j * 16 + 8, :LANES] = low_rows
                emit_blocks(
                    z, meta_ref, outs[0], outs[1],
                    ((gc_s, z.cw, 1), (gq_s, z.w, 1), (gkv_s, z.w, 1), (place_s, 16, 1)),
                )

    def lanes_of(rows):
        return pl.BlockSpec((rows, LANES), lambda i: (0, i + done))

    args = [meta, q, k, v, do, misc]
    in_specs = [smem(), lanes_of(T), lanes_of(K), lanes_of(K), lanes_of(T), whole(misc.shape)]
    if z.parts > 1:
        args += list(halo)
        in_specs += [whole((16, D))] * 2
    remote = (dq, dkv, x, spectral, stream, slope, normed, sn, mid)
    args += list(remote)
    in_specs += [anywhere()] * 9
    scratch = [pltpu.VMEM((T, W), bfloat), pltpu.VMEM((2, D, K), bfloat)]
    homes = (x.shape, (K, D)) + tuple(a.shape for a in remote[4:])
    scratch += [pltpu.VMEM(s, a.dtype) for s, a in zip(homes, remote[2:])]
    scratch += [
        pltpu.VMEM((T, D), float32),
        pltpu.VMEM((T, D), float32),
        pltpu.VMEM((T, D), bfloat),
        pltpu.VMEM((K, 2 * D), bfloat),
        pltpu.VMEM((hd, K), float32),
        pltpu.VMEM((hd, K), float32),
        pltpu.SemaphoreType.DMA((10 + z.segments + z.n,)),
    ]
    grads = [((taps, D), float32), ((D, D), float32), ((D, 2 * D), float32), ((8, D), float32)]
    if z.direct:
        args += weights[0]
        in_specs += [anywhere()] * z.n
        scratch += [pltpu.VMEM(s, d) for s, d in grads] + [
            pltpu.VMEM((z.n * 16, D), float32),
            pltpu.VMEM((z.n, z.first_rows - z.cw, D), bfloat),
            pltpu.VMEM((D, D), bfloat),
            pltpu.VMEM((D, 2 * D), bfloat),
        ]
        shapes = block_shapes(z, z.first_grads)
    else:
        for array in (weights[1], weights[2], weights[7]):
            args.append(array)
            in_specs.append(whole(array.shape))
        shapes = grads
    return pl.pallas_call(
        kernel,
        grid=(steps,),
        out_shape=[jax.ShapeDtypeStruct(s, d) for s, d in shapes],
        in_specs=in_specs,
        out_specs=[whole(s) for s, d in shapes],
        scratch_shapes=scratch,
        compiler_params=pltpu.CompilerParams(vmem_limit_bytes=VMEM_LIMIT),
        cost_estimate=pl.CostEstimate(flops=30_000_000_000, bytes_accessed=20_000_000, transcendentals=8_000_000),
        name="back",
    )(*args)


def pairs(count, mask):
    return [(i, i ^ mask) for i in range(count)]


def tree_sum(values):
    while len(values) > 1:
        values = [values[i] + values[i + 1] for i in range(0, len(values), 2)]
    return values[0]


def from_chips(z, own):
    return [own] + [lax.ppermute(own, "tm", pairs(z.n, 2 * m)) for m in range(1, z.n // 2)]


def with_core(z, same):
    other = [lax.ppermute(share, "tm", pairs(z.n, 1)) for share in same]
    return [share for pair in zip(same, other) for share in pair]


def over_core(z, keep, send):
    there = lax.ppermute(send, "tm", pairs(z.n, 1))
    sums = [keep[m] + there[m].astype(float32) for m in range(z.n // 2)]
    return sums[:1] + [value.astype(bfloat) for value in sums[1:]]


def over_plane(z, blocks):
    mine = blocks[:1]
    for m in range(1, z.n // 2):
        mine.append(lax.ppermute(blocks[m], "tm", pairs(z.n, 2 * m)).astype(float32))
    return tree_sum(mine)


def over_planes(z, mine):
    parts = [mine[0]]
    for m in range(1, z.planes):
        there = lax.ppermute(mine[m].astype(bfloat), "seg", pairs(z.planes, m))
        parts.append(there.astype(float32))
    low = tree_sum(parts).astype(bfloat)
    return [low] + [lax.ppermute(low, "seg", pairs(z.planes, m)) for m in range(1, z.planes)]


def adam_update(master, first, second, grad, factor, rate):
    clipped = grad * factor
    first_new = beta_first * first + (1.0 - beta_first) * clipped
    second_new = beta_second * second + (1.0 - beta_second) * clipped * clipped
    moment_hat = first_new / (1.0 - beta_first**STEP)
    square_hat = second_new / (1.0 - beta_second**STEP)
    master_new = master - rate * (
        moment_hat / (jnp.sqrt(square_hat) + adam_epsilon) + weight_decay * master
    )
    return (master_new, first_new, second_new)


RATES = (
    learn_rate, learn_rate, learn_rate, fast_rate, learn_rate, learn_rate, learn_rate, fast_rate,
)


def gather_quarters(z, meta_ref, refs, out_ref):
    quarter = refs[0].shape[0]
    for m, ref in enumerate(refs):
        start = pl.multiple_of((meta_ref[8] ^ m) * quarter, 16)
        out_ref[pl.ds(start, quarter), :] = ref[...].astype(float32)


def square_sums(z, meta, first, second):
    D = z.D

    def kernel(meta_ref, *refs):
        planes = z.planes
        a_o, b_o, sq_o = refs[2 * planes :]
        gather_quarters(z, meta_ref, refs[:planes], a_o)
        gather_quarters(z, meta_ref, refs[planes : 2 * planes], b_o)
        loss_row = z.cw + 3 * z.w + 5
        total = jnp.zeros((8, D), float32)
        for ref, skip in ((a_o, loss_row), (b_o, -1)):
            for r in range(0, ref.shape[0], 8):
                here = ref[r : r + 8, :]
                if r <= skip < r + 8:
                    here = jnp.where(iota((8, D), 0) == skip - r, 0.0, here)
                total = total + here * here
        sq_o[0:8, :] = total[:, :LANES] + total[:, LANES : 2 * LANES] + total[:, 2 * LANES :]
        loss = a_o[loss_row - 5 : loss_row + 3, :LANES]
        sq_o[8:16, :] = jnp.where(iota((8, LANES), 0) == 5, loss * (1.0 / z.n), 0.0)

    vmem = pl.BlockSpec(memory_space=pltpu.VMEM)
    shapes = [(z.first_grads, D), (z.second_grads, D), (16, LANES)]
    return pl.pallas_call(
        kernel,
        out_shape=[jax.ShapeDtypeStruct(s, float32) for s in shapes],
        in_specs=[smem()] + [vmem] * (2 * z.planes),
        out_specs=[vmem] * 3,
        compiler_params=pltpu.CompilerParams(vmem_limit_bytes=16 * 1024 * 1024),
        name="square_sums",
    )(meta, *first, *second)


def update(z, squares, first_sum, second_sum, masters, firsts, seconds):
    D, O, w, cw = z.D, z.out, z.w, z.cw
    given = len(squares)

    def kernel(*refs):
        sq_refs = refs[:given]
        a_ref, b_ref = refs[given : given + 2]
        ins = refs[given + 2 : given + 26]
        loss_o, norm_o = refs[given + 26 : given + 28]
        outs = refs[given + 28 :]
        sums = tree_sum([ref[...] for ref in sq_refs])
        norm = jnp.sqrt(jnp.sum(sums[0:8, :], keepdims=True))
        loss_o[...] = jnp.sum(sums[8:16, :], keepdims=True)
        norm_o[...] = norm
        factor = jnp.minimum(1.0, clip_limit / (norm + 1e-06))
        places = {
            0: [(a_ref, 0, cw, 0)],
            1: [(a_ref, cw, w, 0)],
            2: [(a_ref, cw + w + c * w, w, c * D) for c in range(2)],
            3: [(b_ref, 0, w, 0)],
            4: [(b_ref, w + c * w, w, c * D) for c in range(z.F // D)],
            5: [(b_ref, w + z.uw, z.fw, 0)],
        }

        def step(index, here, grad):
            values = adam_update(
                ins[index][here], ins[8 + index][here], ins[16 + index][here], grad, factor, RATES[index]
            )
            for kind, value in enumerate(values):
                outs[8 * kind + index][here] = value

        def block(index, ref, start, lane):
            def body(i, carry):
                here = pl.ds(pl.multiple_of(i * 16, 16), 16)
                step(index, (here, slice(lane, lane + D)), ref[pl.ds(pl.multiple_of(start + i * 16, 16), 16), :])
                return carry

            return body

        for index, pieces in places.items():
            for ref, start, count, lane in pieces:
                lax.fori_loop(0, count // 16, block(index, ref, start, lane), 0)
        start = w + z.uw + z.fw
        for g in range(D // O):
            here = (slice(g * z.hw, (g + 1) * z.hw), slice(0, O))
            step(6, here, b_ref[start : start + z.hw, g * O : (g + 1) * O])
        gains = a_ref[cw + 3 * w : cw + 3 * w + 8, :][:5, :w]
        step(7, (slice(0, 5), slice(0, w)), gains)

    vmem = pl.BlockSpec(memory_space=pltpu.VMEM)
    outs = [jax.ShapeDtypeStruct((1, 1), float32)] * 2
    outs += [jax.ShapeDtypeStruct(m.shape, float32) for m in masters] * 3
    return pl.pallas_call(
        kernel,
        out_shape=outs,
        in_specs=[vmem] * (given + 26),
        out_specs=[vmem] * 26,
        compiler_params=pltpu.CompilerParams(vmem_limit_bytes=20 * 1024 * 1024),
        name="update",
    )(*squares, first_sum, second_sum, *masters, *firsts, *seconds)


def on_device(*arguments):
    feats, spectral, target, valid_samples, stem_weights = arguments[:5]
    masters, firsts, seconds = arguments[5:13], arguments[13:21], arguments[21:29]
    n = lax.axis_size("tm")
    planes = lax.axis_size("seg")
    z = Sizes(n, planes, feats, spectral, target, masters[0], masters[4])
    S, T, D = z.segments, z.tokens, z.D
    place = lax.axis_index("tm")
    portion, member = place // S, place % S

    if z.direct:
        blobs = pack_weights(z, jnp.reshape(place, (1,)).astype(jnp.int32), masters)
        same_first = from_chips(z, blobs[0])
    else:
        weights = [lax.all_gather(a.astype(bfloat), "tm", axis=0, tiled=True) for a in masters[:7]]
        gains = lax.all_gather(masters[7].astype(bfloat), "tm", axis=1, tiled=True)
        weights.append(jnp.pad(gains.astype(float32), ((0, 3), (0, 0))))
    groups = None if z.parts == 1 else [[p * S + i for i in range(S)] for p in range(z.parts)]

    packed = pack_tokens(z, jnp.transpose(feats, (0, 2, 1)), spectral, target)
    if z.direct:
        packed, *same_first = lax.optimization_barrier((packed, *same_first))
    moved = lax.all_to_all(packed, "tm", 0, 0, axis_index_groups=groups, tiled=True)
    if z.direct:
        weights = [with_core(z, same_first)]
        blob, valid_samples, _ = lax.optimization_barrier((blobs[1], valid_samples, weights[0][1]))
        same_second = from_chips(z, blob)
    rows = z.tokens_dev
    spectral_all, target, halo = moved, moved, None
    if z.parts > 1:
        target = moved[:, :rows, D:]
        spectral_all = lax.all_gather(
            moved[:, :rows, :D].reshape(T, D), "tm", axis=0, tiled=True,
            axis_index_groups=[[p * S + i for p in range(z.parts)] for i in range(S)],
        )
        last = moved[S - 1, rows:, 4 * rows - 2 :].T.reshape(1, -1)
        lead = moved[0, rows:, :2].T.reshape(1, -1)
        halo = (
            lax.ppermute(jnp.pad(last, ((0, 15), (0, 0))), "tm", [(i, i + S) for i in range(n - S)]),
            lax.ppermute(jnp.pad(lead, ((0, 15), (0, 0))), "tm", [(i + S, i) for i in range(n - S)]),
        )
    local_count = jnp.sum(valid_samples)[None]
    if z.direct:
        counts = [local_count] + [lax.ppermute(local_count, "seg", pairs(planes, m)) for m in range(1, planes)]
        sample_count = tree_sum(counts).astype(float32)
    else:
        sample_count = lax.psum(local_count, "seg").astype(float32)
    meta = jnp.concatenate(
        [
            jnp.stack([portion * T, lax.dynamic_index_in_dim(valid_samples, member, keepdims=False)]),
            lax.dynamic_index_in_dim(stem_weights, member, keepdims=False),
            jnp.stack([place // 2, place % 2, lax.axis_index("seg")]),
        ]
    ).astype(jnp.int32)
    meta, sample_count = lax.optimization_barrier((meta, sample_count))

    x, stream, slope, normed, sn, q, k, v, att = front(z, meta, moved, spectral_all, halo, weights)
    if z.direct:
        att, *same_second = lax.optimization_barrier((att, *same_second))
        weights.append(with_core(z, same_second))
    second = middle(z, meta, sample_count, stream, att, target, weights)
    do, mid, misc = second[:3]
    done = 2
    dq, dkv = attend_back(z, q, k, v, do, done)
    if z.direct:
        second_blocks = over_core(z, second[3], second[4])
        dq, *second_blocks = lax.optimization_barrier((dq, *second_blocks))
    first = back(
        z, done, meta, q, k, v, do, dq, dkv, x, spectral_all, halo, stream, slope, normed, sn, mid, misc, weights
    )

    if z.direct:
        second_mine = over_plane(z, second_blocks)
        send, second_mine = lax.optimization_barrier((first[1], second_mine))
        first_blocks = over_core(z, first[0], send)
        second_parts = over_planes(z, second_mine)
        first_parts = over_planes(z, over_plane(z, first_blocks))
        first_sum, second_sum, both = square_sums(z, meta, first_parts, second_parts)
        both = both + lax.ppermute(both, "tm", pairs(n, 1))
        squares = [both] + [lax.ppermute(both, "tm", pairs(n, 2 * m)) for m in range(1, n // 2)]
        result = update(z, squares, first_sum, second_sum, masters, firsts, seconds)
        return (result[0].reshape(()), sample_count.reshape(()), result[1].reshape(()), *result[2:])

    grads = (first[0], first[1], first[2], second[3], second[4], second[5], second[6])
    shards = [lax.psum_scatter(g, "tm", scatter_dimension=0, tiled=True) for g in grads]
    shards.append(lax.psum_scatter(first[3][:5], "tm", scatter_dimension=1, tiled=True))
    reduced = lax.psum(tuple(shards), "seg")
    loss_sum = lax.psum(jnp.sum(first[3][5]), ("seg", "tm"))
    squares = lax.psum(sum(jnp.sum(shard * shard) for shard in reduced), "tm")
    grad_norm = jnp.sqrt(squares)
    factor = jnp.minimum(1.0, clip_limit / (grad_norm + 1e-06))
    updated = [
        adam_update(m, f, s, g, factor, r)
        for m, f, s, g, r in zip(masters, firsts, seconds, reduced, RATES)
    ]
    return (
        loss_sum, sample_count.reshape(()), grad_norm,
        *[u[0] for u in updated], *[u[1] for u in updated], *[u[2] for u in updated],
    )


def solution(mesh):
    rows, columns = P("tm", None), P(None, "tm")
    leaves = (rows,) * 7 + (columns,)
    tokens = P("seg", "tm", None)
    return jax.shard_map(
        on_device,
        mesh=mesh,
        in_specs=(tokens, tokens, tokens, P("seg"), P("seg", None)) + leaves * 3,
        out_specs=(P(), P(), P()) + leaves * 3,
        check_vma=False,
    )
```

profile of v0, /device:TPU:0, one launch (start us, length us, event | category | flops | bytes accessed | tf_op | source)
XLA Modules:
  0.0 213.1 jit_solution(5593538055428054175)
XLA Ops:
  0.7 2.2 %pack_weights.1 = (bf16[352,384]{1,0:T(8,128)(2,1)}, bf16[448,384]{1,0:T(8,128)(2,1)}) custom-call(s32[1]{0:T(128)} %bitcast.1.place_ref, f32[192,384]{1,0:T(8,128)} %refs_6_.1, f32[48,384]{1,0:T(8,128)} %refs_7_.1, f32[48,768]{1,0:T(8,128)} %refs_8_.1, f32[48,384]{1,0:T(8,128)} %refs_9_.1, f32[48,1536]{1,0:T(8,128)} %refs_10_.1, f32[192,384]{1,0:T(8,128)} %refs_11_.1, ...), custom_call_target="tpu_custom_call" | custom-call | tf_op jit(solution)/shard_map/pack_weights/pallas_call | solution.py:156
  2.9 3.9 %collective-permute-start.2 = (bf16[352,384]{1,0:T(8,128)(2,1)}, bf16[352,384]{1,0:T(8,128)(2,1)}, u32[]{:S(2)}, u32[]{:S(2)}) collective-permute-start(bf16[352,384]{1,0:T(8,128)(2,1)} %get-tuple-element.99.refs_2_.refs_0_.refs_9_), channel_id=1, source_target_pairs={{0,6},{1,7},{2,4},{3,5},{4,2},{5,3},{6,0},{7,1},{8,14},{9,15},{10,... | collective-permute-start | bytes 811016 | tf_op jit(solution)/shard_map/ppermute | solution.py:929
  6.7 0.5 collective-permute-start.1
  7.3 2.8 %pack_tokens.1 = bf16[8,320,512]{2,1,0:T(8,128)(2,1)} custom-call(bf16[8,192,512]{2,1,0:T(8,128)(2,1)} %bitcast.55, bf16[8,128,384]{2,1,0:T(8,128)(2,1)} %s_ref.1, bf16[8,128,128]{2,1,0:T(8,128)(2,1)} %t_ref.1), custom_call_target="tpu_custom_call" | custom-call | tf_op jit(solution)/shard_map/pack_tokens/pallas_call | solution.py:192
  10.2 4.3 %collective-permute-done.2.refs_8_.refs_6_.refs_15_ = bf16[352,384]{1,0:T(8,128)(2,1)} collective-permute-done((bf16[352,384]{1,0:T(8,128)(2,1)}, bf16[352,384]{1,0:T(8,128)(2,1)}, u32[]{:S(2)}, u32[]{:S(2)}) %collective-permute-start.2) | collective-permute-done | bytes 270368 | tf_op jit(solution)/shard_map/ppermute | solution.py:929
  14.4 4.9 %collective-permute-done.1.refs_6_.refs_4_.refs_13_ = bf16[352,384]{1,0:T(8,128)(2,1)} collective-permute-done((bf16[352,384]{1,0:T(8,128)(2,1)}, bf16[352,384]{1,0:T(8,128)(2,1)}, u32[]{:S(2)}, u32[]{:S(2)}) %collective-permute-start.1) | collective-permute-done | bytes 270368 | tf_op jit(solution)/shard_map/ppermute | solution.py:929
  19.6 3.6 %all-to-all-start = ((bf16[8,320,512]{2,1,0:T(8,128)(2,1)}), bf16[8,320,512]{2,1,0:T(8,128)(2,1)S(1)}, u32[]{:S(2)}, u32[]{:S(2)}) async-start(bf16[8,320,512]{2,1,0:T(8,128)(2,1)} %pack_tokens.1), calls=%async_computation | async-start | bytes 5242880 | tf_op jit(solution)/shard_map/all_to_all | solution.py:1099
  23.3 0.4 collective-permute-start.3
  23.8 0.3 collective-permute-start.8
  24.5 0.6 collective-permute-done.3.refs_3_.refs_1_.refs_10_
  25.2 0.6 reduce_sum.9
  25.8 0.6 dynamic_slice.8
  26.4 3.6 %collective-permute-start.6 = (s32[1]{0:T(128)}, s32[1]{0:T(128)}, u32[]{:S(2)}, u32[]{:S(2)}) collective-permute-start(s32[1]{0:T(128)} %bitcast.6), channel_id=1, source_target_pairs={{0,24},{8,16},{16,8},{24,0},{1,25},{9,17},{17,9},{25,1},{2,26},{10... | collective-permute-start | bytes 20 | tf_op jit(solution)/shard_map/ppermute | solution.py:1120
  30.0 1.2 concatenate.3.meta_ref
  31.2 2.4 %collective-permute-done.4 = s32[1]{0:T(128)} collective-permute-done((s32[1]{0:T(128)}, s32[1]{0:T(128)}, u32[]{:S(2)}, u32[]{:S(2)}) %collective-permute-start.4) | collective-permute-done | bytes 36 | tf_op jit(solution)/shard_map/ppermute | solution.py:1120
  35.0 2.7 %collective-permute-start.12 = (bf16[448,384]{1,0:T(8,128)(2,1)S(1)}, bf16[448,384]{1,0:T(8,128)(2,1)S(1)}, u32[]{:S(2)}, u32[]{:S(2)}) collective-permute-start(bf16[448,384]{1,0:T(8,128)(2,1)S(1)} %copy-done.29), channel_id=1, source_target_pairs={{0,6},{1,7},{2,4},{3,5},{4,2},{5,3},{6,0},{7,1},{8,14},{9,15},{10,... | collective-permute-start | bytes 1032200 | tf_op jit(solution)/shard_map/ppermute | solution.py:929
  37.7 0.4 collective-permute-done.5
  38.1 1.7 collective-permute-start.11
  41.2 1.5 collective-permute-start.10
  42.7 13.3 %all-to-all-done.refs_0_.refs_1_.target_ref.refs_3_ = bf16[8,320,512]{2,1,0:T(8,128)(2,1)S(1)} async-done(((bf16[8,320,512]{2,1,0:T(8,128)(2,1)}), bf16[8,320,512]{2,1,0:T(8,128)(2,1)S(1)}, u32[]{:S(2)}, u32[]{:S(2)}) %all-to-all-start) | async-done | bytes 2621472 | tf_op jit(solution)/shard_map/all_to_all | solution.py:1099
  56.0 1.5 copy-done.27
  57.6 25.7 %front.1 = (bf16[1024,768]{1,0:T(8,128)(2,1)}, f32[1024,384]{1,0:T(8,128)}, f32[1024,384]{1,0:T(8,128)}, bf16[1024,384]{1,0:T(8,128)(2,1)}, bf16[1024,384]{1,0:T...) custom-call(s32[9]{0:T(128)} %concatenate.3.meta_ref, ...), custom_call_target="tpu_custom_call" | custom-call | flops 20000000000 | bytes 20000000 | tf_op jit(solution)/shard_map/front/pallas_call | solution.py:433
  83.4 0.5 collective-permute-start.14
  84.0 0.4 collective-permute-start.16
  84.4 0.6 collective-permute-done.13.refs_9_
  85.0 0.7 collective-permute-done.14.refs_11_
  85.7 1.0 collective-permute-done.15.refs_13_
  86.7 0.7 copy-done.33
  87.5 26.1 %middle.1 = (bf16[1024,1024]{1,0:T(8,128)(2,1)}, f32[1024,384]{1,0:T(8,128)}, f32[8,384]{1,0:T(8,128)}, f32[4,4,112,384]{3,2,1,0:T(8,128)}, bf16[4,4,112,384]{3,2,1,0:T(8,128)(2,1)}) custom-call(s32[9]{0:T(128)} %concatenate.3.meta_ref, f32[1]{0:T(128)} %convert_element_type.137.count_ref, f32[1024,384]{1,0:T(8,128)} %get-tuple-element.110.stream_ref.refs_4_, ...), custom_call_target="tpu_custom_call" | custom-call | flops 20000000000 | bytes 20000000 | tf_op jit(solution)/shard_map/middle/pallas_call | solution.py:669
  113.7 7.3 %attend_back.1 = (bf16[1024,256]{1,0:T(8,128)(2,1)}, bf16[2,96,1024]{2,1,0:T(8,128)(2,1)}) custom-call(bf16[1024,1024]{1,0:T(8,128)(2,1)} %get-tuple-element.106.q_ref, bf16[1024,1024]{1,0:T(8,128)(2,1)} %get-tuple-element.107.k_ref, bf16[1024,1024]{1,0:T(8,128)(2,1)} %get-tuple-element.108.v_ref, bf16[1024,1024]{1,0:T(8,128)(2,1)} %get-tuple-element.118.do_ref), custom_call_target="tpu_custom_call" | custom-call | flops 8000000000 | bytes 12000000 | tf_op jit(solution)/shard_map/attend_back/pallas_call | solution.py:717
  121.1 2.5 %fusion.3 = (bf16[4,112,384]{2,1,0:T(8,128)(2,1)S(1)}, bf16[4,112,384]{2,1,0:T(8,128)(2,1)}, bf16[4,112,384]{2,1,0:T(8,128)(2,1)}, f32[4,112,384]{2,1,0:T(8,128)S(1)}) fusion(f32[4,4,112,384]{3,2,1,0:T(8,128)S(1)} %copy-done.26, bf16[4,4,112,384]{3,2,1,0:T(8,128)(2,1)} %collective-permute-done.17), kind=kLoop, calls=%fused_computation.12 | loop fusion | flops 1892352 | bytes 5849088 | tf_op jit(solution)/shard_map/convert_element_type | solution.py:940
  123.6 0.4 collective-permute-start.18
  124.0 0.7 collective-permute-start.19
  124.6 2.4 %collective-permute-start.20 = (bf16[4,112,384]{2,1,0:T(8,128)(2,1)S(1)}, bf16[4,112,384]{2,1,0:T(8,128)(2,1)S(1)}, u32[]{:S(2)}, u32[]{:S(2)}) collective-permute-start(bf16[4,112,384]{2,1,0:T(8,128)(2,1)S(1)} %get-tuple-element.135), channel_id=1, source_target_pairs={{0,6},{1,7},{2,4},{3,5},{4,2},{5,3},{6,0},{7,1},{8,14},{9,15},{10,... | collective-permute-start | bytes 1032200 | tf_op jit(solution)/shard_map/ppermute | solution.py:946
  127.1 28.4 %back.1 = (f32[4,4,96,384]{3,2,1,0:T(8,128)}, bf16[4,4,96,384]{3,2,1,0:T(8,128)(2,1)}) custom-call(s32[9]{0:T(128)} %concatenate.3.meta_ref, bf16[1024,1024]{1,0:T(8,128)(2,1)} %get-tuple-element.106.q_ref, bf16[1024,1024]{1,0:T(8,128)(2,1)} %get-tuple-element.107.k_ref, bf16[1024,1024]{1,0:T(8,128)(2,1)} %get-tuple-element.108.v_ref, ...), custom_call_target="tpu_custom_call" | custom-call | flops 30000001024 | bytes 20000000 | tf_op jit(solution)/shard_map/back/pallas_call | solution.py:905
  155.8 3.0 %collective-permute-done.21 = bf16[4,4,96,384]{3,2,1,0:T(8,128)(2,1)S(1)} collective-permute-done((bf16[4,4,96,384]{3,2,1,0:T(8,128)(2,1)}, bf16[4,4,96,384]{3,2,1,0:T(8,128)(2,1)S(1)}, u32[]{:S(2)}, u32[]{:S(2)}) %collective-permute-start.21) | collective-permute-done | bytes 1179680 | tf_op jit(solution)/shard_map/ppermute | solution.py:938
  159.0 0.5 collective-permute-start.22
  159.5 1.6 collective-permute-start.24
  161.1 1.5 collective-permute-start.23
  162.6 1.6 collective-permute-start.31
  164.3 2.5 %collective-permute-start.33 = (bf16[112,384]{1,0:T(8,128)(2,1)S(1)}, bf16[112,384]{1,0:T(8,128)(2,1)S(1)}, u32[]{:S(2)}, u32[]{:S(2)}) collective-permute-start(bf16[112,384]{1,0:T(8,128)(2,1)S(1)} %get-tuple-element.177), channel_id=1, source_target_pairs={{0,24},{8,16},{16,8},{24,0},{1,25},{9,17},{17,9},{25,1},{2,26},{10... | collective-permute-start | bytes 258056 | tf_op jit(solution)/shard_map/ppermute | solution.py:953
  166.8 2.2 %collective-permute-done.22 = bf16[4,96,384]{2,1,0:T(8,128)(2,1)S(1)} collective-permute-done((bf16[4,96,384]{2,1,0:T(8,128)(2,1)S(1)}, bf16[4,96,384]{2,1,0:T(8,128)(2,1)S(1)}, u32[]{:S(2)}, u32[]{:S(2)}) %collective-permute-start.22) | collective-permute-done | bytes 294944 | tf_op jit(solution)/shard_map/ppermute | solution.py:946
  169.2 2.7 %collective-permute-start.32 = (bf16[112,384]{1,0:T(8,128)(2,1)S(1)}, bf16[112,384]{1,0:T(8,128)(2,1)S(1)}, u32[]{:S(2)}, u32[]{:S(2)}) collective-permute-start(bf16[112,384]{1,0:T(8,128)(2,1)S(1)} %get-tuple-element.178), channel_id=1, source_target_pairs={{0,16},{8,24},{16,0},{24,8},{1,17},{9,25},{17,1},{25,9},{2,18},{10... | collective-permute-start | bytes 258056 | tf_op jit(solution)/shard_map/ppermute | solution.py:953
  171.8 2.7 %collective-permute-done.24 = bf16[4,96,384]{2,1,0:T(8,128)(2,1)S(1)} collective-permute-done((bf16[4,96,384]{2,1,0:T(8,128)(2,1)S(1)}, bf16[4,96,384]{2,1,0:T(8,128)(2,1)S(1)}, u32[]{:S(2)}, u32[]{:S(2)}) %collective-permute-start.24) | collective-permute-done | bytes 294944 | tf_op jit(solution)/shard_map/ppermute | solution.py:946
  174.5 1.4 collective-permute-done.23
  176.1 1.6 collective-permute-start.25
  177.7 2.5 %collective-permute-start.27 = (bf16[96,384]{1,0:T(8,128)(2,1)S(1)}, bf16[96,384]{1,0:T(8,128)(2,1)S(1)}, u32[]{:S(2)}, u32[]{:S(2)}) collective-permute-start(bf16[96,384]{1,0:T(8,128)(2,1)S(1)} %get-tuple-element.180), channel_id=1, source_target_pairs={{0,24},{8,16},{16,8},{24,0},{1,25},{9,17},{17,9},{25,1},{2,26},{10... | collective-permute-start | bytes 221192 | tf_op jit(solution)/shard_map/ppermute | solution.py:953
  180.4 3.0 %collective-permute-start.36 = (bf16[112,384]{1,0:T(8,128)(2,1)S(1)}, bf16[112,384]{1,0:T(8,128)(2,1)S(1)}, u32[]{:S(2)}, u32[]{:S(2)}) collective-permute-start(bf16[112,384]{1,0:T(8,128)(2,1)S(1)} %fusion.8.refs_4_), channel_id=1, source_target_pairs={{0,24},{8,16},{16,8},{24,0},{1,25},{9,17},{17,9},{25,1},{2,26},{10... | collective-permute-start | bytes 258056 | tf_op jit(solution)/shard_map/ppermute | solution.py:956
  183.4 0.3 collective-permute-start.35
  183.7 1.1 collective-permute-start.34
  184.9 5.6 %collective-permute-done.26 = bf16[96,384]{1,0:T(8,128)(2,1)S(1)} collective-permute-done((bf16[96,384]{1,0:T(8,128)(2,1)S(1)}, bf16[96,384]{1,0:T(8,128)(2,1)S(1)}, u32[]{:S(2)}, u32[]{:S(2)}) %collective-permute-start.26) | collective-permute-done | bytes 73760 | tf_op jit(solution)/shard_map/ppermute | solution.py:953
  190.5 4.6 %collective-permute-start.30 = (bf16[96,384]{1,0:T(8,128)(2,1)S(1)}, bf16[96,384]{1,0:T(8,128)(2,1)S(1)}, u32[]{:S(2)}, u32[]{:S(2)}) collective-permute-start(bf16[96,384]{1,0:T(8,128)(2,1)S(1)} %fusion.11.refs_0_), channel_id=1, source_target_pairs={{0,24},{8,16},{16,8},{24,0},{1,25},{9,17},{17,9},{25,1},{2,26},{10... | collective-permute-start | bytes 221192 | tf_op jit(solution)/shard_map/ppermute | solution.py:956
  195.1 0.6 collective-permute-start.28
  195.7 1.8 collective-permute-done.30.refs_3_
  197.5 2.8 %collective-permute-done.29.refs_2_ = bf16[96,384]{1,0:T(8,128)(2,1)S(1)} collective-permute-done((bf16[96,384]{1,0:T(8,128)(2,1)S(1)}, bf16[96,384]{1,0:T(8,128)(2,1)S(1)}, u32[]{:S(2)}, u32[]{:S(2)}) %collective-permute-start.29) | collective-permute-done | bytes 73760 | tf_op jit(solution)/shard_map/ppermute | solution.py:956
  200.3 0.7 square_sums.1
  201.2 1.2 collective-permute-done.37
  202.3 1.3 collective-permute-start.40
  203.7 0.7 collective-permute-start.39
  204.3 1.5 collective-permute-start.38
  205.8 1.1 collective-permute-done.40.refs_3_
  206.9 0.4 collective-permute-done.39.refs_2_
  207.3 0.7 collective-permute-done.38.refs_1_
  208.2 3.8 %update.1 = (f32[1,1]{1,0:T(1,128)}, f32[1,1]{1,0:T(1,128)}, f32[192,384]{1,0:T(8,128)}, f32[48,384]{1,0:T(8,128)}, f32[48,768]{1,0:T(8,128)}, /*index=5*/f32[48...) custom-call(f32[16,128]{1,0:T(8,128)S(1)} %add.127.refs_0_, ...), custom_call_target="tpu_custom_call" | custom-call | tf_op jit(solution)/shard_map/update/pallas_call | solution.py:1067
  (118 shorter events, 2.5 us)
Async XLA Ops:
  2.9 11.6 %collective-permute-start.2 = (bf16[352,384]{1,0:T(8,128)(2,1)}, bf16[352,384]{1,0:T(8,128)(2,1)}, u32[]{:S(2)}, u32[]{:S(2)}) collective-permute-start(bf16[352,384]{1,0:T(8,128)(2,1)} %get-tuple-element.99.refs_2_.refs_0_.refs_9_), channel_id=1, source_target_pairs={{0,6},{1,7},{2,4},{3,5},{4,2},{5,3},{6,0},{7,1},{8,14},{9,15},{10,... | collective-permute-start | bytes 811016 | tf_op jit(solution)/shard_map/ppermute | solution.py:929
  6.7 12.6 %collective-permute-start.1 = (bf16[352,384]{1,0:T(8,128)(2,1)}, bf16[352,384]{1,0:T(8,128)(2,1)}, u32[]{:S(2)}, u32[]{:S(2)}) collective-permute-start(bf16[352,384]{1,0:T(8,128)(2,1)} %get-tuple-element.99.refs_2_.refs_0_.refs_9_), channel_id=1, source_target_pairs={{0,4},{1,5},{2,6},{3,7},{4,0},{5,1},{6,2},{7,3},{8,12},{9,13},{10,... | collective-permute-start | bytes 811016 | tf_op jit(solution)/shard_map/ppermute | solution.py:929
  7.3 12.4 %collective-permute-start = (bf16[352,384]{1,0:T(8,128)(2,1)}, bf16[352,384]{1,0:T(8,128)(2,1)}, u32[]{:S(2)}, u32[]{:S(2)}) collective-permute-start(bf16[352,384]{1,0:T(8,128)(2,1)} %get-tuple-element.99.refs_2_.refs_0_.refs_9_), channel_id=1, source_target_pairs={{0,2},{1,3},{2,0},{3,1},{4,6},{5,7},{6,4},{7,5},{8,10},{9,11},{10,... | collective-permute-start | bytes 811016 | tf_op jit(solution)/shard_map/ppermute | solution.py:929
  19.6 36.4 %all-to-all-start = ((bf16[8,320,512]{2,1,0:T(8,128)(2,1)}), bf16[8,320,512]{2,1,0:T(8,128)(2,1)S(1)}, u32[]{:S(2)}, u32[]{:S(2)}) async-start(bf16[8,320,512]{2,1,0:T(8,128)(2,1)} %pack_tokens.1), calls=%async_computation | async-start | bytes 5242880 | tf_op jit(solution)/shard_map/all_to_all | solution.py:1099
  23.3 1.9 collective-permute-start.3
  23.7 17.5 %collective-permute-start.7 = (bf16[352,384]{1,0:T(8,128)(2,1)}, bf16[352,384]{1,0:T(8,128)(2,1)}, u32[]{:S(2)}, u32[]{:S(2)}) collective-permute-start(bf16[352,384]{1,0:T(8,128)(2,1)} %collective-permute-done.refs_4_.refs_2_.refs_11_), channel_id=1, source_target_pairs={{0,1},{1,0},{2,3},{3,2},{4,5},{5,4},{6,7},{7,6},{8,9},{9,8},{10,11... | collective-permute-start | bytes 811016 | tf_op jit(solution)/shard_map/ppermute | solution.py:933
  23.8 18.9 %collective-permute-start.8 = (bf16[352,384]{1,0:T(8,128)(2,1)}, bf16[352,384]{1,0:T(8,128)(2,1)}, u32[]{:S(2)}, u32[]{:S(2)}) collective-permute-start(bf16[352,384]{1,0:T(8,128)(2,1)} %collective-permute-done.1.refs_6_.refs_4_.refs_13_), channel_id=1, source_target_pairs={{0,1},{1,0},{2,3},{3,2},{4,5},{5,4},{6,7},{7,6},{8,9},{9,8},{10,11... | collective-permute-start | bytes 811016 | tf_op jit(solution)/shard_map/ppermute | solution.py:933
  24.2 18.5 %collective-permute-start.9 = (bf16[352,384]{1,0:T(8,128)(2,1)}, bf16[352,384]{1,0:T(8,128)(2,1)}, u32[]{:S(2)}, u32[]{:S(2)}) collective-permute-start(bf16[352,384]{1,0:T(8,128)(2,1)} %collective-permute-done.2.refs_8_.refs_6_.refs_15_), channel_id=1, source_target_pairs={{0,1},{1,0},{2,3},{3,2},{4,5},{5,4},{6,7},{7,6},{8,9},{9,8},{10,11... | collective-permute-start | bytes 811016 | tf_op jit(solution)/shard_map/ppermute | solution.py:933
  26.4 8.6 %collective-permute-start.6 = (s32[1]{0:T(128)}, s32[1]{0:T(128)}, u32[]{:S(2)}, u32[]{:S(2)}) collective-permute-start(s32[1]{0:T(128)} %bitcast.6), channel_id=1, source_target_pairs={{0,24},{8,16},{16,8},{24,0},{1,25},{9,17},{17,9},{25,1},{2,26},{10... | collective-permute-start | bytes 20 | tf_op jit(solution)/shard_map/ppermute | solution.py:1120
  30.0 3.6 %collective-permute-start.4 = (s32[1]{0:T(128)}, s32[1]{0:T(128)}, u32[]{:S(2)}, u32[]{:S(2)}) collective-permute-start(s32[1]{0:T(128)} %bitcast.6), channel_id=1, source_target_pairs={{0,8},{8,0},{16,24},{24,16},{1,9},{9,1},{17,25},{25,17},{2,10},{10... | collective-permute-start | bytes 20 | tf_op jit(solution)/shard_map/ppermute | solution.py:1120
  33.6 4.5 %collective-permute-start.5 = (s32[1]{0:T(128)}, s32[1]{0:T(128)}, u32[]{:S(2)}, u32[]{:S(2)}) collective-permute-start(s32[1]{0:T(128)} %bitcast.6), channel_id=1, source_target_pairs={{0,16},{8,24},{16,0},{24,8},{1,17},{9,25},{17,1},{25,9},{2,18},{10... | collective-permute-start | bytes 20 | tf_op jit(solution)/shard_map/ppermute | solution.py:1120
  35.0 48.2 %collective-permute-start.12 = (bf16[448,384]{1,0:T(8,128)(2,1)S(1)}, bf16[448,384]{1,0:T(8,128)(2,1)S(1)}, u32[]{:S(2)}, u32[]{:S(2)}) collective-permute-start(bf16[448,384]{1,0:T(8,128)(2,1)S(1)} %copy-done.29), channel_id=1, source_target_pairs={{0,6},{1,7},{2,4},{3,5},{4,2},{5,3},{6,0},{7,1},{8,14},{9,15},{10,... | collective-permute-start | bytes 1032200 | tf_op jit(solution)/shard_map/ppermute | solution.py:929
  38.1 45.1 %collective-permute-start.11 = (bf16[448,384]{1,0:T(8,128)(2,1)S(1)}, bf16[448,384]{1,0:T(8,128)(2,1)}, u32[]{:S(2)}, u32[]{:S(2)}) collective-permute-start(bf16[448,384]{1,0:T(8,128)(2,1)S(1)} %copy-done.29), channel_id=1, source_target_pairs={{0,4},{1,5},{2,6},{3,7},{4,0},{5,1},{6,2},{7,3},{8,12},{9,13},{10,... | collective-permute-start | bytes 1032200 | tf_op jit(solution)/shard_map/ppermute | solution.py:929
  41.2 42.1 %collective-permute-start.10 = (bf16[448,384]{1,0:T(8,128)(2,1)S(1)}, bf16[448,384]{1,0:T(8,128)(2,1)}, u32[]{:S(2)}, u32[]{:S(2)}) collective-permute-start(bf16[448,384]{1,0:T(8,128)(2,1)S(1)} %copy-done.29), channel_id=1, source_target_pairs={{0,2},{1,3},{2,0},{3,1},{4,6},{5,7},{6,4},{7,5},{8,10},{9,11},{10,... | collective-permute-start | bytes 1032200 | tf_op jit(solution)/shard_map/ppermute | solution.py:929
  83.3 1.7 collective-permute-start.13
  83.4 2.3 %collective-permute-start.14 = (bf16[448,384]{1,0:T(8,128)(2,1)}, bf16[448,384]{1,0:T(8,128)(2,1)S(1)}, u32[]{:S(2)}, u32[]{:S(2)}) collective-permute-start(bf16[448,384]{1,0:T(8,128)(2,1)} %collective-permute-done.10.refs_10_), channel_id=1, source_target_pairs={{0,1},{1,0},{2,3},{3,2},{4,5},{5,4},{6,7},{7,6},{8,9},{9,8},{10,11... | collective-permute-start | bytes 1032200 | tf_op jit(solution)/shard_map/ppermute | solution.py:933
  83.9 2.8 %collective-permute-start.15 = (bf16[448,384]{1,0:T(8,128)(2,1)}, bf16[448,384]{1,0:T(8,128)(2,1)S(1)}, u32[]{:S(2)}, u32[]{:S(2)}) collective-permute-start(bf16[448,384]{1,0:T(8,128)(2,1)} %collective-permute-done.11.refs_12_), channel_id=1, source_target_pairs={{0,1},{1,0},{2,3},{3,2},{4,5},{5,4},{6,7},{7,6},{8,9},{9,8},{10,11... | collective-permute-start | bytes 1032200 | tf_op jit(solution)/shard_map/ppermute | solution.py:933
  84.0 2.8 %collective-permute-start.16 = (bf16[448,384]{1,0:T(8,128)(2,1)S(1)}, bf16[448,384]{1,0:T(8,128)(2,1)S(1)}, u32[]{:S(2)}, u32[]{:S(2)}) collective-permute-start(bf16[448,384]{1,0:T(8,128)(2,1)S(1)} %collective-permute-done.12.refs_14_), channel_id=1, source_target_pairs={{0,1},{1,0},{2,3},{3,2},{4,5},{5,4},{6,7},{7,6},{8,9},{9,8},{10,11... | collective-permute-start | bytes 1032200 | tf_op jit(solution)/shard_map/ppermute | solution.py:933
  113.6 7.4 %collective-permute-start.17 = (bf16[4,4,112,384]{3,2,1,0:T(8,128)(2,1)}, bf16[4,4,112,384]{3,2,1,0:T(8,128)(2,1)}, u32[]{:S(2)}, u32[]{:S(2)}) collective-permute-start(bf16[4,4,112,384]{3,2,1,0:T(8,128)(2,1)} %get-tuple-element.122), channel_id=1, source_target_pairs={{0,1},{1,0},{2,3},{3,2},{4,5},{5,4},{6,7},{7,6},{8,9},{9,8},{10,11... | collective-permute-start | bytes 4128776 | tf_op jit(solution)/shard_map/ppermute | solution.py:938
  123.6 31.9 %collective-permute-start.18 = (bf16[4,112,384]{2,1,0:T(8,128)(2,1)}, bf16[4,112,384]{2,1,0:T(8,128)(2,1)S(1)}, u32[]{:S(2)}, u32[]{:S(2)}) collective-permute-start(bf16[4,112,384]{2,1,0:T(8,128)(2,1)} %get-tuple-element.133), channel_id=1, source_target_pairs={{0,2},{1,3},{2,0},{3,1},{4,6},{5,7},{6,4},{7,5},{8,10},{9,11},{10,... | collective-permute-start | bytes 1032200 | tf_op jit(solution)/shard_map/ppermute | solution.py:946
  124.0 31.5 %collective-permute-start.19 = (bf16[4,112,384]{2,1,0:T(8,128)(2,1)}, bf16[4,112,384]{2,1,0:T(8,128)(2,1)S(1)}, u32[]{:S(2)}, u32[]{:S(2)}) collective-permute-start(bf16[4,112,384]{2,1,0:T(8,128)(2,1)} %get-tuple-element.134), channel_id=1, source_target_pairs={{0,4},{1,5},{2,6},{3,7},{4,0},{5,1},{6,2},{7,3},{8,12},{9,13},{10,... | collective-permute-start | bytes 1032200 | tf_op jit(solution)/shard_map/ppermute | solution.py:946
  124.6 30.9 %collective-permute-start.20 = (bf16[4,112,384]{2,1,0:T(8,128)(2,1)S(1)}, bf16[4,112,384]{2,1,0:T(8,128)(2,1)S(1)}, u32[]{:S(2)}, u32[]{:S(2)}) collective-permute-start(bf16[4,112,384]{2,1,0:T(8,128)(2,1)S(1)} %get-tuple-element.135), channel_id=1, source_target_pairs={{0,6},{1,7},{2,4},{3,5},{4,2},{5,3},{6,0},{7,1},{8,14},{9,15},{10,... | collective-permute-start | bytes 1032200 | tf_op jit(solution)/shard_map/ppermute | solution.py:946
  155.7 3.1 %collective-permute-start.21 = (bf16[4,4,96,384]{3,2,1,0:T(8,128)(2,1)}, bf16[4,4,96,384]{3,2,1,0:T(8,128)(2,1)S(1)}, u32[]{:S(2)}, u32[]{:S(2)}) collective-permute-start(bf16[4,4,96,384]{3,2,1,0:T(8,128)(2,1)} %get-tuple-element.136), channel_id=1, source_target_pairs={{0,1},{1,0},{2,3},{3,2},{4,5},{5,4},{6,7},{7,6},{8,9},{9,8},{10,11... | collective-permute-start | bytes 3538952 | tf_op jit(solution)/shard_map/ppermute | solution.py:938
  159.0 9.9 %collective-permute-start.22 = (bf16[4,96,384]{2,1,0:T(8,128)(2,1)S(1)}, bf16[4,96,384]{2,1,0:T(8,128)(2,1)S(1)}, u32[]{:S(2)}, u32[]{:S(2)}) collective-permute-start(bf16[4,96,384]{2,1,0:T(8,128)(2,1)S(1)} %get-tuple-element.173), channel_id=1, source_target_pairs={{0,2},{1,3},{2,0},{3,1},{4,6},{5,7},{6,4},{7,5},{8,10},{9,11},{10,... | collective-permute-start | bytes 884744 | tf_op jit(solution)/shard_map/ppermute | solution.py:946
  159.5 15.0 %collective-permute-start.24 = (bf16[4,96,384]{2,1,0:T(8,128)(2,1)S(1)}, bf16[4,96,384]{2,1,0:T(8,128)(2,1)S(1)}, u32[]{:S(2)}, u32[]{:S(2)}) collective-permute-start(bf16[4,96,384]{2,1,0:T(8,128)(2,1)S(1)} %get-tuple-element.174), channel_id=1, source_target_pairs={{0,6},{1,7},{2,4},{3,5},{4,2},{5,3},{6,0},{7,1},{8,14},{9,15},{10,... | collective-permute-start | bytes 884744 | tf_op jit(solution)/shard_map/ppermute | solution.py:946
  161.1 14.8 %collective-permute-start.23 = (bf16[4,96,384]{2,1,0:T(8,128)(2,1)S(1)}, bf16[4,96,384]{2,1,0:T(8,128)(2,1)S(1)}, u32[]{:S(2)}, u32[]{:S(2)}) collective-permute-start(bf16[4,96,384]{2,1,0:T(8,128)(2,1)S(1)} %get-tuple-element.175), channel_id=1, source_target_pairs={{0,4},{1,5},{2,6},{3,7},{4,0},{5,1},{6,2},{7,3},{8,12},{9,13},{10,... | collective-permute-start | bytes 884744 | tf_op jit(solution)/shard_map/ppermute | solution.py:946
  162.6 17.6 %collective-permute-start.31 = (bf16[112,384]{1,0:T(8,128)(2,1)S(1)}, bf16[112,384]{1,0:T(8,128)(2,1)S(1)}, u32[]{:S(2)}, u32[]{:S(2)}) collective-permute-start(bf16[112,384]{1,0:T(8,128)(2,1)S(1)} %get-tuple-element.176), channel_id=1, source_target_pairs={{0,8},{8,0},{16,24},{24,16},{1,9},{9,1},{17,25},{25,17},{2,10},{10... | collective-permute-start | bytes 258056 | tf_op jit(solution)/shard_map/ppermute | solution.py:953
  164.3 16.1 %collective-permute-start.33 = (bf16[112,384]{1,0:T(8,128)(2,1)S(1)}, bf16[112,384]{1,0:T(8,128)(2,1)S(1)}, u32[]{:S(2)}, u32[]{:S(2)}) collective-permute-start(bf16[112,384]{1,0:T(8,128)(2,1)S(1)} %get-tuple-element.177), channel_id=1, source_target_pairs={{0,24},{8,16},{16,8},{24,0},{1,25},{9,17},{17,9},{25,1},{2,26},{10... | collective-permute-start | bytes 258056 | tf_op jit(solution)/shard_map/ppermute | solution.py:953
  168.9 39.0 %copy-start.1 = (f32[192,384]{1,0:T(8,128)S(1)}, f32[192,384]{1,0:T(8,128)}, u32[]{:S(2)}) copy-start(f32[192,384]{1,0:T(8,128)} %refs_6_.1) | copy-start | bytes 884740
  168.9 39.0 %copy-start.2 = (f32[48,1536]{1,0:T(8,128)S(1)}, f32[48,1536]{1,0:T(8,128)}, u32[]{:S(2)}) copy-start(f32[48,1536]{1,0:T(8,128)} %refs_10_.1) | copy-start | bytes 884740
  168.9 39.0 %copy-start.3 = (f32[192,384]{1,0:T(8,128)S(1)}, f32[192,384]{1,0:T(8,128)}, u32[]{:S(2)}) copy-start(f32[192,384]{1,0:T(8,128)} %refs_11_.1) | copy-start | bytes 884740
  168.9 39.0 %copy-start.4 = (f32[48,768]{1,0:T(8,128)S(1)}, f32[48,768]{1,0:T(8,128)}, u32[]{:S(2)}) copy-start(f32[48,768]{1,0:T(8,128)} %refs_8_.1) | copy-start | bytes 442372
  168.9 39.1 %copy-start.5 = (f32[192,384]{1,0:T(8,128)S(1)}, f32[192,384]{1,0:T(8,128)}, u32[]{:S(2)}) copy-start(f32[192,384]{1,0:T(8,128)} %refs_14_.1) | copy-start | bytes 884740
  168.9 39.1 %copy-start.6 = (f32[48,1536]{1,0:T(8,128)S(1)}, f32[48,1536]{1,0:T(8,128)}, u32[]{:S(2)}) copy-start(f32[48,1536]{1,0:T(8,128)} %refs_18_.1) | copy-start | bytes 884740
  169.0 39.0 %copy-start.7 = (f32[192,384]{1,0:T(8,128)S(1)}, f32[192,384]{1,0:T(8,128)}, u32[]{:S(2)}) copy-start(f32[192,384]{1,0:T(8,128)} %refs_19_.1) | copy-start | bytes 884740
  169.0 39.0 %copy-start.8 = (f32[192,384]{1,0:T(8,128)S(1)}, f32[192,384]{1,0:T(8,128)}, u32[]{:S(2)}) copy-start(f32[192,384]{1,0:T(8,128)} %refs_22_.1) | copy-start | bytes 884740
  169.0 39.0 %copy-start.9 = (f32[48,1536]{1,0:T(8,128)S(1)}, f32[48,1536]{1,0:T(8,128)}, u32[]{:S(2)}) copy-start(f32[48,1536]{1,0:T(8,128)} %refs_26_.1) | copy-start | bytes 884740
  169.0 39.0 %copy-start.10 = (f32[192,384]{1,0:T(8,128)S(1)}, f32[192,384]{1,0:T(8,128)}, u32[]{:S(2)}) copy-start(f32[192,384]{1,0:T(8,128)} %refs_27_.1) | copy-start | bytes 884740
  169.0 39.0 %copy-start.11 = (f32[48,384]{1,0:T(8,128)S(1)}, f32[48,384]{1,0:T(8,128)}, u32[]{:S(2)}) copy-start(f32[48,384]{1,0:T(8,128)} %refs_7_.1) | copy-start | bytes 221188
  169.0 39.0 %copy-start.12 = (f32[48,384]{1,0:T(8,128)S(1)}, f32[48,384]{1,0:T(8,128)}, u32[]{:S(2)}) copy-start(f32[48,384]{1,0:T(8,128)} %refs_9_.1) | copy-start | bytes 221188
  169.0 39.0 %copy-start.13 = (f32[48,768]{1,0:T(8,128)S(1)}, f32[48,768]{1,0:T(8,128)}, u32[]{:S(2)}) copy-start(f32[48,768]{1,0:T(8,128)} %refs_16_.1) | copy-start | bytes 442372
  169.0 39.0 %copy-start.14 = (f32[48,768]{1,0:T(8,128)S(1)}, f32[48,768]{1,0:T(8,128)}, u32[]{:S(2)}) copy-start(f32[48,768]{1,0:T(8,128)} %refs_24_.1) | copy-start | bytes 442372
  169.0 39.0 %copy-start.15 = (f32[48,128]{1,0:T(8,128)S(1)}, f32[48,128]{1,0:T(8,128)}, u32[]{:S(2)}) copy-start(f32[48,128]{1,0:T(8,128)} %refs_12_.1) | copy-start | bytes 73732
  169.1 39.0 %copy-start.16 = (f32[48,384]{1,0:T(8,128)S(1)}, f32[48,384]{1,0:T(8,128)}, u32[]{:S(2)}) copy-start(f32[48,384]{1,0:T(8,128)} %refs_15_.1) | copy-start | bytes 221188
  169.1 39.0 %copy-start.17 = (f32[48,384]{1,0:T(8,128)S(1)}, f32[48,384]{1,0:T(8,128)}, u32[]{:S(2)}) copy-start(f32[48,384]{1,0:T(8,128)} %refs_17_.1) | copy-start | bytes 221188
  169.1 39.0 %copy-start.18 = (f32[48,384]{1,0:T(8,128)S(1)}, f32[48,384]{1,0:T(8,128)}, u32[]{:S(2)}) copy-start(f32[48,384]{1,0:T(8,128)} %refs_23_.1) | copy-start | bytes 221188
  169.1 39.0 %copy-start.19 = (f32[48,384]{1,0:T(8,128)S(1)}, f32[48,384]{1,0:T(8,128)}, u32[]{:S(2)}) copy-start(f32[48,384]{1,0:T(8,128)} %refs_25_.1) | copy-start | bytes 221188
  169.1 39.0 %copy-start.20 = (f32[48,128]{1,0:T(8,128)S(1)}, f32[48,128]{1,0:T(8,128)}, u32[]{:S(2)}) copy-start(f32[48,128]{1,0:T(8,128)} %refs_20_.1) | copy-start | bytes 73732
  169.1 39.0 %copy-start.21 = (f32[48,128]{1,0:T(8,128)S(1)}, f32[48,128]{1,0:T(8,128)}, u32[]{:S(2)}) copy-start(f32[48,128]{1,0:T(8,128)} %refs_28_.1) | copy-start | bytes 73732
  169.1 39.0 %copy-start.22 = (f32[5,48]{1,0:T(8,128)S(1)}, f32[5,48]{1,0:T(8,128)}, u32[]{:S(2)}) copy-start(f32[5,48]{1,0:T(8,128)} %refs_13_.1) | copy-start | bytes 2884
  169.2 11.2 %collective-permute-start.32 = (bf16[112,384]{1,0:T(8,128)(2,1)S(1)}, bf16[112,384]{1,0:T(8,128)(2,1)S(1)}, u32[]{:S(2)}, u32[]{:S(2)}) collective-permute-start(bf16[112,384]{1,0:T(8,128)(2,1)S(1)} %get-tuple-element.178), channel_id=1, source_target_pairs={{0,16},{8,24},{16,0},{24,8},{1,17},{9,25},{17,1},{25,9},{2,18},{10... | collective-permute-start | bytes 258056 | tf_op jit(solution)/shard_map/ppermute | solution.py:953
  176.1 7.6 %collective-permute-start.25 = (bf16[96,384]{1,0:T(8,128)(2,1)S(1)}, bf16[96,384]{1,0:T(8,128)(2,1)S(1)}, u32[]{:S(2)}, u32[]{:S(2)}) collective-permute-start(bf16[96,384]{1,0:T(8,128)(2,1)S(1)} %get-tuple-element.179), channel_id=1, source_target_pairs={{0,8},{8,0},{16,24},{24,16},{1,9},{9,1},{17,25},{25,17},{2,10},{10... | collective-permute-start | bytes 221192 | tf_op jit(solution)/shard_map/ppermute | solution.py:953
  177.7 7.1 %collective-permute-start.27 = (bf16[96,384]{1,0:T(8,128)(2,1)S(1)}, bf16[96,384]{1,0:T(8,128)(2,1)S(1)}, u32[]{:S(2)}, u32[]{:S(2)}) collective-permute-start(bf16[96,384]{1,0:T(8,128)(2,1)S(1)} %get-tuple-element.180), channel_id=1, source_target_pairs={{0,24},{8,16},{16,8},{24,0},{1,25},{9,17},{17,9},{25,1},{2,26},{10... | collective-permute-start | bytes 221192 | tf_op jit(solution)/shard_map/ppermute | solution.py:953
  180.2 10.3 %collective-permute-start.26 = (bf16[96,384]{1,0:T(8,128)(2,1)S(1)}, bf16[96,384]{1,0:T(8,128)(2,1)S(1)}, u32[]{:S(2)}, u32[]{:S(2)}) collective-permute-start(bf16[96,384]{1,0:T(8,128)(2,1)S(1)} %get-tuple-element.181), channel_id=1, source_target_pairs={{0,16},{8,24},{16,0},{24,8},{1,17},{9,25},{17,1},{25,9},{2,18},{10... | collective-permute-start | bytes 221192 | tf_op jit(solution)/shard_map/ppermute | solution.py:953
  180.4 14.7 %collective-permute-start.36 = (bf16[112,384]{1,0:T(8,128)(2,1)S(1)}, bf16[112,384]{1,0:T(8,128)(2,1)S(1)}, u32[]{:S(2)}, u32[]{:S(2)}) collective-permute-start(bf16[112,384]{1,0:T(8,128)(2,1)S(1)} %fusion.8.refs_4_), channel_id=1, source_target_pairs={{0,24},{8,16},{16,8},{24,0},{1,25},{9,17},{17,9},{25,1},{2,26},{10... | collective-permute-start | bytes 258056 | tf_op jit(solution)/shard_map/ppermute | solution.py:956
  183.4 12.4 %collective-permute-start.35 = (bf16[112,384]{1,0:T(8,128)(2,1)S(1)}, bf16[112,384]{1,0:T(8,128)(2,1)S(1)}, u32[]{:S(2)}, u32[]{:S(2)}) collective-permute-start(bf16[112,384]{1,0:T(8,128)(2,1)S(1)} %fusion.8.refs_4_), channel_id=1, source_target_pairs={{0,16},{8,24},{16,0},{24,8},{1,17},{9,25},{17,1},{25,9},{2,18},{10... | collective-permute-start | bytes 258056 | tf_op jit(solution)/shard_map/ppermute | solution.py:956
  183.7 12.0 %collective-permute-start.34 = (bf16[112,384]{1,0:T(8,128)(2,1)S(1)}, bf16[112,384]{1,0:T(8,128)(2,1)S(1)}, u32[]{:S(2)}, u32[]{:S(2)}) collective-permute-start(bf16[112,384]{1,0:T(8,128)(2,1)S(1)} %fusion.8.refs_4_), channel_id=1, source_target_pairs={{0,8},{8,0},{16,24},{24,16},{1,9},{9,1},{17,25},{25,17},{2,10},{10... | collective-permute-start | bytes 258056 | tf_op jit(solution)/shard_map/ppermute | solution.py:956
  190.5 7.0 %collective-permute-start.30 = (bf16[96,384]{1,0:T(8,128)(2,1)S(1)}, bf16[96,384]{1,0:T(8,128)(2,1)S(1)}, u32[]{:S(2)}, u32[]{:S(2)}) collective-permute-start(bf16[96,384]{1,0:T(8,128)(2,1)S(1)} %fusion.11.refs_0_), channel_id=1, source_target_pairs={{0,24},{8,16},{16,8},{24,0},{1,25},{9,17},{17,9},{25,1},{2,26},{10... | collective-permute-start | bytes 221192 | tf_op jit(solution)/shard_map/ppermute | solution.py:956
  195.1 5.3 %collective-permute-start.29 = (bf16[96,384]{1,0:T(8,128)(2,1)S(1)}, bf16[96,384]{1,0:T(8,128)(2,1)S(1)}, u32[]{:S(2)}, u32[]{:S(2)}) collective-permute-start(bf16[96,384]{1,0:T(8,128)(2,1)S(1)} %fusion.11.refs_0_), channel_id=1, source_target_pairs={{0,16},{8,24},{16,0},{24,8},{1,17},{9,25},{17,1},{25,9},{2,18},{10... | collective-permute-start | bytes 221192 | tf_op jit(solution)/shard_map/ppermute | solution.py:956
  195.1 5.2 %collective-permute-start.28 = (bf16[96,384]{1,0:T(8,128)(2,1)S(1)}, bf16[96,384]{1,0:T(8,128)(2,1)S(1)}, u32[]{:S(2)}, u32[]{:S(2)}) collective-permute-start(bf16[96,384]{1,0:T(8,128)(2,1)S(1)} %fusion.11.refs_0_), channel_id=1, source_target_pairs={{0,8},{8,0},{16,24},{24,16},{1,9},{9,1},{17,25},{25,17},{2,10},{10... | collective-permute-start | bytes 221192 | tf_op jit(solution)/shard_map/ppermute | solution.py:956
  201.1 1.2 collective-permute-start.37
  202.3 4.5 %collective-permute-start.40 = (f32[16,128]{1,0:T(8,128)S(1)}, f32[16,128]{1,0:T(8,128)S(1)}, u32[]{:S(2)}, u32[]{:S(2)}) collective-permute-start(f32[16,128]{1,0:T(8,128)S(1)} %add.127.refs_0_), channel_id=1, source_target_pairs={{0,6},{1,7},{2,4},{3,5},{4,2},{5,3},{6,0},{7,1},{8,14},{9,15},{10,... | collective-permute-start | bytes 24584 | tf_op jit(solution)/shard_map/ppermute | solution.py:1156
  203.7 3.7 %collective-permute-start.39 = (f32[16,128]{1,0:T(8,128)S(1)}, f32[16,128]{1,0:T(8,128)S(1)}, u32[]{:S(2)}, u32[]{:S(2)}) collective-permute-start(f32[16,128]{1,0:T(8,128)S(1)} %add.127.refs_0_), channel_id=1, source_target_pairs={{0,4},{1,5},{2,6},{3,7},{4,0},{5,1},{6,2},{7,3},{8,12},{9,13},{10,... | collective-permute-start | bytes 24584 | tf_op jit(solution)/shard_map/ppermute | solution.py:1156
  204.3 3.7 %collective-permute-start.38 = (f32[16,128]{1,0:T(8,128)S(1)}, f32[16,128]{1,0:T(8,128)S(1)}, u32[]{:S(2)}, u32[]{:S(2)}) collective-permute-start(f32[16,128]{1,0:T(8,128)S(1)} %add.127.refs_0_), channel_id=1, source_target_pairs={{0,2},{1,3},{2,0},{3,1},{4,6},{5,7},{6,4},{7,5},{8,10},{9,11},{10,... | collective-permute-start | bytes 24584 | tf_op jit(solution)/shard_map/ppermute | solution.py:1156
  (16 other events, 222.2 us)
where the time goes:
time: 214 us; the launch traced here: 213 us
  Pallas kernels  97 us (45%)
  waiting for transfers between devices  51.3 us (24%)
  starting transfers between devices  51.2 us (24%)
  between operations  5.17 us (2%)
  local copies, waits for them, and re-layouts  4.59 us (2%)
  other arithmetic  3.8 us (2%)
    pallas_call x1, Pallas kernels, back(): pl.pallas_call(kernel, grid=(steps,), out_shape=[jax.ShapeDtypeStruct(s,...  28.4 us
    pallas_call x1, Pallas kernels, middle(): pl.pallas_call(kernel, grid=(1,), out_shape=[jax.ShapeDtypeStruct(s, d) f...  26.1 us
    pallas_call x1, Pallas kernels, front(): pl.pallas_call(kernel, grid=(H,), out_shape=[jax.ShapeDtypeStruct(s, d) f...  25.7 us
    all_to_all x1, waiting for transfers between devices, on_device(): lax.all_to_all(packed, 'tm', 0, 0, axis_index_groups=groups, tiled=True)  13.3 us
    ppermute x6, starting transfers between devices, over_planes(): there = lax.ppermute(mine[m].astype(bfloat), 'seg', pairs(z.planes, m))  11 us
    ppermute x6, starting transfers between devices, from_chips(): lax.ppermute(own, 'tm', pairs(z.n, 2 * m))  10.4 us
    ppermute x6, starting transfers between devices, over_planes(): lax.ppermute(low, 'seg', pairs(z.planes, m))  9.66 us
    ppermute x6, waiting for transfers between devices, from_chips(): lax.ppermute(own, 'tm', pairs(z.n, 2 * m))  9.48 us
  transfers between devices with their start and end apart: 42, of which 21 were waited for; matrix products, arithmetic and copies ran while one was open for 1% of the time, Pallas kernels for 30%

commit v1 on v0

--- a/solution.py
+++ b/solution.py
@@ -113,7 +113,7 @@
         self.second_grads = -(-self.second_rows // step) * step
         self.direct = self.parts == 1 and self.w % 16 == 0 and self.hw % 16 == 0 and self.hw > 0
         self.block = 256
-        self.middle_block = 256
+        self.middle_block = 512
         self.query_block = 1024 if self.keys <= 1024 else 256
 
 
@@ -612,7 +612,13 @@
         spare_grad = tn(att_s[...], bg_s[...])
         for h in range(H):
             go_s[h * hd : (h + 1) * hd, :] = spare_grad[h * LANES : h * LANES + hd, :]
-        gu_s[...] = tn(fin_s[...], hg_s[...])
+
+        def up_columns(c, carry):
+            here = pl.ds(pl.multiple_of(c * D, LANES), D)
+            gu_s[:, here] = tn(fin_s[...], hg_s[:, here])
+            return carry
+
+        lax.fori_loop(0, F // D, up_columns, 0)
         gd_s[...] = tn(act_s[...], fg_s[...])
         gh_s[...] = tn(low_s[...], pg_s[...])
         if z.direct:
@@ -813,27 +819,18 @@
 
             for c in range(K // T):
                 cg_s[...] = nt(dkvt_s[c * T : (c + 1) * T, :], wkv[...])
-
-                def key_block(i, carry):
-                    rows = pl.ds(pl.multiple_of(i * B, B), B)
-                    source = pl.ds(pl.multiple_of(c * T + i * B, B), B)
-                    unit, _ = norm_parts(sp_ref[source, :].astype(float32))
+                for i in range(T // B):
+                    rows = slice(i * B, (i + 1) * B)
+                    unit, _ = norm_parts(sp_ref[c * T + i * B : c * T + (i + 1) * B, :].astype(float32))
                     misc_s[1:2, :] += jnp.sum(cg_s[rows, :] * unit, 0, keepdims=True)
-                    return carry
-
-                lax.fori_loop(0, T // B, key_block, 0)
             dn_s[...] = nt(dqc_s[...], wq[...])
-
-            def token_block(i, carry):
-                rows = pl.ds(pl.multiple_of(i * B, B), B)
+            for i in range(T // B):
+                rows = slice(i * B, (i + 1) * B)
                 unit, scale = norm_parts(stream_ref[rows, :])
                 part, gain_grad = norm_back(unit, scale, gain_query, dn_s[rows, :])
                 misc_s[0:1, :] += gain_grad
                 conv_grad = (mid_ref[rows, :] + part) * slope_ref[rows, :]
                 cg_s[rows, :] = conv_grad.astype(bfloat).astype(float32)
-                return carry
-
-            lax.fori_loop(0, T // B, token_block, 0)
             conv_grad = cg_s[...]
             gc_s[half : half + frame, :] = tn(x_ref[...], conv_grad.astype(bfloat))
             row = iota((T, D), 0)
@@ -1045,15 +1042,15 @@
 
         def block(index, ref, start, lane):
             def body(i, carry):
-                here = pl.ds(pl.multiple_of(i * 16, 16), 16)
-                step(index, (here, slice(lane, lane + D)), ref[pl.ds(pl.multiple_of(start + i * 16, 16), 16), :])
+                here = pl.ds(pl.multiple_of(i * w, 16), w)
+                step(index, (here, slice(lane, lane + D)), ref[pl.ds(pl.multiple_of(start + i * w, 16), w), :])
                 return carry
 
             return body
 
         for index, pieces in places.items():
             for ref, start, count, lane in pieces:
-                lax.fori_loop(0, count // 16, block(index, ref, start, lane), 0)
+                lax.fori_loop(0, count // w, block(index, ref, start, lane), 0)
         start = w + z.uw + z.fw
         for g in range(D // O):
             here = (slice(g * z.hw, (g + 1) * z.hw), slice(0, O))

time: 214 us -> 210 us (0.981)
  Pallas kernels: 97 us -> 93.1 us
    pallas_call x1, Pallas kernels: 28.4 us -> 26.2 us  [back(): pl.pallas_call(kernel, grid=(steps,), out_shape=[jax.ShapeDtypeStruct(s,...]
where the time goes in v1:
time: 210 us; the launch traced here: 209 us
  Pallas kernels  93.1 us (44%)
  starting transfers between devices  51.3 us (24%)
  waiting for transfers between devices  51.3 us (24%)
  between operations  5.15 us (2%)
  local copies, waits for them, and re-layouts  4.59 us (2%)
  other arithmetic  3.8 us (2%)
    pallas_call x1, Pallas kernels, back(): pl.pallas_call(kernel, grid=(steps,), out_shape=[jax.ShapeDtypeStruct(s,...  26.2 us
    pallas_call x1, Pallas kernels, front(): pl.pallas_call(kernel, grid=(H,), out_shape=[jax.ShapeDtypeStruct(s, d) f...  25.7 us
    pallas_call x1, Pallas kernels, middle(): pl.pallas_call(kernel, grid=(1,), out_shape=[jax.ShapeDtypeStruct(s, d) f...  25.1 us
    all_to_all x1, waiting for transfers between devices, on_device(): lax.all_to_all(packed, 'tm', 0, 0, axis_index_groups=groups, tiled=True)  13.3 us
    ppermute x6, starting transfers between devices, over_planes(): there = lax.ppermute(mine[m].astype(bfloat), 'seg', pairs(z.planes, m))  11 us
    ppermute x6, starting transfers between devices, from_chips(): lax.ppermute(own, 'tm', pairs(z.n, 2 * m))  10.4 us
    ppermute x6, starting transfers between devices, over_planes(): lax.ppermute(low, 'seg', pairs(z.planes, m))  9.66 us
    ppermute x6, waiting for transfers between devices, from_chips(): lax.ppermute(own, 'tm', pairs(z.n, 2 * m))  9.48 us
  transfers between devices with their start and end apart: 42, of which 21 were waited for; matrix products, arithmetic and copies ran while one was open for 1% of the time, Pallas kernels for 30%

profile of v1, /device:TPU:0, one launch (start us, length us, event | category | flops | bytes accessed | tf_op | source)
XLA Modules:
  0.0 209.3 jit_solution(12404096919544951819)
XLA Ops:
  0.7 2.2 %pack_weights.1 = (bf16[352,384]{1,0:T(8,128)(2,1)}, bf16[448,384]{1,0:T(8,128)(2,1)}) custom-call(s32[1]{0:T(128)} %bitcast.1.place_ref, f32[192,384]{1,0:T(8,128)} %refs_6_.1, f32[48,384]{1,0:T(8,128)} %refs_7_.1, f32[48,768]{1,0:T(8,128)} %refs_8_.1, f32[48,384]{1,0:T(8,128)} %refs_9_.1, f32[48,1536]{1,0:T(8,128)} %refs_10_.1, f32[192,384]{1,0:T(8,128)} %refs_11_.1, ...), custom_call_target="tpu_custom_call" | custom-call | tf_op jit(solution)/shard_map/pack_weights/pallas_call | solution.py:156
  2.9 3.9 %collective-permute-start.2 = (bf16[352,384]{1,0:T(8,128)(2,1)}, bf16[352,384]{1,0:T(8,128)(2,1)}, u32[]{:S(2)}, u32[]{:S(2)}) collective-permute-start(bf16[352,384]{1,0:T(8,128)(2,1)} %get-tuple-element.99.refs_2_.refs_0_.refs_9_), channel_id=1, source_target_pairs={{0,6},{1,7},{2,4},{3,5},{4,2},{5,3},{6,0},{7,1},{8,14},{9,15},{10,... | collective-permute-start | bytes 811016 | tf_op jit(solution)/shard_map/ppermute | solution.py:926
  6.7 0.5 collective-permute-start.1
  7.3 2.8 %pack_tokens.1 = bf16[8,320,512]{2,1,0:T(8,128)(2,1)} custom-call(bf16[8,192,512]{2,1,0:T(8,128)(2,1)} %bitcast.55, bf16[8,128,384]{2,1,0:T(8,128)(2,1)} %s_ref.1, bf16[8,128,128]{2,1,0:T(8,128)(2,1)} %t_ref.1), custom_call_target="tpu_custom_call" | custom-call | tf_op jit(solution)/shard_map/pack_tokens/pallas_call | solution.py:192
  10.2 4.3 %collective-permute-done.2.refs_8_.refs_6_.refs_15_ = bf16[352,384]{1,0:T(8,128)(2,1)} collective-permute-done((bf16[352,384]{1,0:T(8,128)(2,1)}, bf16[352,384]{1,0:T(8,128)(2,1)}, u32[]{:S(2)}, u32[]{:S(2)}) %collective-permute-start.2) | collective-permute-done | bytes 270368 | tf_op jit(solution)/shard_map/ppermute | solution.py:926
  14.4 4.9 %collective-permute-done.1.refs_6_.refs_4_.refs_13_ = bf16[352,384]{1,0:T(8,128)(2,1)} collective-permute-done((bf16[352,384]{1,0:T(8,128)(2,1)}, bf16[352,384]{1,0:T(8,128)(2,1)}, u32[]{:S(2)}, u32[]{:S(2)}) %collective-permute-start.1) | collective-permute-done | bytes 270368 | tf_op jit(solution)/shard_map/ppermute | solution.py:926
  19.6 3.6 %all-to-all-start = ((bf16[8,320,512]{2,1,0:T(8,128)(2,1)}), bf16[8,320,512]{2,1,0:T(8,128)(2,1)S(1)}, u32[]{:S(2)}, u32[]{:S(2)}) async-start(bf16[8,320,512]{2,1,0:T(8,128)(2,1)} %pack_tokens.1), calls=%async_computation | async-start | bytes 5242880 | tf_op jit(solution)/shard_map/all_to_all | solution.py:1096
  23.3 0.4 collective-permute-start.3
  23.8 0.3 collective-permute-start.8
  24.5 0.6 collective-permute-done.3.refs_3_.refs_1_.refs_10_
  25.2 0.6 reduce_sum.9
  25.8 0.6 dynamic_slice.8
  26.4 3.6 %collective-permute-start.6 = (s32[1]{0:T(128)}, s32[1]{0:T(128)}, u32[]{:S(2)}, u32[]{:S(2)}) collective-permute-start(s32[1]{0:T(128)} %bitcast.6), channel_id=1, source_target_pairs={{0,24},{8,16},{16,8},{24,0},{1,25},{9,17},{17,9},{25,1},{2,26},{10... | collective-permute-start | bytes 20 | tf_op jit(solution)/shard_map/ppermute | solution.py:1117
  30.0 1.2 concatenate.3.meta_ref
  31.2 2.4 %collective-permute-done.4 = s32[1]{0:T(128)} collective-permute-done((s32[1]{0:T(128)}, s32[1]{0:T(128)}, u32[]{:S(2)}, u32[]{:S(2)}) %collective-permute-start.4) | collective-permute-done | bytes 36 | tf_op jit(solution)/shard_map/ppermute | solution.py:1117
  35.0 2.7 %collective-permute-start.12 = (bf16[448,384]{1,0:T(8,128)(2,1)S(1)}, bf16[448,384]{1,0:T(8,128)(2,1)S(1)}, u32[]{:S(2)}, u32[]{:S(2)}) collective-permute-start(bf16[448,384]{1,0:T(8,128)(2,1)S(1)} %copy-done.29), channel_id=1, source_target_pairs={{0,6},{1,7},{2,4},{3,5},{4,2},{5,3},{6,0},{7,1},{8,14},{9,15},{10,... | collective-permute-start | bytes 1032200 | tf_op jit(solution)/shard_map/ppermute | solution.py:926
  37.7 0.4 collective-permute-done.5
  38.1 1.7 collective-permute-start.11
  41.2 1.5 collective-permute-start.10
  42.7 13.3 %all-to-all-done.refs_0_.refs_1_.target_ref.refs_3_ = bf16[8,320,512]{2,1,0:T(8,128)(2,1)S(1)} async-done(((bf16[8,320,512]{2,1,0:T(8,128)(2,1)}), bf16[8,320,512]{2,1,0:T(8,128)(2,1)S(1)}, u32[]{:S(2)}, u32[]{:S(2)}) %all-to-all-start) | async-done | bytes 2621472 | tf_op jit(solution)/shard_map/all_to_all | solution.py:1096
  56.0 1.5 copy-done.27
  57.6 25.7 %front.1 = (bf16[1024,768]{1,0:T(8,128)(2,1)}, f32[1024,384]{1,0:T(8,128)}, f32[1024,384]{1,0:T(8,128)}, bf16[1024,384]{1,0:T(8,128)(2,1)}, bf16[1024,384]{1,0:T...) custom-call(s32[9]{0:T(128)} %concatenate.3.meta_ref, ...), custom_call_target="tpu_custom_call" | custom-call | flops 20000000000 | bytes 20000000 | tf_op jit(solution)/shard_map/front/pallas_call | solution.py:433
  83.4 0.5 collective-permute-start.14
  84.0 0.4 collective-permute-start.16
  84.4 0.6 collective-permute-done.13.refs_9_
  85.0 0.7 collective-permute-done.14.refs_11_
  85.7 1.0 collective-permute-done.15.refs_13_
  86.7 0.7 copy-done.33
  87.5 25.1 %middle.1 = (bf16[1024,1024]{1,0:T(8,128)(2,1)}, f32[1024,384]{1,0:T(8,128)}, f32[8,384]{1,0:T(8,128)}, f32[4,4,112,384]{3,2,1,0:T(8,128)}, bf16[4,4,112,384]{3,2,1,0:T(8,128)(2,1)}) custom-call(s32[9]{0:T(128)} %concatenate.3.meta_ref, f32[1]{0:T(128)} %convert_element_type.137.count_ref, f32[1024,384]{1,0:T(8,128)} %get-tuple-element.110.stream_ref.refs_4_, ...), custom_call_target="tpu_custom_call" | custom-call | flops 20000000000 | bytes 20000000 | tf_op jit(solution)/shard_map/middle/pallas_call | solution.py:675
  112.9 7.3 %attend_back.1 = (bf16[1024,256]{1,0:T(8,128)(2,1)}, bf16[2,96,1024]{2,1,0:T(8,128)(2,1)}) custom-call(bf16[1024,1024]{1,0:T(8,128)(2,1)} %get-tuple-element.106.q_ref, bf16[1024,1024]{1,0:T(8,128)(2,1)} %get-tuple-element.107.k_ref, bf16[1024,1024]{1,0:T(8,128)(2,1)} %get-tuple-element.108.v_ref, bf16[1024,1024]{1,0:T(8,128)(2,1)} %get-tuple-element.118.do_ref), custom_call_target="tpu_custom_call" | custom-call | flops 8000000000 | bytes 12000000 | tf_op jit(solution)/shard_map/attend_back/pallas_call | solution.py:723
  120.2 2.5 %fusion.3 = (bf16[4,112,384]{2,1,0:T(8,128)(2,1)S(1)}, bf16[4,112,384]{2,1,0:T(8,128)(2,1)}, bf16[4,112,384]{2,1,0:T(8,128)(2,1)}, f32[4,112,384]{2,1,0:T(8,128)S(1)}) fusion(f32[4,4,112,384]{3,2,1,0:T(8,128)S(1)} %copy-done.26, bf16[4,4,112,384]{3,2,1,0:T(8,128)(2,1)} %collective-permute-done.17), kind=kLoop, calls=%fused_computation.12 | loop fusion | flops 1892352 | bytes 5849088 | tf_op jit(solution)/shard_map/convert_element_type | solution.py:937
  122.7 0.4 collective-permute-start.18
  123.2 0.7 collective-permute-start.19
  123.8 2.4 %collective-permute-start.20 = (bf16[4,112,384]{2,1,0:T(8,128)(2,1)S(1)}, bf16[4,112,384]{2,1,0:T(8,128)(2,1)S(1)}, u32[]{:S(2)}, u32[]{:S(2)}) collective-permute-start(bf16[4,112,384]{2,1,0:T(8,128)(2,1)S(1)} %get-tuple-element.135), channel_id=1, source_target_pairs={{0,6},{1,7},{2,4},{3,5},{4,2},{5,3},{6,0},{7,1},{8,14},{9,15},{10,... | collective-permute-start | bytes 1032200 | tf_op jit(solution)/shard_map/ppermute | solution.py:943
  126.2 26.2 %back.1 = (f32[4,4,96,384]{3,2,1,0:T(8,128)}, bf16[4,4,96,384]{3,2,1,0:T(8,128)(2,1)}) custom-call(s32[9]{0:T(128)} %concatenate.3.meta_ref, bf16[1024,1024]{1,0:T(8,128)(2,1)} %get-tuple-element.106.q_ref, bf16[1024,1024]{1,0:T(8,128)(2,1)} %get-tuple-element.107.k_ref, bf16[1024,1024]{1,0:T(8,128)(2,1)} %get-tuple-element.108.v_ref, ...), custom_call_target="tpu_custom_call" | custom-call | flops 30000001024 | bytes 20000000 | tf_op jit(solution)/shard_map/back/pallas_call | solution.py:902
  152.7 3.0 %collective-permute-done.21 = bf16[4,4,96,384]{3,2,1,0:T(8,128)(2,1)S(1)} collective-permute-done((bf16[4,4,96,384]{3,2,1,0:T(8,128)(2,1)}, bf16[4,4,96,384]{3,2,1,0:T(8,128)(2,1)S(1)}, u32[]{:S(2)}, u32[]{:S(2)}) %collective-permute-start.21) | collective-permute-done | bytes 1179680 | tf_op jit(solution)/shard_map/ppermute | solution.py:935
  155.9 0.5 collective-permute-start.22
  156.4 1.6 collective-permute-start.24
  158.0 1.5 collective-permute-start.23
  159.6 1.6 collective-permute-start.31
  161.2 2.5 %collective-permute-start.33 = (bf16[112,384]{1,0:T(8,128)(2,1)S(1)}, bf16[112,384]{1,0:T(8,128)(2,1)S(1)}, u32[]{:S(2)}, u32[]{:S(2)}) collective-permute-start(bf16[112,384]{1,0:T(8,128)(2,1)S(1)} %get-tuple-element.177), channel_id=1, source_target_pairs={{0,24},{8,16},{16,8},{24,0},{1,25},{9,17},{17,9},{25,1},{2,26},{10... | collective-permute-start | bytes 258056 | tf_op jit(solution)/shard_map/ppermute | solution.py:950
  163.7 2.2 %collective-permute-done.22 = bf16[4,96,384]{2,1,0:T(8,128)(2,1)S(1)} collective-permute-done((bf16[4,96,384]{2,1,0:T(8,128)(2,1)S(1)}, bf16[4,96,384]{2,1,0:T(8,128)(2,1)S(1)}, u32[]{:S(2)}, u32[]{:S(2)}) %collective-permute-start.22) | collective-permute-done | bytes 294944 | tf_op jit(solution)/shard_map/ppermute | solution.py:943
  166.1 2.7 %collective-permute-start.32 = (bf16[112,384]{1,0:T(8,128)(2,1)S(1)}, bf16[112,384]{1,0:T(8,128)(2,1)S(1)}, u32[]{:S(2)}, u32[]{:S(2)}) collective-permute-start(bf16[112,384]{1,0:T(8,128)(2,1)S(1)} %get-tuple-element.178), channel_id=1, source_target_pairs={{0,16},{8,24},{16,0},{24,8},{1,17},{9,25},{17,1},{25,9},{2,18},{10... | collective-permute-start | bytes 258056 | tf_op jit(solution)/shard_map/ppermute | solution.py:950
  168.8 2.7 %collective-permute-done.24 = bf16[4,96,384]{2,1,0:T(8,128)(2,1)S(1)} collective-permute-done((bf16[4,96,384]{2,1,0:T(8,128)(2,1)S(1)}, bf16[4,96,384]{2,1,0:T(8,128)(2,1)S(1)}, u32[]{:S(2)}, u32[]{:S(2)}) %collective-permute-start.24) | collective-permute-done | bytes 294944 | tf_op jit(solution)/shard_map/ppermute | solution.py:943
  171.4 1.4 collective-permute-done.23
  173.0 1.6 collective-permute-start.25
  174.7 2.5 %collective-permute-start.27 = (bf16[96,384]{1,0:T(8,128)(2,1)S(1)}, bf16[96,384]{1,0:T(8,128)(2,1)S(1)}, u32[]{:S(2)}, u32[]{:S(2)}) collective-permute-start(bf16[96,384]{1,0:T(8,128)(2,1)S(1)} %get-tuple-element.180), channel_id=1, source_target_pairs={{0,24},{8,16},{16,8},{24,0},{1,25},{9,17},{17,9},{25,1},{2,26},{10... | collective-permute-start | bytes 221192 | tf_op jit(solution)/shard_map/ppermute | solution.py:950
  177.3 3.0 %collective-permute-start.36 = (bf16[112,384]{1,0:T(8,128)(2,1)S(1)}, bf16[112,384]{1,0:T(8,128)(2,1)S(1)}, u32[]{:S(2)}, u32[]{:S(2)}) collective-permute-start(bf16[112,384]{1,0:T(8,128)(2,1)S(1)} %fusion.8.refs_4_), channel_id=1, source_target_pairs={{0,24},{8,16},{16,8},{24,0},{1,25},{9,17},{17,9},{25,1},{2,26},{10... | collective-permute-start | bytes 258056 | tf_op jit(solution)/shard_map/ppermute | solution.py:953
  180.3 0.3 collective-permute-start.35
  180.7 1.1 collective-permute-start.34
  181.8 5.6 %collective-permute-done.26 = bf16[96,384]{1,0:T(8,128)(2,1)S(1)} collective-permute-done((bf16[96,384]{1,0:T(8,128)(2,1)S(1)}, bf16[96,384]{1,0:T(8,128)(2,1)S(1)}, u32[]{:S(2)}, u32[]{:S(2)}) %collective-permute-start.26) | collective-permute-done | bytes 73760 | tf_op jit(solution)/shard_map/ppermute | solution.py:950
  187.4 4.6 %collective-permute-start.30 = (bf16[96,384]{1,0:T(8,128)(2,1)S(1)}, bf16[96,384]{1,0:T(8,128)(2,1)S(1)}, u32[]{:S(2)}, u32[]{:S(2)}) collective-permute-start(bf16[96,384]{1,0:T(8,128)(2,1)S(1)} %fusion.11.refs_0_), channel_id=1, source_target_pairs={{0,24},{8,16},{16,8},{24,0},{1,25},{9,17},{17,9},{25,1},{2,26},{10... | collective-permute-start | bytes 221192 | tf_op jit(solution)/shard_map/ppermute | solution.py:953
  192.0 0.6 collective-permute-start.28
  192.7 1.8 collective-permute-done.30.refs_3_
  194.4 2.8 %collective-permute-done.29.refs_2_ = bf16[96,384]{1,0:T(8,128)(2,1)S(1)} collective-permute-done((bf16[96,384]{1,0:T(8,128)(2,1)S(1)}, bf16[96,384]{1,0:T(8,128)(2,1)S(1)}, u32[]{:S(2)}, u32[]{:S(2)}) %collective-permute-start.29) | collective-permute-done | bytes 73760 | tf_op jit(solution)/shard_map/ppermute | solution.py:953
  197.3 0.7 square_sums.1
  198.1 1.2 collective-permute-done.37
  199.2 1.3 collective-permute-start.40
  200.6 0.7 collective-permute-start.39
  201.2 1.5 collective-permute-start.38
  202.7 1.1 collective-permute-done.40.refs_3_
  203.8 0.4 collective-permute-done.39.refs_2_
  204.2 0.7 collective-permute-done.38.refs_1_
  205.1 3.1 %update.1 = (f32[1,1]{1,0:T(1,128)}, f32[1,1]{1,0:T(1,128)}, f32[192,384]{1,0:T(8,128)}, f32[48,384]{1,0:T(8,128)}, f32[48,768]{1,0:T(8,128)}, /*index=5*/f32[48...) custom-call(f32[16,128]{1,0:T(8,128)S(1)} %add.127.refs_0_, ...), custom_call_target="tpu_custom_call" | custom-call | tf_op jit(solution)/shard_map/update/pallas_call | solution.py:1064
  (118 shorter events, 2.6 us)
Async XLA Ops:
  2.9 11.6 %collective-permute-start.2 = (bf16[352,384]{1,0:T(8,128)(2,1)}, bf16[352,384]{1,0:T(8,128)(2,1)}, u32[]{:S(2)}, u32[]{:S(2)}) collective-permute-start(bf16[352,384]{1,0:T(8,128)(2,1)} %get-tuple-element.99.refs_2_.refs_0_.refs_9_), channel_id=1, source_target_pairs={{0,6},{1,7},{2,4},{3,5},{4,2},{5,3},{6,0},{7,1},{8,14},{9,15},{10,... | collective-permute-start | bytes 811016 | tf_op jit(solution)/shard_map/ppermute | solution.py:926
  6.7 12.6 %collective-permute-start.1 = (bf16[352,384]{1,0:T(8,128)(2,1)}, bf16[352,384]{1,0:T(8,128)(2,1)}, u32[]{:S(2)}, u32[]{:S(2)}) collective-permute-start(bf16[352,384]{1,0:T(8,128)(2,1)} %get-tuple-element.99.refs_2_.refs_0_.refs_9_), channel_id=1, source_target_pairs={{0,4},{1,5},{2,6},{3,7},{4,0},{5,1},{6,2},{7,3},{8,12},{9,13},{10,... | collective-permute-start | bytes 811016 | tf_op jit(solution)/shard_map/ppermute | solution.py:926
  7.3 12.4 %collective-permute-start = (bf16[352,384]{1,0:T(8,128)(2,1)}, bf16[352,384]{1,0:T(8,128)(2,1)}, u32[]{:S(2)}, u32[]{:S(2)}) collective-permute-start(bf16[352,384]{1,0:T(8,128)(2,1)} %get-tuple-element.99.refs_2_.refs_0_.refs_9_), channel_id=1, source_target_pairs={{0,2},{1,3},{2,0},{3,1},{4,6},{5,7},{6,4},{7,5},{8,10},{9,11},{10,... | collective-permute-start | bytes 811016 | tf_op jit(solution)/shard_map/ppermute | solution.py:926
  19.6 36.4 %all-to-all-start = ((bf16[8,320,512]{2,1,0:T(8,128)(2,1)}), bf16[8,320,512]{2,1,0:T(8,128)(2,1)S(1)}, u32[]{:S(2)}, u32[]{:S(2)}) async-start(bf16[8,320,512]{2,1,0:T(8,128)(2,1)} %pack_tokens.1), calls=%async_computation | async-start | bytes 5242880 | tf_op jit(solution)/shard_map/all_to_all | solution.py:1096
  23.3 1.9 collective-permute-start.3
  23.7 17.5 %collective-permute-start.7 = (bf16[352,384]{1,0:T(8,128)(2,1)}, bf16[352,384]{1,0:T(8,128)(2,1)}, u32[]{:S(2)}, u32[]{:S(2)}) collective-permute-start(bf16[352,384]{1,0:T(8,128)(2,1)} %collective-permute-done.refs_4_.refs_2_.refs_11_), channel_id=1, source_target_pairs={{0,1},{1,0},{2,3},{3,2},{4,5},{5,4},{6,7},{7,6},{8,9},{9,8},{10,11... | collective-permute-start | bytes 811016 | tf_op jit(solution)/shard_map/ppermute | solution.py:930
  23.8 18.9 %collective-permute-start.8 = (bf16[352,384]{1,0:T(8,128)(2,1)}, bf16[352,384]{1,0:T(8,128)(2,1)}, u32[]{:S(2)}, u32[]{:S(2)}) collective-permute-start(bf16[352,384]{1,0:T(8,128)(2,1)} %collective-permute-done.1.refs_6_.refs_4_.refs_13_), channel_id=1, source_target_pairs={{0,1},{1,0},{2,3},{3,2},{4,5},{5,4},{6,7},{7,6},{8,9},{9,8},{10,11... | collective-permute-start | bytes 811016 | tf_op jit(solution)/shard_map/ppermute | solution.py:930
  24.2 18.5 %collective-permute-start.9 = (bf16[352,384]{1,0:T(8,128)(2,1)}, bf16[352,384]{1,0:T(8,128)(2,1)}, u32[]{:S(2)}, u32[]{:S(2)}) collective-permute-start(bf16[352,384]{1,0:T(8,128)(2,1)} %collective-permute-done.2.refs_8_.refs_6_.refs_15_), channel_id=1, source_target_pairs={{0,1},{1,0},{2,3},{3,2},{4,5},{5,4},{6,7},{7,6},{8,9},{9,8},{10,11... | collective-permute-start | bytes 811016 | tf_op jit(solution)/shard_map/ppermute | solution.py:930
  26.4 8.6 %collective-permute-start.6 = (s32[1]{0:T(128)}, s32[1]{0:T(128)}, u32[]{:S(2)}, u32[]{:S(2)}) collective-permute-start(s32[1]{0:T(128)} %bitcast.6), channel_id=1, source_target_pairs={{0,24},{8,16},{16,8},{24,0},{1,25},{9,17},{17,9},{25,1},{2,26},{10... | collective-permute-start | bytes 20 | tf_op jit(solution)/shard_map/ppermute | solution.py:1117
  30.0 3.6 %collective-permute-start.4 = (s32[1]{0:T(128)}, s32[1]{0:T(128)}, u32[]{:S(2)}, u32[]{:S(2)}) collective-permute-start(s32[1]{0:T(128)} %bitcast.6), channel_id=1, source_target_pairs={{0,8},{8,0},{16,24},{24,16},{1,9},{9,1},{17,25},{25,17},{2,10},{10... | collective-permute-start | bytes 20 | tf_op jit(solution)/shard_map/ppermute | solution.py:1117
  33.6 4.5 %collective-permute-start.5 = (s32[1]{0:T(128)}, s32[1]{0:T(128)}, u32[]{:S(2)}, u32[]{:S(2)}) collective-permute-start(s32[1]{0:T(128)} %bitcast.6), channel_id=1, source_target_pairs={{0,16},{8,24},{16,0},{24,8},{1,17},{9,25},{17,1},{25,9},{2,18},{10... | collective-permute-start | bytes 20 | tf_op jit(solution)/shard_map/ppermute | solution.py:1117
  35.0 48.2 %collective-permute-start.12 = (bf16[448,384]{1,0:T(8,128)(2,1)S(1)}, bf16[448,384]{1,0:T(8,128)(2,1)S(1)}, u32[]{:S(2)}, u32[]{:S(2)}) collective-permute-start(bf16[448,384]{1,0:T(8,128)(2,1)S(1)} %copy-done.29), channel_id=1, source_target_pairs={{0,6},{1,7},{2,4},{3,5},{4,2},{5,3},{6,0},{7,1},{8,14},{9,15},{10,... | collective-permute-start | bytes 1032200 | tf_op jit(solution)/shard_map/ppermute | solution.py:926
  38.1 45.1 %collective-permute-start.11 = (bf16[448,384]{1,0:T(8,128)(2,1)S(1)}, bf16[448,384]{1,0:T(8,128)(2,1)}, u32[]{:S(2)}, u32[]{:S(2)}) collective-permute-start(bf16[448,384]{1,0:T(8,128)(2,1)S(1)} %copy-done.29), channel_id=1, source_target_pairs={{0,4},{1,5},{2,6},{3,7},{4,0},{5,1},{6,2},{7,3},{8,12},{9,13},{10,... | collective-permute-start | bytes 1032200 | tf_op jit(solution)/shard_map/ppermute | solution.py:926
  41.2 42.1 %collective-permute-start.10 = (bf16[448,384]{1,0:T(8,128)(2,1)S(1)}, bf16[448,384]{1,0:T(8,128)(2,1)}, u32[]{:S(2)}, u32[]{:S(2)}) collective-permute-start(bf16[448,384]{1,0:T(8,128)(2,1)S(1)} %copy-done.29), channel_id=1, source_target_pairs={{0,2},{1,3},{2,0},{3,1},{4,6},{5,7},{6,4},{7,5},{8,10},{9,11},{10,... | collective-permute-start | bytes 1032200 | tf_op jit(solution)/shard_map/ppermute | solution.py:926
  83.3 1.7 collective-permute-start.13
  83.4 2.3 %collective-permute-start.14 = (bf16[448,384]{1,0:T(8,128)(2,1)}, bf16[448,384]{1,0:T(8,128)(2,1)S(1)}, u32[]{:S(2)}, u32[]{:S(2)}) collective-permute-start(bf16[448,384]{1,0:T(8,128)(2,1)} %collective-permute-done.10.refs_10_), channel_id=1, source_target_pairs={{0,1},{1,0},{2,3},{3,2},{4,5},{5,4},{6,7},{7,6},{8,9},{9,8},{10,11... | collective-permute-start | bytes 1032200 | tf_op jit(solution)/shard_map/ppermute | solution.py:930
  83.9 2.8 %collective-permute-start.15 = (bf16[448,384]{1,0:T(8,128)(2,1)}, bf16[448,384]{1,0:T(8,128)(2,1)S(1)}, u32[]{:S(2)}, u32[]{:S(2)}) collective-permute-start(bf16[448,384]{1,0:T(8,128)(2,1)} %collective-permute-done.11.refs_12_), channel_id=1, source_target_pairs={{0,1},{1,0},{2,3},{3,2},{4,5},{5,4},{6,7},{7,6},{8,9},{9,8},{10,11... | collective-permute-start | bytes 1032200 | tf_op jit(solution)/shard_map/ppermute | solution.py:930
  84.0 2.8 %collective-permute-start.16 = (bf16[448,384]{1,0:T(8,128)(2,1)S(1)}, bf16[448,384]{1,0:T(8,128)(2,1)S(1)}, u32[]{:S(2)}, u32[]{:S(2)}) collective-permute-start(bf16[448,384]{1,0:T(8,128)(2,1)S(1)} %collective-permute-done.12.refs_14_), channel_id=1, source_target_pairs={{0,1},{1,0},{2,3},{3,2},{4,5},{5,4},{6,7},{7,6},{8,9},{9,8},{10,11... | collective-permute-start | bytes 1032200 | tf_op jit(solution)/shard_map/ppermute | solution.py:930
  112.7 7.5 %collective-permute-start.17 = (bf16[4,4,112,384]{3,2,1,0:T(8,128)(2,1)}, bf16[4,4,112,384]{3,2,1,0:T(8,128)(2,1)}, u32[]{:S(2)}, u32[]{:S(2)}) collective-permute-start(bf16[4,4,112,384]{3,2,1,0:T(8,128)(2,1)} %get-tuple-element.122), channel_id=1, source_target_pairs={{0,1},{1,0},{2,3},{3,2},{4,5},{5,4},{6,7},{7,6},{8,9},{9,8},{10,11... | collective-permute-start | bytes 4128776 | tf_op jit(solution)/shard_map/ppermute | solution.py:935
  122.7 29.7 %collective-permute-start.18 = (bf16[4,112,384]{2,1,0:T(8,128)(2,1)}, bf16[4,112,384]{2,1,0:T(8,128)(2,1)S(1)}, u32[]{:S(2)}, u32[]{:S(2)}) collective-permute-start(bf16[4,112,384]{2,1,0:T(8,128)(2,1)} %get-tuple-element.133), channel_id=1, source_target_pairs={{0,2},{1,3},{2,0},{3,1},{4,6},{5,7},{6,4},{7,5},{8,10},{9,11},{10,... | collective-permute-start | bytes 1032200 | tf_op jit(solution)/shard_map/ppermute | solution.py:943
  123.2 29.3 %collective-permute-start.19 = (bf16[4,112,384]{2,1,0:T(8,128)(2,1)}, bf16[4,112,384]{2,1,0:T(8,128)(2,1)S(1)}, u32[]{:S(2)}, u32[]{:S(2)}) collective-permute-start(bf16[4,112,384]{2,1,0:T(8,128)(2,1)} %get-tuple-element.134), channel_id=1, source_target_pairs={{0,4},{1,5},{2,6},{3,7},{4,0},{5,1},{6,2},{7,3},{8,12},{9,13},{10,... | collective-permute-start | bytes 1032200 | tf_op jit(solution)/shard_map/ppermute | solution.py:943
  123.8 28.6 %collective-permute-start.20 = (bf16[4,112,384]{2,1,0:T(8,128)(2,1)S(1)}, bf16[4,112,384]{2,1,0:T(8,128)(2,1)S(1)}, u32[]{:S(2)}, u32[]{:S(2)}) collective-permute-start(bf16[4,112,384]{2,1,0:T(8,128)(2,1)S(1)} %get-tuple-element.135), channel_id=1, source_target_pairs={{0,6},{1,7},{2,4},{3,5},{4,2},{5,3},{6,0},{7,1},{8,14},{9,15},{10,... | collective-permute-start | bytes 1032200 | tf_op jit(solution)/shard_map/ppermute | solution.py:943
  152.6 3.1 %collective-permute-start.21 = (bf16[4,4,96,384]{3,2,1,0:T(8,128)(2,1)}, bf16[4,4,96,384]{3,2,1,0:T(8,128)(2,1)S(1)}, u32[]{:S(2)}, u32[]{:S(2)}) collective-permute-start(bf16[4,4,96,384]{3,2,1,0:T(8,128)(2,1)} %get-tuple-element.136), channel_id=1, source_target_pairs={{0,1},{1,0},{2,3},{3,2},{4,5},{5,4},{6,7},{7,6},{8,9},{9,8},{10,11... | collective-permute-start | bytes 3538952 | tf_op jit(solution)/shard_map/ppermute | solution.py:935
  155.9 9.9 %collective-permute-start.22 = (bf16[4,96,384]{2,1,0:T(8,128)(2,1)S(1)}, bf16[4,96,384]{2,1,0:T(8,128)(2,1)S(1)}, u32[]{:S(2)}, u32[]{:S(2)}) collective-permute-start(bf16[4,96,384]{2,1,0:T(8,128)(2,1)S(1)} %get-tuple-element.173), channel_id=1, source_target_pairs={{0,2},{1,3},{2,0},{3,1},{4,6},{5,7},{6,4},{7,5},{8,10},{9,11},{10,... | collective-permute-start | bytes 884744 | tf_op jit(solution)/shard_map/ppermute | solution.py:943
  156.4 15.0 %collective-permute-start.24 = (bf16[4,96,384]{2,1,0:T(8,128)(2,1)S(1)}, bf16[4,96,384]{2,1,0:T(8,128)(2,1)S(1)}, u32[]{:S(2)}, u32[]{:S(2)}) collective-permute-start(bf16[4,96,384]{2,1,0:T(8,128)(2,1)S(1)} %get-tuple-element.174), channel_id=1, source_target_pairs={{0,6},{1,7},{2,4},{3,5},{4,2},{5,3},{6,0},{7,1},{8,14},{9,15},{10,... | collective-permute-start | bytes 884744 | tf_op jit(solution)/shard_map/ppermute | solution.py:943
  158.0 14.8 %collective-permute-start.23 = (bf16[4,96,384]{2,1,0:T(8,128)(2,1)S(1)}, bf16[4,96,384]{2,1,0:T(8,128)(2,1)S(1)}, u32[]{:S(2)}, u32[]{:S(2)}) collective-permute-start(bf16[4,96,384]{2,1,0:T(8,128)(2,1)S(1)} %get-tuple-element.175), channel_id=1, source_target_pairs={{0,4},{1,5},{2,6},{3,7},{4,0},{5,1},{6,2},{7,3},{8,12},{9,13},{10,... | collective-permute-start | bytes 884744 | tf_op jit(solution)/shard_map/ppermute | solution.py:943
  159.6 17.6 %collective-permute-start.31 = (bf16[112,384]{1,0:T(8,128)(2,1)S(1)}, bf16[112,384]{1,0:T(8,128)(2,1)S(1)}, u32[]{:S(2)}, u32[]{:S(2)}) collective-permute-start(bf16[112,384]{1,0:T(8,128)(2,1)S(1)} %get-tuple-element.176), channel_id=1, source_target_pairs={{0,8},{8,0},{16,24},{24,16},{1,9},{9,1},{17,25},{25,17},{2,10},{10... | collective-permute-start | bytes 258056 | tf_op jit(solution)/shard_map/ppermute | solution.py:950
  161.2 16.1 %collective-permute-start.33 = (bf16[112,384]{1,0:T(8,128)(2,1)S(1)}, bf16[112,384]{1,0:T(8,128)(2,1)S(1)}, u32[]{:S(2)}, u32[]{:S(2)}) collective-permute-start(bf16[112,384]{1,0:T(8,128)(2,1)S(1)} %get-tuple-element.177), channel_id=1, source_target_pairs={{0,24},{8,16},{16,8},{24,0},{1,25},{9,17},{17,9},{25,1},{2,26},{10... | collective-permute-start | bytes 258056 | tf_op jit(solution)/shard_map/ppermute | solution.py:950
  165.8 39.0 %copy-start.1 = (f32[192,384]{1,0:T(8,128)S(1)}, f32[192,384]{1,0:T(8,128)}, u32[]{:S(2)}) copy-start(f32[192,384]{1,0:T(8,128)} %refs_6_.1) | copy-start | bytes 884740
  165.8 39.0 %copy-start.2 = (f32[48,1536]{1,0:T(8,128)S(1)}, f32[48,1536]{1,0:T(8,128)}, u32[]{:S(2)}) copy-start(f32[48,1536]{1,0:T(8,128)} %refs_10_.1) | copy-start | bytes 884740
  165.8 39.0 %copy-start.3 = (f32[192,384]{1,0:T(8,128)S(1)}, f32[192,384]{1,0:T(8,128)}, u32[]{:S(2)}) copy-start(f32[192,384]{1,0:T(8,128)} %refs_11_.1) | copy-start | bytes 884740
  165.8 39.0 %copy-start.4 = (f32[48,768]{1,0:T(8,128)S(1)}, f32[48,768]{1,0:T(8,128)}, u32[]{:S(2)}) copy-start(f32[48,768]{1,0:T(8,128)} %refs_8_.1) | copy-start | bytes 442372
  165.9 39.0 %copy-start.5 = (f32[192,384]{1,0:T(8,128)S(1)}, f32[192,384]{1,0:T(8,128)}, u32[]{:S(2)}) copy-start(f32[192,384]{1,0:T(8,128)} %refs_14_.1) | copy-start | bytes 884740
  165.9 39.0 %copy-start.6 = (f32[48,1536]{1,0:T(8,128)S(1)}, f32[48,1536]{1,0:T(8,128)}, u32[]{:S(2)}) copy-start(f32[48,1536]{1,0:T(8,128)} %refs_18_.1) | copy-start | bytes 884740
  165.9 39.0 %copy-start.7 = (f32[192,384]{1,0:T(8,128)S(1)}, f32[192,384]{1,0:T(8,128)}, u32[]{:S(2)}) copy-start(f32[192,384]{1,0:T(8,128)} %refs_19_.1) | copy-start | bytes 884740
  165.9 39.0 %copy-start.8 = (f32[192,384]{1,0:T(8,128)S(1)}, f32[192,384]{1,0:T(8,128)}, u32[]{:S(2)}) copy-start(f32[192,384]{1,0:T(8,128)} %refs_22_.1) | copy-start | bytes 884740
  165.9 39.0 %copy-start.9 = (f32[48,1536]{1,0:T(8,128)S(1)}, f32[48,1536]{1,0:T(8,128)}, u32[]{:S(2)}) copy-start(f32[48,1536]{1,0:T(8,128)} %refs_26_.1) | copy-start | bytes 884740
  165.9 39.0 %copy-start.10 = (f32[192,384]{1,0:T(8,128)S(1)}, f32[192,384]{1,0:T(8,128)}, u32[]{:S(2)}) copy-start(f32[192,384]{1,0:T(8,128)} %refs_27_.1) | copy-start | bytes 884740
  165.9 39.0 %copy-start.11 = (f32[48,384]{1,0:T(8,128)S(1)}, f32[48,384]{1,0:T(8,128)}, u32[]{:S(2)}) copy-start(f32[48,384]{1,0:T(8,128)} %refs_7_.1) | copy-start | bytes 221188
  165.9 39.0 %copy-start.12 = (f32[48,384]{1,0:T(8,128)S(1)}, f32[48,384]{1,0:T(8,128)}, u32[]{:S(2)}) copy-start(f32[48,384]{1,0:T(8,128)} %refs_9_.1) | copy-start | bytes 221188
  165.9 39.0 %copy-start.13 = (f32[48,768]{1,0:T(8,128)S(1)}, f32[48,768]{1,0:T(8,128)}, u32[]{:S(2)}) copy-start(f32[48,768]{1,0:T(8,128)} %refs_16_.1) | copy-start | bytes 442372
  166.0 39.0 %copy-start.14 = (f32[48,768]{1,0:T(8,128)S(1)}, f32[48,768]{1,0:T(8,128)}, u32[]{:S(2)}) copy-start(f32[48,768]{1,0:T(8,128)} %refs_24_.1) | copy-start | bytes 442372
  166.0 39.0 %copy-start.15 = (f32[48,128]{1,0:T(8,128)S(1)}, f32[48,128]{1,0:T(8,128)}, u32[]{:S(2)}) copy-start(f32[48,128]{1,0:T(8,128)} %refs_12_.1) | copy-start | bytes 73732
  166.0 39.0 %copy-start.16 = (f32[48,384]{1,0:T(8,128)S(1)}, f32[48,384]{1,0:T(8,128)}, u32[]{:S(2)}) copy-start(f32[48,384]{1,0:T(8,128)} %refs_15_.1) | copy-start | bytes 221188
  166.0 39.0 %copy-start.17 = (f32[48,384]{1,0:T(8,128)S(1)}, f32[48,384]{1,0:T(8,128)}, u32[]{:S(2)}) copy-start(f32[48,384]{1,0:T(8,128)} %refs_17_.1) | copy-start | bytes 221188
  166.0 39.0 %copy-start.18 = (f32[48,384]{1,0:T(8,128)S(1)}, f32[48,384]{1,0:T(8,128)}, u32[]{:S(2)}) copy-start(f32[48,384]{1,0:T(8,128)} %refs_23_.1) | copy-start | bytes 221188
  166.0 39.0 %copy-start.19 = (f32[48,384]{1,0:T(8,128)S(1)}, f32[48,384]{1,0:T(8,128)}, u32[]{:S(2)}) copy-start(f32[48,384]{1,0:T(8,128)} %refs_25_.1) | copy-start | bytes 221188
  166.0 39.0 %copy-start.20 = (f32[48,128]{1,0:T(8,128)S(1)}, f32[48,128]{1,0:T(8,128)}, u32[]{:S(2)}) copy-start(f32[48,128]{1,0:T(8,128)} %refs_20_.1) | copy-start | bytes 73732
  166.0 39.0 %copy-start.21 = (f32[48,128]{1,0:T(8,128)S(1)}, f32[48,128]{1,0:T(8,128)}, u32[]{:S(2)}) copy-start(f32[48,128]{1,0:T(8,128)} %refs_28_.1) | copy-start | bytes 73732
  166.1 39.0 %copy-start.22 = (f32[5,48]{1,0:T(8,128)S(1)}, f32[5,48]{1,0:T(8,128)}, u32[]{:S(2)}) copy-start(f32[5,48]{1,0:T(8,128)} %refs_13_.1) | copy-start | bytes 2884
  166.1 11.2 %collective-permute-start.32 = (bf16[112,384]{1,0:T(8,128)(2,1)S(1)}, bf16[112,384]{1,0:T(8,128)(2,1)S(1)}, u32[]{:S(2)}, u32[]{:S(2)}) collective-permute-start(bf16[112,384]{1,0:T(8,128)(2,1)S(1)} %get-tuple-element.178), channel_id=1, source_target_pairs={{0,16},{8,24},{16,0},{24,8},{1,17},{9,25},{17,1},{25,9},{2,18},{10... | collective-permute-start | bytes 258056 | tf_op jit(solution)/shard_map/ppermute | solution.py:950
  173.0 7.6 %collective-permute-start.25 = (bf16[96,384]{1,0:T(8,128)(2,1)S(1)}, bf16[96,384]{1,0:T(8,128)(2,1)S(1)}, u32[]{:S(2)}, u32[]{:S(2)}) collective-permute-start(bf16[96,384]{1,0:T(8,128)(2,1)S(1)} %get-tuple-element.179), channel_id=1, source_target_pairs={{0,8},{8,0},{16,24},{24,16},{1,9},{9,1},{17,25},{25,17},{2,10},{10... | collective-permute-start | bytes 221192 | tf_op jit(solution)/shard_map/ppermute | solution.py:950
  174.7 7.1 %collective-permute-start.27 = (bf16[96,384]{1,0:T(8,128)(2,1)S(1)}, bf16[96,384]{1,0:T(8,128)(2,1)S(1)}, u32[]{:S(2)}, u32[]{:S(2)}) collective-permute-start(bf16[96,384]{1,0:T(8,128)(2,1)S(1)} %get-tuple-element.180), channel_id=1, source_target_pairs={{0,24},{8,16},{16,8},{24,0},{1,25},{9,17},{17,9},{25,1},{2,26},{10... | collective-permute-start | bytes 221192 | tf_op jit(solution)/shard_map/ppermute | solution.py:950
  177.1 10.3 %collective-permute-start.26 = (bf16[96,384]{1,0:T(8,128)(2,1)S(1)}, bf16[96,384]{1,0:T(8,128)(2,1)S(1)}, u32[]{:S(2)}, u32[]{:S(2)}) collective-permute-start(bf16[96,384]{1,0:T(8,128)(2,1)S(1)} %get-tuple-element.181), channel_id=1, source_target_pairs={{0,16},{8,24},{16,0},{24,8},{1,17},{9,25},{17,1},{25,9},{2,18},{10... | collective-permute-start | bytes 221192 | tf_op jit(solution)/shard_map/ppermute | solution.py:950
  177.3 14.7 %collective-permute-start.36 = (bf16[112,384]{1,0:T(8,128)(2,1)S(1)}, bf16[112,384]{1,0:T(8,128)(2,1)S(1)}, u32[]{:S(2)}, u32[]{:S(2)}) collective-permute-start(bf16[112,384]{1,0:T(8,128)(2,1)S(1)} %fusion.8.refs_4_), channel_id=1, source_target_pairs={{0,24},{8,16},{16,8},{24,0},{1,25},{9,17},{17,9},{25,1},{2,26},{10... | collective-permute-start | bytes 258056 | tf_op jit(solution)/shard_map/ppermute | solution.py:953
  180.3 12.4 %collective-permute-start.35 = (bf16[112,384]{1,0:T(8,128)(2,1)S(1)}, bf16[112,384]{1,0:T(8,128)(2,1)S(1)}, u32[]{:S(2)}, u32[]{:S(2)}) collective-permute-start(bf16[112,384]{1,0:T(8,128)(2,1)S(1)} %fusion.8.refs_4_), channel_id=1, source_target_pairs={{0,16},{8,24},{16,0},{24,8},{1,17},{9,25},{17,1},{25,9},{2,18},{10... | collective-permute-start | bytes 258056 | tf_op jit(solution)/shard_map/ppermute | solution.py:953
  180.7 12.0 %collective-permute-start.34 = (bf16[112,384]{1,0:T(8,128)(2,1)S(1)}, bf16[112,384]{1,0:T(8,128)(2,1)S(1)}, u32[]{:S(2)}, u32[]{:S(2)}) collective-permute-start(bf16[112,384]{1,0:T(8,128)(2,1)S(1)} %fusion.8.refs_4_), channel_id=1, source_target_pairs={{0,8},{8,0},{16,24},{24,16},{1,9},{9,1},{17,25},{25,17},{2,10},{10... | collective-permute-start | bytes 258056 | tf_op jit(solution)/shard_map/ppermute | solution.py:953
  187.4 7.0 %collective-permute-start.30 = (bf16[96,384]{1,0:T(8,128)(2,1)S(1)}, bf16[96,384]{1,0:T(8,128)(2,1)S(1)}, u32[]{:S(2)}, u32[]{:S(2)}) collective-permute-start(bf16[96,384]{1,0:T(8,128)(2,1)S(1)} %fusion.11.refs_0_), channel_id=1, source_target_pairs={{0,24},{8,16},{16,8},{24,0},{1,25},{9,17},{17,9},{25,1},{2,26},{10... | collective-permute-start | bytes 221192 | tf_op jit(solution)/shard_map/ppermute | solution.py:953
  192.0 5.3 %collective-permute-start.29 = (bf16[96,384]{1,0:T(8,128)(2,1)S(1)}, bf16[96,384]{1,0:T(8,128)(2,1)S(1)}, u32[]{:S(2)}, u32[]{:S(2)}) collective-permute-start(bf16[96,384]{1,0:T(8,128)(2,1)S(1)} %fusion.11.refs_0_), channel_id=1, source_target_pairs={{0,16},{8,24},{16,0},{24,8},{1,17},{9,25},{17,1},{25,9},{2,18},{10... | collective-permute-start | bytes 221192 | tf_op jit(solution)/shard_map/ppermute | solution.py:953
  192.0 5.2 %collective-permute-start.28 = (bf16[96,384]{1,0:T(8,128)(2,1)S(1)}, bf16[96,384]{1,0:T(8,128)(2,1)S(1)}, u32[]{:S(2)}, u32[]{:S(2)}) collective-permute-start(bf16[96,384]{1,0:T(8,128)(2,1)S(1)} %fusion.11.refs_0_), channel_id=1, source_target_pairs={{0,8},{8,0},{16,24},{24,16},{1,9},{9,1},{17,25},{25,17},{2,10},{10... | collective-permute-start | bytes 221192 | tf_op jit(solution)/shard_map/ppermute | solution.py:953
  198.0 1.2 collective-permute-start.37
  199.2 4.5 %collective-permute-start.40 = (f32[16,128]{1,0:T(8,128)S(1)}, f32[16,128]{1,0:T(8,128)S(1)}, u32[]{:S(2)}, u32[]{:S(2)}) collective-permute-start(f32[16,128]{1,0:T(8,128)S(1)} %add.127.refs_0_), channel_id=1, source_target_pairs={{0,6},{1,7},{2,4},{3,5},{4,2},{5,3},{6,0},{7,1},{8,14},{9,15},{10,... | collective-permute-start | bytes 24584 | tf_op jit(solution)/shard_map/ppermute | solution.py:1153
  200.6 3.7 %collective-permute-start.39 = (f32[16,128]{1,0:T(8,128)S(1)}, f32[16,128]{1,0:T(8,128)S(1)}, u32[]{:S(2)}, u32[]{:S(2)}) collective-permute-start(f32[16,128]{1,0:T(8,128)S(1)} %add.127.refs_0_), channel_id=1, source_target_pairs={{0,4},{1,5},{2,6},{3,7},{4,0},{5,1},{6,2},{7,3},{8,12},{9,13},{10,... | collective-permute-start | bytes 24584 | tf_op jit(solution)/shard_map/ppermute | solution.py:1153
  201.2 3.7 %collective-permute-start.38 = (f32[16,128]{1,0:T(8,128)S(1)}, f32[16,128]{1,0:T(8,128)S(1)}, u32[]{:S(2)}, u32[]{:S(2)}) collective-permute-start(f32[16,128]{1,0:T(8,128)S(1)} %add.127.refs_0_), channel_id=1, source_target_pairs={{0,2},{1,3},{2,0},{3,1},{4,6},{5,7},{6,4},{7,5},{8,10},{9,11},{10,... | collective-permute-start | bytes 24584 | tf_op jit(solution)/shard_map/ppermute | solution.py:1153
  (16 other events, 222.2 us)

commit v2 on v1

--- a/solution.py
+++ b/solution.py
@@ -612,13 +612,7 @@
         spare_grad = tn(att_s[...], bg_s[...])
         for h in range(H):
             go_s[h * hd : (h + 1) * hd, :] = spare_grad[h * LANES : h * LANES + hd, :]
-
-        def up_columns(c, carry):
-            here = pl.ds(pl.multiple_of(c * D, LANES), D)
-            gu_s[:, here] = tn(fin_s[...], hg_s[:, here])
-            return carry
-
-        lax.fori_loop(0, F // D, up_columns, 0)
+        gu_s[...] = tn(fin_s[...], hg_s[...])
         gd_s[...] = tn(act_s[...], fg_s[...])
         gh_s[...] = tn(low_s[...], pg_s[...])
         if z.direct:
@@ -912,6 +906,21 @@
     )(*args)
 
 
+def place_meta(meta):
+    def kernel(meta_ref, o_ref):
+        for i in range(meta.shape[0]):
+            o_ref[i] = meta_ref[i]
+
+    return pl.pallas_call(
+        kernel,
+        out_shape=jax.ShapeDtypeStruct(meta.shape, meta.dtype),
+        in_specs=[smem()],
+        out_specs=smem(),
+        compiler_params=pltpu.CompilerParams(vmem_limit_bytes=63 * 1024 * 1024),
+        name="place_meta",
+    )(meta)
+
+
 def pairs(count, mask):
     return [(i, i ^ mask) for i in range(count)]
 
@@ -1126,6 +1135,8 @@
         ]
     ).astype(jnp.int32)
     meta, sample_count = lax.optimization_barrier((meta, sample_count))
+    if z.direct:
+        meta = place_meta(meta)
 
     x, stream, slope, normed, sn, q, k, v, att = front(z, meta, moved, spectral_all, halo, weights)
     if z.direct:

time: 210 us -> 208 us (level)
  no operation moved by 1% of the time
where the time goes in v2:
time: 208 us; the launch traced here: 207 us
  Pallas kernels  93 us (45%)
  starting transfers between devices  52.1 us (25%)
  waiting for transfers between devices  50.4 us (24%)
  between operations  4.99 us (2%)
  other arithmetic  3.8 us (2%)
  local copies, waits for them, and re-layouts  3.06 us (1%)
    pallas_call x1, Pallas kernels, back(): pl.pallas_call(kernel, grid=(steps,), out_shape=[jax.ShapeDtypeStruct(s,...  26.2 us
    pallas_call x1, Pallas kernels, front(): pl.pallas_call(kernel, grid=(H,), out_shape=[jax.ShapeDtypeStruct(s, d) f...  25.7 us
    pallas_call x1, Pallas kernels, middle(): pl.pallas_call(kernel, grid=(1,), out_shape=[jax.ShapeDtypeStruct(s, d) f...  23.9 us
    all_to_all x1, waiting for transfers between devices, on_device(): lax.all_to_all(packed, 'tm', 0, 0, axis_index_groups=groups, tiled=True)  12 us
    ppermute x6, starting transfers between devices, over_planes(): there = lax.ppermute(mine[m].astype(bfloat), 'seg', pairs(z.planes, m))  11 us
    ppermute x6, starting transfers between devices, from_chips(): lax.ppermute(own, 'tm', pairs(z.n, 2 * m))  10.4 us
    ppermute x6, starting transfers between devices, over_planes(): lax.ppermute(low, 'seg', pairs(z.planes, m))  9.66 us
    ppermute x6, waiting for transfers between devices, from_chips(): lax.ppermute(own, 'tm', pairs(z.n, 2 * m))  9.48 us
  transfers between devices with their start and end apart: 42, of which 21 were waited for; matrix products, arithmetic and copies ran while one was open for 1% of the time, Pallas kernels for 30%

profile of v2, /device:TPU:0, one launch (start us, length us, event | category | flops | bytes accessed | tf_op | source)
XLA Modules:
  0.0 207.3 jit_solution(17026501156175091580)
XLA Ops:
  0.7 2.2 %pack_weights.1 = (bf16[352,384]{1,0:T(8,128)(2,1)}, bf16[448,384]{1,0:T(8,128)(2,1)}) custom-call(s32[1]{0:T(128)} %bitcast.1.place_ref, f32[192,384]{1,0:T(8,128)} %refs_6_.1, f32[48,384]{1,0:T(8,128)} %refs_7_.1, f32[48,768]{1,0:T(8,128)} %refs_8_.1, f32[48,384]{1,0:T(8,128)} %refs_9_.1, f32[48,1536]{1,0:T(8,128)} %refs_10_.1, f32[192,384]{1,0:T(8,128)} %refs_11_.1, ...), custom_call_target="tpu_custom_call" | custom-call | tf_op jit(solution)/shard_map/pack_weights/pallas_call | solution.py:156
  2.9 3.9 %collective-permute-start.2 = (bf16[352,384]{1,0:T(8,128)(2,1)}, bf16[352,384]{1,0:T(8,128)(2,1)}, u32[]{:S(2)}, u32[]{:S(2)}) collective-permute-start(bf16[352,384]{1,0:T(8,128)(2,1)} %get-tuple-element.99.refs_2_.refs_0_.refs_9_), channel_id=1, source_target_pairs={{0,6},{1,7},{2,4},{3,5},{4,2},{5,3},{6,0},{7,1},{8,14},{9,15},{10,... | collective-permute-start | bytes 811016 | tf_op jit(solution)/shard_map/ppermute | solution.py:935
  6.7 0.5 collective-permute-start.1
  7.3 2.8 %pack_tokens.1 = bf16[8,320,512]{2,1,0:T(8,128)(2,1)} custom-call(bf16[8,192,512]{2,1,0:T(8,128)(2,1)} %bitcast.55, bf16[8,128,384]{2,1,0:T(8,128)(2,1)} %s_ref.1, bf16[8,128,128]{2,1,0:T(8,128)(2,1)} %t_ref.1), custom_call_target="tpu_custom_call" | custom-call | tf_op jit(solution)/shard_map/pack_tokens/pallas_call | solution.py:192
  10.2 4.3 %collective-permute-done.2.refs_8_.refs_6_.refs_15_ = bf16[352,384]{1,0:T(8,128)(2,1)} collective-permute-done((bf16[352,384]{1,0:T(8,128)(2,1)}, bf16[352,384]{1,0:T(8,128)(2,1)}, u32[]{:S(2)}, u32[]{:S(2)}) %collective-permute-start.2) | collective-permute-done | bytes 270368 | tf_op jit(solution)/shard_map/ppermute | solution.py:935
  14.4 4.9 %collective-permute-done.1.refs_6_.refs_4_.refs_13_ = bf16[352,384]{1,0:T(8,128)(2,1)} collective-permute-done((bf16[352,384]{1,0:T(8,128)(2,1)}, bf16[352,384]{1,0:T(8,128)(2,1)}, u32[]{:S(2)}, u32[]{:S(2)}) %collective-permute-start.1) | collective-permute-done | bytes 270368 | tf_op jit(solution)/shard_map/ppermute | solution.py:935
  19.6 4.4 %all-to-all-start = ((bf16[8,320,512]{2,1,0:T(8,128)(2,1)}), bf16[8,320,512]{2,1,0:T(8,128)(2,1)}, u32[]{:S(2)}, u32[]{:S(2)}) async-start(bf16[8,320,512]{2,1,0:T(8,128)(2,1)} %pack_tokens.1), calls=%async_computation | async-start | bytes 5242880 | tf_op jit(solution)/shard_map/all_to_all | solution.py:1105
  24.0 0.4 collective-permute-start.3
  24.6 0.3 collective-permute-start.8
  25.3 0.6 collective-permute-done.3.refs_3_.refs_1_.refs_10_
  25.9 0.6 reduce_sum.9
  26.5 0.6 dynamic_slice.8
  27.1 3.6 %collective-permute-start.6 = (s32[1]{0:T(128)}, s32[1]{0:T(128)}, u32[]{:S(2)}, u32[]{:S(2)}) collective-permute-start(s32[1]{0:T(128)} %bitcast.6), channel_id=1, source_target_pairs={{0,24},{8,16},{16,8},{24,0},{1,25},{9,17},{17,9},{25,1},{2,26},{10... | collective-permute-start | bytes 20 | tf_op jit(solution)/shard_map/ppermute | solution.py:1126
  30.7 1.2 concatenate.3.meta_ref
  32.0 2.5 %collective-permute-done.4 = s32[1]{0:T(128)} collective-permute-done((s32[1]{0:T(128)}, s32[1]{0:T(128)}, u32[]{:S(2)}, u32[]{:S(2)}) %collective-permute-start.4) | collective-permute-done | bytes 36 | tf_op jit(solution)/shard_map/ppermute | solution.py:1126
  35.8 2.7 %collective-permute-start.12 = (bf16[448,384]{1,0:T(8,128)(2,1)S(1)}, bf16[448,384]{1,0:T(8,128)(2,1)S(1)}, u32[]{:S(2)}, u32[]{:S(2)}) collective-permute-start(bf16[448,384]{1,0:T(8,128)(2,1)S(1)} %copy-done.28), channel_id=1, source_target_pairs={{0,6},{1,7},{2,4},{3,5},{4,2},{5,3},{6,0},{7,1},{8,14},{9,15},{10,... | collective-permute-start | bytes 1032200 | tf_op jit(solution)/shard_map/ppermute | solution.py:935
  38.5 0.7 collective-permute-done.5
  39.2 1.7 collective-permute-start.11
  42.2 1.2 place_meta.1.meta_ref
  43.4 1.5 collective-permute-start.10
  44.9 12.0 %all-to-all-done.refs_0_.refs_1_.target_ref.refs_3_ = bf16[8,320,512]{2,1,0:T(8,128)(2,1)} async-done(((bf16[8,320,512]{2,1,0:T(8,128)(2,1)}), bf16[8,320,512]{2,1,0:T(8,128)(2,1)}, u32[]{:S(2)}, u32[]{:S(2)}) %all-to-all-start) | async-done | bytes 2621472 | tf_op jit(solution)/shard_map/all_to_all | solution.py:1105
  56.9 25.7 %front.1 = (bf16[1024,768]{1,0:T(8,128)(2,1)}, f32[1024,384]{1,0:T(8,128)}, f32[1024,384]{1,0:T(8,128)}, bf16[1024,384]{1,0:T(8,128)(2,1)}, bf16[1024,384]{1,0:T...) custom-call(s32[9]{0:T(128)} %place_meta.1.meta_ref, ...), custom_call_target="tpu_custom_call" | custom-call | flops 20000000000 | bytes 20000000 | tf_op jit(solution)/shard_map/front/pallas_call | solution.py:433
  82.7 0.5 collective-permute-start.14
  83.3 0.4 collective-permute-start.16
  83.7 0.6 collective-permute-done.13.refs_9_
  84.3 0.5 collective-permute-done.14.refs_11_
  84.8 1.2 collective-permute-done.15.refs_13_
  86.1 0.7 copy-done.33
  86.9 23.9 %middle.1 = (bf16[1024,1024]{1,0:T(8,128)(2,1)}, f32[1024,384]{1,0:T(8,128)}, f32[8,384]{1,0:T(8,128)}, f32[4,4,112,384]{3,2,1,0:T(8,128)}, bf16[4,4,112,384]{3,2,1,0:T(8,128)(2,1)}) custom-call(s32[9]{0:T(128)} %place_meta.1.meta_ref, f32[1]{0:T(128)} %convert_element_type.137.count_ref, f32[1024,384]{1,0:T(8,128)} %get-tuple-element.110.stream_ref.refs_4_, ...), custom_call_target="tpu_custom_call" | custom-call | flops 20000000000 | bytes 20000000 | tf_op jit(solution)/shard_map/middle/pallas_call | solution.py:669
  110.9 7.3 %attend_back.1 = (bf16[1024,256]{1,0:T(8,128)(2,1)}, bf16[2,96,1024]{2,1,0:T(8,128)(2,1)}) custom-call(bf16[1024,1024]{1,0:T(8,128)(2,1)} %get-tuple-element.106.q_ref, bf16[1024,1024]{1,0:T(8,128)(2,1)} %get-tuple-element.107.k_ref, bf16[1024,1024]{1,0:T(8,128)(2,1)} %get-tuple-element.108.v_ref, bf16[1024,1024]{1,0:T(8,128)(2,1)} %get-tuple-element.118.do_ref), custom_call_target="tpu_custom_call" | custom-call | flops 8000000000 | bytes 12000000 | tf_op jit(solution)/shard_map/attend_back/pallas_call | solution.py:717
  118.3 2.5 %fusion.3 = (bf16[4,112,384]{2,1,0:T(8,128)(2,1)S(1)}, bf16[4,112,384]{2,1,0:T(8,128)(2,1)}, bf16[4,112,384]{2,1,0:T(8,128)(2,1)}, f32[4,112,384]{2,1,0:T(8,128)S(1)}) fusion(f32[4,4,112,384]{3,2,1,0:T(8,128)S(1)} %copy-done.26, bf16[4,4,112,384]{3,2,1,0:T(8,128)(2,1)} %collective-permute-done.17), kind=kLoop, calls=%fused_computation.12 | loop fusion | flops 1892352 | bytes 5849088 | tf_op jit(solution)/shard_map/convert_element_type | solution.py:946
  120.8 0.4 collective-permute-start.18
  121.2 0.7 collective-permute-start.19
  121.9 2.4 %collective-permute-start.20 = (bf16[4,112,384]{2,1,0:T(8,128)(2,1)S(1)}, bf16[4,112,384]{2,1,0:T(8,128)(2,1)S(1)}, u32[]{:S(2)}, u32[]{:S(2)}) collective-permute-start(bf16[4,112,384]{2,1,0:T(8,128)(2,1)S(1)} %get-tuple-element.135), channel_id=1, source_target_pairs={{0,6},{1,7},{2,4},{3,5},{4,2},{5,3},{6,0},{7,1},{8,14},{9,15},{10,... | collective-permute-start | bytes 1032200 | tf_op jit(solution)/shard_map/ppermute | solution.py:952
  124.3 26.2 %back.1 = (f32[4,4,96,384]{3,2,1,0:T(8,128)}, bf16[4,4,96,384]{3,2,1,0:T(8,128)(2,1)}) custom-call(s32[9]{0:T(128)} %place_meta.1.meta_ref, bf16[1024,1024]{1,0:T(8,128)(2,1)} %get-tuple-element.106.q_ref, bf16[1024,1024]{1,0:T(8,128)(2,1)} %get-tuple-element.107.k_ref, bf16[1024,1024]{1,0:T(8,128)(2,1)} %get-tuple-element.108.v_ref, ...), custom_call_target="tpu_custom_call" | custom-call | flops 30000001024 | bytes 20000000 | tf_op jit(solution)/shard_map/back/pallas_call | solution.py:896
  150.7 3.0 %collective-permute-done.21 = bf16[4,4,96,384]{3,2,1,0:T(8,128)(2,1)S(1)} collective-permute-done((bf16[4,4,96,384]{3,2,1,0:T(8,128)(2,1)}, bf16[4,4,96,384]{3,2,1,0:T(8,128)(2,1)S(1)}, u32[]{:S(2)}, u32[]{:S(2)}) %collective-permute-start.21) | collective-permute-done | bytes 1179680 | tf_op jit(solution)/shard_map/ppermute | solution.py:944
  154.0 0.5 collective-permute-start.22
  154.5 1.6 collective-permute-start.24
  156.1 1.5 collective-permute-start.23
  157.6 1.6 collective-permute-start.31
  159.3 2.5 %collective-permute-start.33 = (bf16[112,384]{1,0:T(8,128)(2,1)S(1)}, bf16[112,384]{1,0:T(8,128)(2,1)S(1)}, u32[]{:S(2)}, u32[]{:S(2)}) collective-permute-start(bf16[112,384]{1,0:T(8,128)(2,1)S(1)} %get-tuple-element.177), channel_id=1, source_target_pairs={{0,24},{8,16},{16,8},{24,0},{1,25},{9,17},{17,9},{25,1},{2,26},{10... | collective-permute-start | bytes 258056 | tf_op jit(solution)/shard_map/ppermute | solution.py:959
  161.8 2.2 %collective-permute-done.22 = bf16[4,96,384]{2,1,0:T(8,128)(2,1)S(1)} collective-permute-done((bf16[4,96,384]{2,1,0:T(8,128)(2,1)S(1)}, bf16[4,96,384]{2,1,0:T(8,128)(2,1)S(1)}, u32[]{:S(2)}, u32[]{:S(2)}) %collective-permute-start.22) | collective-permute-done | bytes 294944 | tf_op jit(solution)/shard_map/ppermute | solution.py:952
  164.2 2.7 %collective-permute-start.32 = (bf16[112,384]{1,0:T(8,128)(2,1)S(1)}, bf16[112,384]{1,0:T(8,128)(2,1)S(1)}, u32[]{:S(2)}, u32[]{:S(2)}) collective-permute-start(bf16[112,384]{1,0:T(8,128)(2,1)S(1)} %get-tuple-element.178), channel_id=1, source_target_pairs={{0,16},{8,24},{16,0},{24,8},{1,17},{9,25},{17,1},{25,9},{2,18},{10... | collective-permute-start | bytes 258056 | tf_op jit(solution)/shard_map/ppermute | solution.py:959
  166.8 2.7 %collective-permute-done.24 = bf16[4,96,384]{2,1,0:T(8,128)(2,1)S(1)} collective-permute-done((bf16[4,96,384]{2,1,0:T(8,128)(2,1)S(1)}, bf16[4,96,384]{2,1,0:T(8,128)(2,1)S(1)}, u32[]{:S(2)}, u32[]{:S(2)}) %collective-permute-start.24) | collective-permute-done | bytes 294944 | tf_op jit(solution)/shard_map/ppermute | solution.py:952
  169.5 1.4 collective-permute-done.23
  171.1 1.6 collective-permute-start.25
  172.7 2.5 %collective-permute-start.27 = (bf16[96,384]{1,0:T(8,128)(2,1)S(1)}, bf16[96,384]{1,0:T(8,128)(2,1)S(1)}, u32[]{:S(2)}, u32[]{:S(2)}) collective-permute-start(bf16[96,384]{1,0:T(8,128)(2,1)S(1)} %get-tuple-element.180), channel_id=1, source_target_pairs={{0,24},{8,16},{16,8},{24,0},{1,25},{9,17},{17,9},{25,1},{2,26},{10... | collective-permute-start | bytes 221192 | tf_op jit(solution)/shard_map/ppermute | solution.py:959
  175.4 3.0 %collective-permute-start.36 = (bf16[112,384]{1,0:T(8,128)(2,1)S(1)}, bf16[112,384]{1,0:T(8,128)(2,1)S(1)}, u32[]{:S(2)}, u32[]{:S(2)}) collective-permute-start(bf16[112,384]{1,0:T(8,128)(2,1)S(1)} %fusion.8.refs_4_), channel_id=1, source_target_pairs={{0,24},{8,16},{16,8},{24,0},{1,25},{9,17},{17,9},{25,1},{2,26},{10... | collective-permute-start | bytes 258056 | tf_op jit(solution)/shard_map/ppermute | solution.py:962
  178.4 0.3 collective-permute-start.35
  178.7 1.1 collective-permute-start.34
  179.8 5.6 %collective-permute-done.26 = bf16[96,384]{1,0:T(8,128)(2,1)S(1)} collective-permute-done((bf16[96,384]{1,0:T(8,128)(2,1)S(1)}, bf16[96,384]{1,0:T(8,128)(2,1)S(1)}, u32[]{:S(2)}, u32[]{:S(2)}) %collective-permute-start.26) | collective-permute-done | bytes 73760 | tf_op jit(solution)/shard_map/ppermute | solution.py:959
  185.5 4.6 %collective-permute-start.30 = (bf16[96,384]{1,0:T(8,128)(2,1)S(1)}, bf16[96,384]{1,0:T(8,128)(2,1)S(1)}, u32[]{:S(2)}, u32[]{:S(2)}) collective-permute-start(bf16[96,384]{1,0:T(8,128)(2,1)S(1)} %fusion.11.refs_0_), channel_id=1, source_target_pairs={{0,24},{8,16},{16,8},{24,0},{1,25},{9,17},{17,9},{25,1},{2,26},{10... | collective-permute-start | bytes 221192 | tf_op jit(solution)/shard_map/ppermute | solution.py:962
  190.1 0.6 collective-permute-start.28
  190.7 1.8 collective-permute-done.30.refs_3_
  192.5 2.8 %collective-permute-done.29.refs_2_ = bf16[96,384]{1,0:T(8,128)(2,1)S(1)} collective-permute-done((bf16[96,384]{1,0:T(8,128)(2,1)S(1)}, bf16[96,384]{1,0:T(8,128)(2,1)S(1)}, u32[]{:S(2)}, u32[]{:S(2)}) %collective-permute-start.29) | collective-permute-done | bytes 73760 | tf_op jit(solution)/shard_map/ppermute | solution.py:962
  195.3 0.7 square_sums.1
  196.1 1.2 collective-permute-done.37
  197.3 1.3 collective-permute-start.40
  198.6 0.7 collective-permute-start.39
  199.3 1.5 collective-permute-start.38
  200.8 1.1 collective-permute-done.40.refs_3_
  201.9 0.4 collective-permute-done.39.refs_2_
  202.3 0.7 collective-permute-done.38.refs_1_
  203.2 3.1 %update.1 = (f32[1,1]{1,0:T(1,128)}, f32[1,1]{1,0:T(1,128)}, f32[192,384]{1,0:T(8,128)}, f32[48,384]{1,0:T(8,128)}, f32[48,768]{1,0:T(8,128)}, /*index=5*/f32[48...) custom-call(f32[16,128]{1,0:T(8,128)S(1)} %add.127.refs_0_, ...), custom_call_target="tpu_custom_call" | custom-call | tf_op jit(solution)/shard_map/update/pallas_call | solution.py:1073
  (119 shorter events, 2.6 us)
Async XLA Ops:
  2.9 11.6 %collective-permute-start.2 = (bf16[352,384]{1,0:T(8,128)(2,1)}, bf16[352,384]{1,0:T(8,128)(2,1)}, u32[]{:S(2)}, u32[]{:S(2)}) collective-permute-start(bf16[352,384]{1,0:T(8,128)(2,1)} %get-tuple-element.99.refs_2_.refs_0_.refs_9_), channel_id=1, source_target_pairs={{0,6},{1,7},{2,4},{3,5},{4,2},{5,3},{6,0},{7,1},{8,14},{9,15},{10,... | collective-permute-start | bytes 811016 | tf_op jit(solution)/shard_map/ppermute | solution.py:935
  6.7 12.6 %collective-permute-start.1 = (bf16[352,384]{1,0:T(8,128)(2,1)}, bf16[352,384]{1,0:T(8,128)(2,1)}, u32[]{:S(2)}, u32[]{:S(2)}) collective-permute-start(bf16[352,384]{1,0:T(8,128)(2,1)} %get-tuple-element.99.refs_2_.refs_0_.refs_9_), channel_id=1, source_target_pairs={{0,4},{1,5},{2,6},{3,7},{4,0},{5,1},{6,2},{7,3},{8,12},{9,13},{10,... | collective-permute-start | bytes 811016 | tf_op jit(solution)/shard_map/ppermute | solution.py:935
  7.3 12.4 %collective-permute-start = (bf16[352,384]{1,0:T(8,128)(2,1)}, bf16[352,384]{1,0:T(8,128)(2,1)}, u32[]{:S(2)}, u32[]{:S(2)}) collective-permute-start(bf16[352,384]{1,0:T(8,128)(2,1)} %get-tuple-element.99.refs_2_.refs_0_.refs_9_), channel_id=1, source_target_pairs={{0,2},{1,3},{2,0},{3,1},{4,6},{5,7},{6,4},{7,5},{8,10},{9,11},{10,... | collective-permute-start | bytes 811016 | tf_op jit(solution)/shard_map/ppermute | solution.py:935
  19.6 37.2 %all-to-all-start = ((bf16[8,320,512]{2,1,0:T(8,128)(2,1)}), bf16[8,320,512]{2,1,0:T(8,128)(2,1)}, u32[]{:S(2)}, u32[]{:S(2)}) async-start(bf16[8,320,512]{2,1,0:T(8,128)(2,1)} %pack_tokens.1), calls=%async_computation | async-start | bytes 5242880 | tf_op jit(solution)/shard_map/all_to_all | solution.py:1105
  24.0 1.9 collective-permute-start.3
  24.4 19.0 %collective-permute-start.7 = (bf16[352,384]{1,0:T(8,128)(2,1)}, bf16[352,384]{1,0:T(8,128)(2,1)}, u32[]{:S(2)}, u32[]{:S(2)}) collective-permute-start(bf16[352,384]{1,0:T(8,128)(2,1)} %collective-permute-done.refs_4_.refs_2_.refs_11_), channel_id=1, source_target_pairs={{0,1},{1,0},{2,3},{3,2},{4,5},{5,4},{6,7},{7,6},{8,9},{9,8},{10,11... | collective-permute-start | bytes 811016 | tf_op jit(solution)/shard_map/ppermute | solution.py:939
  24.6 20.3 %collective-permute-start.8 = (bf16[352,384]{1,0:T(8,128)(2,1)}, bf16[352,384]{1,0:T(8,128)(2,1)}, u32[]{:S(2)}, u32[]{:S(2)}) collective-permute-start(bf16[352,384]{1,0:T(8,128)(2,1)} %collective-permute-done.1.refs_6_.refs_4_.refs_13_), channel_id=1, source_target_pairs={{0,1},{1,0},{2,3},{3,2},{4,5},{5,4},{6,7},{7,6},{8,9},{9,8},{10,11... | collective-permute-start | bytes 811016 | tf_op jit(solution)/shard_map/ppermute | solution.py:939
  24.9 20.0 %collective-permute-start.9 = (bf16[352,384]{1,0:T(8,128)(2,1)}, bf16[352,384]{1,0:T(8,128)(2,1)}, u32[]{:S(2)}, u32[]{:S(2)}) collective-permute-start(bf16[352,384]{1,0:T(8,128)(2,1)} %collective-permute-done.2.refs_8_.refs_6_.refs_15_), channel_id=1, source_target_pairs={{0,1},{1,0},{2,3},{3,2},{4,5},{5,4},{6,7},{7,6},{8,9},{9,8},{10,11... | collective-permute-start | bytes 811016 | tf_op jit(solution)/shard_map/ppermute | solution.py:939
  27.1 8.6 %collective-permute-start.6 = (s32[1]{0:T(128)}, s32[1]{0:T(128)}, u32[]{:S(2)}, u32[]{:S(2)}) collective-permute-start(s32[1]{0:T(128)} %bitcast.6), channel_id=1, source_target_pairs={{0,24},{8,16},{16,8},{24,0},{1,25},{9,17},{17,9},{25,1},{2,26},{10... | collective-permute-start | bytes 20 | tf_op jit(solution)/shard_map/ppermute | solution.py:1126
  30.7 3.8 %collective-permute-start.4 = (s32[1]{0:T(128)}, s32[1]{0:T(128)}, u32[]{:S(2)}, u32[]{:S(2)}) collective-permute-start(s32[1]{0:T(128)} %bitcast.6), channel_id=1, source_target_pairs={{0,8},{8,0},{16,24},{24,16},{1,9},{9,1},{17,25},{25,17},{2,10},{10... | collective-permute-start | bytes 20 | tf_op jit(solution)/shard_map/ppermute | solution.py:1126
  34.5 4.7 %collective-permute-start.5 = (s32[1]{0:T(128)}, s32[1]{0:T(128)}, u32[]{:S(2)}, u32[]{:S(2)}) collective-permute-start(s32[1]{0:T(128)} %bitcast.6), channel_id=1, source_target_pairs={{0,16},{8,24},{16,0},{24,8},{1,17},{9,25},{17,1},{25,9},{2,18},{10... | collective-permute-start | bytes 20 | tf_op jit(solution)/shard_map/ppermute | solution.py:1126
  35.8 46.8 %collective-permute-start.12 = (bf16[448,384]{1,0:T(8,128)(2,1)S(1)}, bf16[448,384]{1,0:T(8,128)(2,1)S(1)}, u32[]{:S(2)}, u32[]{:S(2)}) collective-permute-start(bf16[448,384]{1,0:T(8,128)(2,1)S(1)} %copy-done.28), channel_id=1, source_target_pairs={{0,6},{1,7},{2,4},{3,5},{4,2},{5,3},{6,0},{7,1},{8,14},{9,15},{10,... | collective-permute-start | bytes 1032200 | tf_op jit(solution)/shard_map/ppermute | solution.py:935
  39.2 43.4 %collective-permute-start.11 = (bf16[448,384]{1,0:T(8,128)(2,1)S(1)}, bf16[448,384]{1,0:T(8,128)(2,1)}, u32[]{:S(2)}, u32[]{:S(2)}) collective-permute-start(bf16[448,384]{1,0:T(8,128)(2,1)S(1)} %copy-done.28), channel_id=1, source_target_pairs={{0,4},{1,5},{2,6},{3,7},{4,0},{5,1},{6,2},{7,3},{8,12},{9,13},{10,... | collective-permute-start | bytes 1032200 | tf_op jit(solution)/shard_map/ppermute | solution.py:935
  43.4 39.2 %collective-permute-start.10 = (bf16[448,384]{1,0:T(8,128)(2,1)S(1)}, bf16[448,384]{1,0:T(8,128)(2,1)S(1)}, u32[]{:S(2)}, u32[]{:S(2)}) collective-permute-start(bf16[448,384]{1,0:T(8,128)(2,1)S(1)} %copy-done.28), channel_id=1, source_target_pairs={{0,2},{1,3},{2,0},{3,1},{4,6},{5,7},{6,4},{7,5},{8,10},{9,11},{10,... | collective-permute-start | bytes 1032200 | tf_op jit(solution)/shard_map/ppermute | solution.py:935
  82.6 1.7 collective-permute-start.13
  82.7 2.1 %collective-permute-start.14 = (bf16[448,384]{1,0:T(8,128)(2,1)S(1)}, bf16[448,384]{1,0:T(8,128)(2,1)S(1)}, u32[]{:S(2)}, u32[]{:S(2)}) collective-permute-start(bf16[448,384]{1,0:T(8,128)(2,1)S(1)} %collective-permute-done.10.refs_10_), channel_id=1, source_target_pairs={{0,1},{1,0},{2,3},{3,2},{4,5},{5,4},{6,7},{7,6},{8,9},{9,8},{10,11... | collective-permute-start | bytes 1032200 | tf_op jit(solution)/shard_map/ppermute | solution.py:939
  83.2 2.8 %collective-permute-start.15 = (bf16[448,384]{1,0:T(8,128)(2,1)}, bf16[448,384]{1,0:T(8,128)(2,1)S(1)}, u32[]{:S(2)}, u32[]{:S(2)}) collective-permute-start(bf16[448,384]{1,0:T(8,128)(2,1)} %collective-permute-done.11.refs_12_), channel_id=1, source_target_pairs={{0,1},{1,0},{2,3},{3,2},{4,5},{5,4},{6,7},{7,6},{8,9},{9,8},{10,11... | collective-permute-start | bytes 1032200 | tf_op jit(solution)/shard_map/ppermute | solution.py:939
  83.3 2.8 %collective-permute-start.16 = (bf16[448,384]{1,0:T(8,128)(2,1)S(1)}, bf16[448,384]{1,0:T(8,128)(2,1)S(1)}, u32[]{:S(2)}, u32[]{:S(2)}) collective-permute-start(bf16[448,384]{1,0:T(8,128)(2,1)S(1)} %collective-permute-done.12.refs_14_), channel_id=1, source_target_pairs={{0,1},{1,0},{2,3},{3,2},{4,5},{5,4},{6,7},{7,6},{8,9},{9,8},{10,11... | collective-permute-start | bytes 1032200 | tf_op jit(solution)/shard_map/ppermute | solution.py:939
  110.7 7.5 %collective-permute-start.17 = (bf16[4,4,112,384]{3,2,1,0:T(8,128)(2,1)}, bf16[4,4,112,384]{3,2,1,0:T(8,128)(2,1)}, u32[]{:S(2)}, u32[]{:S(2)}) collective-permute-start(bf16[4,4,112,384]{3,2,1,0:T(8,128)(2,1)} %get-tuple-element.122), channel_id=1, source_target_pairs={{0,1},{1,0},{2,3},{3,2},{4,5},{5,4},{6,7},{7,6},{8,9},{9,8},{10,11... | collective-permute-start | bytes 4128776 | tf_op jit(solution)/shard_map/ppermute | solution.py:944
  120.8 29.7 %collective-permute-start.18 = (bf16[4,112,384]{2,1,0:T(8,128)(2,1)}, bf16[4,112,384]{2,1,0:T(8,128)(2,1)S(1)}, u32[]{:S(2)}, u32[]{:S(2)}) collective-permute-start(bf16[4,112,384]{2,1,0:T(8,128)(2,1)} %get-tuple-element.133), channel_id=1, source_target_pairs={{0,2},{1,3},{2,0},{3,1},{4,6},{5,7},{6,4},{7,5},{8,10},{9,11},{10,... | collective-permute-start | bytes 1032200 | tf_op jit(solution)/shard_map/ppermute | solution.py:952
  121.2 29.3 %collective-permute-start.19 = (bf16[4,112,384]{2,1,0:T(8,128)(2,1)}, bf16[4,112,384]{2,1,0:T(8,128)(2,1)S(1)}, u32[]{:S(2)}, u32[]{:S(2)}) collective-permute-start(bf16[4,112,384]{2,1,0:T(8,128)(2,1)} %get-tuple-element.134), channel_id=1, source_target_pairs={{0,4},{1,5},{2,6},{3,7},{4,0},{5,1},{6,2},{7,3},{8,12},{9,13},{10,... | collective-permute-start | bytes 1032200 | tf_op jit(solution)/shard_map/ppermute | solution.py:952
  121.9 28.6 %collective-permute-start.20 = (bf16[4,112,384]{2,1,0:T(8,128)(2,1)S(1)}, bf16[4,112,384]{2,1,0:T(8,128)(2,1)S(1)}, u32[]{:S(2)}, u32[]{:S(2)}) collective-permute-start(bf16[4,112,384]{2,1,0:T(8,128)(2,1)S(1)} %get-tuple-element.135), channel_id=1, source_target_pairs={{0,6},{1,7},{2,4},{3,5},{4,2},{5,3},{6,0},{7,1},{8,14},{9,15},{10,... | collective-permute-start | bytes 1032200 | tf_op jit(solution)/shard_map/ppermute | solution.py:952
  150.7 3.1 %collective-permute-start.21 = (bf16[4,4,96,384]{3,2,1,0:T(8,128)(2,1)}, bf16[4,4,96,384]{3,2,1,0:T(8,128)(2,1)S(1)}, u32[]{:S(2)}, u32[]{:S(2)}) collective-permute-start(bf16[4,4,96,384]{3,2,1,0:T(8,128)(2,1)} %get-tuple-element.136), channel_id=1, source_target_pairs={{0,1},{1,0},{2,3},{3,2},{4,5},{5,4},{6,7},{7,6},{8,9},{9,8},{10,11... | collective-permute-start | bytes 3538952 | tf_op jit(solution)/shard_map/ppermute | solution.py:944
  154.0 9.9 %collective-permute-start.22 = (bf16[4,96,384]{2,1,0:T(8,128)(2,1)S(1)}, bf16[4,96,384]{2,1,0:T(8,128)(2,1)S(1)}, u32[]{:S(2)}, u32[]{:S(2)}) collective-permute-start(bf16[4,96,384]{2,1,0:T(8,128)(2,1)S(1)} %get-tuple-element.173), channel_id=1, source_target_pairs={{0,2},{1,3},{2,0},{3,1},{4,6},{5,7},{6,4},{7,5},{8,10},{9,11},{10,... | collective-permute-start | bytes 884744 | tf_op jit(solution)/shard_map/ppermute | solution.py:952
  154.5 15.1 %collective-permute-start.24 = (bf16[4,96,384]{2,1,0:T(8,128)(2,1)S(1)}, bf16[4,96,384]{2,1,0:T(8,128)(2,1)S(1)}, u32[]{:S(2)}, u32[]{:S(2)}) collective-permute-start(bf16[4,96,384]{2,1,0:T(8,128)(2,1)S(1)} %get-tuple-element.174), channel_id=1, source_target_pairs={{0,6},{1,7},{2,4},{3,5},{4,2},{5,3},{6,0},{7,1},{8,14},{9,15},{10,... | collective-permute-start | bytes 884744 | tf_op jit(solution)/shard_map/ppermute | solution.py:952
  156.1 14.8 %collective-permute-start.23 = (bf16[4,96,384]{2,1,0:T(8,128)(2,1)S(1)}, bf16[4,96,384]{2,1,0:T(8,128)(2,1)S(1)}, u32[]{:S(2)}, u32[]{:S(2)}) collective-permute-start(bf16[4,96,384]{2,1,0:T(8,128)(2,1)S(1)} %get-tuple-element.175), channel_id=1, source_target_pairs={{0,4},{1,5},{2,6},{3,7},{4,0},{5,1},{6,2},{7,3},{8,12},{9,13},{10,... | collective-permute-start | bytes 884744 | tf_op jit(solution)/shard_map/ppermute | solution.py:952
  157.6 17.6 %collective-permute-start.31 = (bf16[112,384]{1,0:T(8,128)(2,1)S(1)}, bf16[112,384]{1,0:T(8,128)(2,1)S(1)}, u32[]{:S(2)}, u32[]{:S(2)}) collective-permute-start(bf16[112,384]{1,0:T(8,128)(2,1)S(1)} %get-tuple-element.176), channel_id=1, source_target_pairs={{0,8},{8,0},{16,24},{24,16},{1,9},{9,1},{17,25},{25,17},{2,10},{10... | collective-permute-start | bytes 258056 | tf_op jit(solution)/shard_map/ppermute | solution.py:959
  159.3 16.0 %collective-permute-start.33 = (bf16[112,384]{1,0:T(8,128)(2,1)S(1)}, bf16[112,384]{1,0:T(8,128)(2,1)S(1)}, u32[]{:S(2)}, u32[]{:S(2)}) collective-permute-start(bf16[112,384]{1,0:T(8,128)(2,1)S(1)} %get-tuple-element.177), channel_id=1, source_target_pairs={{0,24},{8,16},{16,8},{24,0},{1,25},{9,17},{17,9},{25,1},{2,26},{10... | collective-permute-start | bytes 258056 | tf_op jit(solution)/shard_map/ppermute | solution.py:959
  163.9 39.0 %copy-start.1 = (f32[192,384]{1,0:T(8,128)S(1)}, f32[192,384]{1,0:T(8,128)}, u32[]{:S(2)}) copy-start(f32[192,384]{1,0:T(8,128)} %refs_6_.1) | copy-start | bytes 884740
  163.9 39.0 %copy-start.2 = (f32[48,1536]{1,0:T(8,128)S(1)}, f32[48,1536]{1,0:T(8,128)}, u32[]{:S(2)}) copy-start(f32[48,1536]{1,0:T(8,128)} %refs_10_.1) | copy-start | bytes 884740
  163.9 39.0 %copy-start.3 = (f32[192,384]{1,0:T(8,128)S(1)}, f32[192,384]{1,0:T(8,128)}, u32[]{:S(2)}) copy-start(f32[192,384]{1,0:T(8,128)} %refs_11_.1) | copy-start | bytes 884740
  163.9 39.0 %copy-start.4 = (f32[48,768]{1,0:T(8,128)S(1)}, f32[48,768]{1,0:T(8,128)}, u32[]{:S(2)}) copy-start(f32[48,768]{1,0:T(8,128)} %refs_8_.1) | copy-start | bytes 442372
  163.9 39.0 %copy-start.5 = (f32[192,384]{1,0:T(8,128)S(1)}, f32[192,384]{1,0:T(8,128)}, u32[]{:S(2)}) copy-start(f32[192,384]{1,0:T(8,128)} %refs_14_.1) | copy-start | bytes 884740
  163.9 39.0 %copy-start.6 = (f32[48,1536]{1,0:T(8,128)S(1)}, f32[48,1536]{1,0:T(8,128)}, u32[]{:S(2)}) copy-start(f32[48,1536]{1,0:T(8,128)} %refs_18_.1) | copy-start | bytes 884740
  163.9 39.0 %copy-start.7 = (f32[192,384]{1,0:T(8,128)S(1)}, f32[192,384]{1,0:T(8,128)}, u32[]{:S(2)}) copy-start(f32[192,384]{1,0:T(8,128)} %refs_19_.1) | copy-start | bytes 884740
  164.0 39.0 %copy-start.8 = (f32[192,384]{1,0:T(8,128)S(1)}, f32[192,384]{1,0:T(8,128)}, u32[]{:S(2)}) copy-start(f32[192,384]{1,0:T(8,128)} %refs_22_.1) | copy-start | bytes 884740
  164.0 39.0 %copy-start.9 = (f32[48,1536]{1,0:T(8,128)S(1)}, f32[48,1536]{1,0:T(8,128)}, u32[]{:S(2)}) copy-start(f32[48,1536]{1,0:T(8,128)} %refs_26_.1) | copy-start | bytes 884740
  164.0 39.0 %copy-start.10 = (f32[192,384]{1,0:T(8,128)S(1)}, f32[192,384]{1,0:T(8,128)}, u32[]{:S(2)}) copy-start(f32[192,384]{1,0:T(8,128)} %refs_27_.1) | copy-start | bytes 884740
  164.0 39.0 %copy-start.11 = (f32[48,384]{1,0:T(8,128)S(1)}, f32[48,384]{1,0:T(8,128)}, u32[]{:S(2)}) copy-start(f32[48,384]{1,0:T(8,128)} %refs_7_.1) | copy-start | bytes 221188
  164.0 39.0 %copy-start.12 = (f32[48,384]{1,0:T(8,128)S(1)}, f32[48,384]{1,0:T(8,128)}, u32[]{:S(2)}) copy-start(f32[48,384]{1,0:T(8,128)} %refs_9_.1) | copy-start | bytes 221188
  164.0 39.0 %copy-start.13 = (f32[48,768]{1,0:T(8,128)S(1)}, f32[48,768]{1,0:T(8,128)}, u32[]{:S(2)}) copy-start(f32[48,768]{1,0:T(8,128)} %refs_16_.1) | copy-start | bytes 442372
  164.0 39.0 %copy-start.14 = (f32[48,768]{1,0:T(8,128)S(1)}, f32[48,768]{1,0:T(8,128)}, u32[]{:S(2)}) copy-start(f32[48,768]{1,0:T(8,128)} %refs_24_.1) | copy-start | bytes 442372
  164.0 39.0 %copy-start.15 = (f32[48,128]{1,0:T(8,128)S(1)}, f32[48,128]{1,0:T(8,128)}, u32[]{:S(2)}) copy-start(f32[48,128]{1,0:T(8,128)} %refs_12_.1) | copy-start | bytes 73732
  164.0 39.0 %copy-start.16 = (f32[48,384]{1,0:T(8,128)S(1)}, f32[48,384]{1,0:T(8,128)}, u32[]{:S(2)}) copy-start(f32[48,384]{1,0:T(8,128)} %refs_15_.1) | copy-start | bytes 221188
  164.1 39.0 %copy-start.17 = (f32[48,384]{1,0:T(8,128)S(1)}, f32[48,384]{1,0:T(8,128)}, u32[]{:S(2)}) copy-start(f32[48,384]{1,0:T(8,128)} %refs_17_.1) | copy-start | bytes 221188
  164.1 39.0 %copy-start.18 = (f32[48,384]{1,0:T(8,128)S(1)}, f32[48,384]{1,0:T(8,128)}, u32[]{:S(2)}) copy-start(f32[48,384]{1,0:T(8,128)} %refs_23_.1) | copy-start | bytes 221188
  164.1 39.0 %copy-start.19 = (f32[48,384]{1,0:T(8,128)S(1)}, f32[48,384]{1,0:T(8,128)}, u32[]{:S(2)}) copy-start(f32[48,384]{1,0:T(8,128)} %refs_25_.1) | copy-start | bytes 221188
  164.1 39.0 %copy-start.20 = (f32[48,128]{1,0:T(8,128)S(1)}, f32[48,128]{1,0:T(8,128)}, u32[]{:S(2)}) copy-start(f32[48,128]{1,0:T(8,128)} %refs_20_.1) | copy-start | bytes 73732
  164.1 39.0 %copy-start.21 = (f32[48,128]{1,0:T(8,128)S(1)}, f32[48,128]{1,0:T(8,128)}, u32[]{:S(2)}) copy-start(f32[48,128]{1,0:T(8,128)} %refs_28_.1) | copy-start | bytes 73732
  164.1 39.0 %copy-start.22 = (f32[5,48]{1,0:T(8,128)S(1)}, f32[5,48]{1,0:T(8,128)}, u32[]{:S(2)}) copy-start(f32[5,48]{1,0:T(8,128)} %refs_13_.1) | copy-start | bytes 2884
  164.2 11.2 %collective-permute-start.32 = (bf16[112,384]{1,0:T(8,128)(2,1)S(1)}, bf16[112,384]{1,0:T(8,128)(2,1)S(1)}, u32[]{:S(2)}, u32[]{:S(2)}) collective-permute-start(bf16[112,384]{1,0:T(8,128)(2,1)S(1)} %get-tuple-element.178), channel_id=1, source_target_pairs={{0,16},{8,24},{16,0},{24,8},{1,17},{9,25},{17,1},{25,9},{2,18},{10... | collective-permute-start | bytes 258056 | tf_op jit(solution)/shard_map/ppermute | solution.py:959
  171.1 7.6 %collective-permute-start.25 = (bf16[96,384]{1,0:T(8,128)(2,1)S(1)}, bf16[96,384]{1,0:T(8,128)(2,1)S(1)}, u32[]{:S(2)}, u32[]{:S(2)}) collective-permute-start(bf16[96,384]{1,0:T(8,128)(2,1)S(1)} %get-tuple-element.179), channel_id=1, source_target_pairs={{0,8},{8,0},{16,24},{24,16},{1,9},{9,1},{17,25},{25,17},{2,10},{10... | collective-permute-start | bytes 221192 | tf_op jit(solution)/shard_map/ppermute | solution.py:959
  172.7 7.1 %collective-permute-start.27 = (bf16[96,384]{1,0:T(8,128)(2,1)S(1)}, bf16[96,384]{1,0:T(8,128)(2,1)S(1)}, u32[]{:S(2)}, u32[]{:S(2)}) collective-permute-start(bf16[96,384]{1,0:T(8,128)(2,1)S(1)} %get-tuple-element.180), channel_id=1, source_target_pairs={{0,24},{8,16},{16,8},{24,0},{1,25},{9,17},{17,9},{25,1},{2,26},{10... | collective-permute-start | bytes 221192 | tf_op jit(solution)/shard_map/ppermute | solution.py:959
  175.2 10.3 %collective-permute-start.26 = (bf16[96,384]{1,0:T(8,128)(2,1)S(1)}, bf16[96,384]{1,0:T(8,128)(2,1)S(1)}, u32[]{:S(2)}, u32[]{:S(2)}) collective-permute-start(bf16[96,384]{1,0:T(8,128)(2,1)S(1)} %get-tuple-element.181), channel_id=1, source_target_pairs={{0,16},{8,24},{16,0},{24,8},{1,17},{9,25},{17,1},{25,9},{2,18},{10... | collective-permute-start | bytes 221192 | tf_op jit(solution)/shard_map/ppermute | solution.py:959
  175.4 14.7 %collective-permute-start.36 = (bf16[112,384]{1,0:T(8,128)(2,1)S(1)}, bf16[112,384]{1,0:T(8,128)(2,1)S(1)}, u32[]{:S(2)}, u32[]{:S(2)}) collective-permute-start(bf16[112,384]{1,0:T(8,128)(2,1)S(1)} %fusion.8.refs_4_), channel_id=1, source_target_pairs={{0,24},{8,16},{16,8},{24,0},{1,25},{9,17},{17,9},{25,1},{2,26},{10... | collective-permute-start | bytes 258056 | tf_op jit(solution)/shard_map/ppermute | solution.py:962
  178.4 12.4 %collective-permute-start.35 = (bf16[112,384]{1,0:T(8,128)(2,1)S(1)}, bf16[112,384]{1,0:T(8,128)(2,1)S(1)}, u32[]{:S(2)}, u32[]{:S(2)}) collective-permute-start(bf16[112,384]{1,0:T(8,128)(2,1)S(1)} %fusion.8.refs_4_), channel_id=1, source_target_pairs={{0,16},{8,24},{16,0},{24,8},{1,17},{9,25},{17,1},{25,9},{2,18},{10... | collective-permute-start | bytes 258056 | tf_op jit(solution)/shard_map/ppermute | solution.py:962
  178.7 12.0 %collective-permute-start.34 = (bf16[112,384]{1,0:T(8,128)(2,1)S(1)}, bf16[112,384]{1,0:T(8,128)(2,1)S(1)}, u32[]{:S(2)}, u32[]{:S(2)}) collective-permute-start(bf16[112,384]{1,0:T(8,128)(2,1)S(1)} %fusion.8.refs_4_), channel_id=1, source_target_pairs={{0,8},{8,0},{16,24},{24,16},{1,9},{9,1},{17,25},{25,17},{2,10},{10... | collective-permute-start | bytes 258056 | tf_op jit(solution)/shard_map/ppermute | solution.py:962
  185.5 7.0 %collective-permute-start.30 = (bf16[96,384]{1,0:T(8,128)(2,1)S(1)}, bf16[96,384]{1,0:T(8,128)(2,1)S(1)}, u32[]{:S(2)}, u32[]{:S(2)}) collective-permute-start(bf16[96,384]{1,0:T(8,128)(2,1)S(1)} %fusion.11.refs_0_), channel_id=1, source_target_pairs={{0,24},{8,16},{16,8},{24,0},{1,25},{9,17},{17,9},{25,1},{2,26},{10... | collective-permute-start | bytes 221192 | tf_op jit(solution)/shard_map/ppermute | solution.py:962
  190.1 5.3 %collective-permute-start.29 = (bf16[96,384]{1,0:T(8,128)(2,1)S(1)}, bf16[96,384]{1,0:T(8,128)(2,1)S(1)}, u32[]{:S(2)}, u32[]{:S(2)}) collective-permute-start(bf16[96,384]{1,0:T(8,128)(2,1)S(1)} %fusion.11.refs_0_), channel_id=1, source_target_pairs={{0,16},{8,24},{16,0},{24,8},{1,17},{9,25},{17,1},{25,9},{2,18},{10... | collective-permute-start | bytes 221192 | tf_op jit(solution)/shard_map/ppermute | solution.py:962
  190.1 5.2 %collective-permute-start.28 = (bf16[96,384]{1,0:T(8,128)(2,1)S(1)}, bf16[96,384]{1,0:T(8,128)(2,1)S(1)}, u32[]{:S(2)}, u32[]{:S(2)}) collective-permute-start(bf16[96,384]{1,0:T(8,128)(2,1)S(1)} %fusion.11.refs_0_), channel_id=1, source_target_pairs={{0,8},{8,0},{16,24},{24,16},{1,9},{9,1},{17,25},{25,17},{2,10},{10... | collective-permute-start | bytes 221192 | tf_op jit(solution)/shard_map/ppermute | solution.py:962
  196.1 1.2 collective-permute-start.37
  197.3 4.5 %collective-permute-start.40 = (f32[16,128]{1,0:T(8,128)S(1)}, f32[16,128]{1,0:T(8,128)S(1)}, u32[]{:S(2)}, u32[]{:S(2)}) collective-permute-start(f32[16,128]{1,0:T(8,128)S(1)} %add.127.refs_0_), channel_id=1, source_target_pairs={{0,6},{1,7},{2,4},{3,5},{4,2},{5,3},{6,0},{7,1},{8,14},{9,15},{10,... | collective-permute-start | bytes 24584 | tf_op jit(solution)/shard_map/ppermute | solution.py:1164
  198.6 3.7 %collective-permute-start.39 = (f32[16,128]{1,0:T(8,128)S(1)}, f32[16,128]{1,0:T(8,128)S(1)}, u32[]{:S(2)}, u32[]{:S(2)}) collective-permute-start(f32[16,128]{1,0:T(8,128)S(1)} %add.127.refs_0_), channel_id=1, source_target_pairs={{0,4},{1,5},{2,6},{3,7},{4,0},{5,1},{6,2},{7,3},{8,12},{9,13},{10,... | collective-permute-start | bytes 24584 | tf_op jit(solution)/shard_map/ppermute | solution.py:1164
  199.3 3.7 %collective-permute-start.38 = (f32[16,128]{1,0:T(8,128)S(1)}, f32[16,128]{1,0:T(8,128)S(1)}, u32[]{:S(2)}, u32[]{:S(2)}) collective-permute-start(f32[16,128]{1,0:T(8,128)S(1)} %add.127.refs_0_), channel_id=1, source_target_pairs={{0,2},{1,3},{2,0},{3,1},{4,6},{5,7},{6,4},{7,5},{8,10},{9,11},{10,... | collective-permute-start | bytes 24584 | tf_op jit(solution)/shard_map/ppermute | solution.py:1164
  (16 other events, 227.4 us)
